TPU v7x, 32 devices: a whole 2x2x4 slice. The times are simulated.
32 devices in a mesh: wide: 16 (over z, x, core), narrow: 2 (over y).
Axes of the slice: x: 2, y: 2, z: 4, core: 2. Of those that a mesh axis runs over, the one named last changes fastest.
Arguments:
- solution: float32 [640, 320, 320], P('wide', 'narrow'), may hold values from -6 to 6
- residual: float32 [640, 320, 320], P('wide', 'narrow'), may hold values from -45 to 45
- direction: float32 [640, 320, 320], P('wide', 'narrow'), may hold values from -14 to 14
- previous_product: float32 [1], replicated, may hold values from 9830400 to 98304000
- basis_x: float32 [640, 640], P('wide'), may hold values from -0.25 to 0.25
- basis_y: float32 [320, 320], P('narrow'), may hold values from -0.3125 to 0.3125
- basis_z: float32 [320, 320], P('narrow'), may hold values from -0.3125 to 0.3125
- eigen_x: float32 [640], replicated, may hold values from 0.2 to 4
- eigen_y: float32 [320], replicated, may hold values from 0.2 to 4
- eigen_z: float32 [320], replicated, may hold values from 0.2 to 4
Outputs:
- solution: float32 [640, 320, 320], P('wide', 'narrow')
- residual: float32 [640, 320, 320], P('wide', 'narrow')
- direction: float32 [640, 320, 320], P('wide', 'narrow')
All inputs are finite; a program needn't handle non-finite values.
Results may differ from a plain program's by a relative error of at most 0.00021.
Values sent between devices are 32-bit elements; how exact they have to be, the bound alone decides.
No kernel may reach another device: no remote copies, remote signals or barrier semaphores. Data moves between devices by JAX's collectives and lax.ppermute only.
A program may use at most 192 MiB of HBM per device.

v0:
```python
import jax
import jax.numpy as jnp
from jax import lax
from jax.sharding import PartitionSpec as P

mass_band = (
    1.0 / 5040.0,
    1.0 / 42.0,
    397.0 / 1680.0,
    151.0 / 315.0,
    397.0 / 1680.0,
    1.0 / 42.0,
    1.0 / 5040.0,
)
stiff_band = (-1.0 / 120.0, -0.2, -0.125, 2.0 / 3.0, -0.125, -0.2, -1.0 / 120.0)
highest = lax.Precision.HIGHEST


def padded_2(x, sides, width):
    for axis, dim in sides:
        count, length = (lax.axis_size(axis), x.shape[dim])
        up = [(i, (i + 1) % count) for i in range(count - 1)]
        down = [(j, i) for i, j in up]
        last = lax.slice_in_dim(x, length - width, length, axis=dim)
        leading = lax.slice_in_dim(x, 0, width, axis=dim)
        before = lax.ppermute(last, axis, up)
        after = lax.ppermute(leading, axis, down)
        x = jnp.concatenate([before, x, after], axis=dim)
    return x


def banded(field, coeffs, axis, length):
    total = coeffs[0] * lax.slice_in_dim(field, 0, length, axis=axis)
    for offset in range(1, 7):
        total = total + coeffs[offset] * lax.slice_in_dim(field, offset, offset + length, axis=axis)
    return total


def apply_padded(padded, length_x, length_y):
    length_z = padded.shape[2]
    along_z = jnp.pad(padded, ((0, 0), (0, 0), (3, 3)))
    mass_z = banded(along_z, mass_band, 2, length_z)
    stiff_z = banded(along_z, stiff_band, 2, length_z)
    first = banded(mass_z, mass_band, 1, length_y)
    second = banded(mass_z, stiff_band, 1, length_y) + banded(stiff_z, mass_band, 1, length_y)
    return banded(first, stiff_band, 0, length_x) + banded(second, mass_band, 0, length_x)


def contract_first(left, right):
    return lax.dot_general(left, right, (((0,), (0,)), ((), ())), precision=highest)


def contract_last(left, right):
    return lax.dot_general(left, right, (((1,), (1,)), ((), ())), precision=highest)


def per_device(
    solution,
    residual,
    direction,
    previous_product,
    basis_x,
    basis_y,
    basis_z,
    eigen_x,
    eigen_y,
    eigen_z,
):
    whole_x = lax.all_gather(basis_x, "wide", axis=0, tiled=True)
    whole_y, whole_z = (
        lax.all_gather(basis_y, "narrow", axis=0, tiled=True),
        lax.all_gather(basis_z, "narrow", axis=0, tiled=True),
    )
    count_wide = lax.axis_size("wide")
    count_narrow = lax.axis_size("narrow")
    index_wide = lax.axis_index("wide")
    index_narrow = lax.axis_index("narrow")
    cells_x, cells_y, cells_z = residual.shape
    total_x = whole_x.shape[0]
    total_y = whole_y.shape[0]
    product_before = previous_product[0]
    spectral = jnp.dot(residual.reshape(cells_x * cells_y, cells_z), whole_z, precision=highest)
    flat = jnp.transpose(spectral.reshape(cells_x, cells_y, cells_z), (1, 2, 0)).reshape(
        cells_y, cells_z * cells_x
    )
    pencil = contract_first(
        whole_y, lax.all_to_all(flat, "narrow", split_axis=1, concat_axis=0, tiled=True)
    )
    rows_y = total_y // count_wide
    part_z = cells_z // count_narrow
    moved = lax.all_to_all(pencil, "wide", split_axis=0, concat_axis=1, tiled=True)
    lined = jnp.transpose(moved.reshape(rows_y, count_wide, part_z, cells_x), (0, 2, 1, 3))
    lined = lined.reshape(rows_y * part_z, total_x)
    spectral_x = jnp.dot(lined, whole_x, precision=highest)
    shift_y = lax.dynamic_slice_in_dim(eigen_y, index_wide * rows_y, rows_y)
    shift_z = lax.dynamic_slice_in_dim(eigen_z, index_narrow * part_z, part_z)
    shift_yz = (shift_y[:, None] + shift_z[None, :]).reshape(rows_y * part_z, 1)
    scaled = spectral_x / (eigen_x[None, :] + shift_yz)
    inverse_x = contract_last(scaled, whole_x)
    unlined = jnp.transpose(inverse_x.reshape(rows_y, part_z, count_wide, cells_x), (0, 2, 1, 3))
    unlined = unlined.reshape(rows_y, count_wide * part_z * cells_x)
    pencil = lax.all_to_all(unlined, "wide", split_axis=1, concat_axis=0, tiled=True)
    pencil = jnp.dot(whole_y, pencil, precision=highest)
    back = lax.all_to_all(pencil, "narrow", split_axis=0, concat_axis=1, tiled=True)
    brick = jnp.transpose(back.reshape(cells_y, cells_z, cells_x), (2, 0, 1))
    result = contract_last(brick.reshape(cells_x * cells_y, cells_z), whole_z)
    precond = result.reshape(cells_x, cells_y, cells_z)
    product_now = lax.psum(jnp.sum(residual * precond), ("wide", "narrow"))
    direction = precond + product_now / product_before * direction
    padded = padded_2(direction, (("wide", 0), ("narrow", 1)), 3)
    image = apply_padded(padded, cells_x, cells_y)
    curvature = lax.psum(jnp.sum(direction * image), ("wide", "narrow"))
    alpha = product_now / curvature
    solution = solution + alpha * direction
    residual = residual - alpha * image
    return (solution, residual, direction)


def solution(mesh):
    placed = (
        P("wide", "narrow", None),
        P("wide", "narrow", None),
        P("wide", "narrow", None),
        P(),
        P("wide", None),
        P("narrow", None),
        P("narrow", None),
        P(),
        P(),
        P(),
    )
    return jax.shard_map(
        per_device,
        mesh=mesh,
        in_specs=placed,
        out_specs=(P("wide", "narrow", None), P("wide", "narrow", None), P("wide", "narrow", None)),
        check_vma=False,
    )
```

profile of v0, /device:TPU:0, one launch (start us, length us, event | category | flops | bytes accessed | tf_op | source)
XLA Modules:
  0.0 1396.6 jit_solution(7913263007731169145)
XLA Ops:
  7.2 9.9 all_gather.9
  17.0 0.0 copy-start.1
  17.0 0.8 copy-done.1
  17.8 22.0 %convolution_bitcast_fusion.1 = f32[160,320,40]{1,0,2:T(8,128)} fusion(f32[40,160,320]{2,1,0:T(8,128)} %param.11, f32[320,320]{1,0:T(8,128)S(1)} %all_gather.9), kind=kOutput, calls=%fused_computation.63 | convolution fusion | flops 7864320000 | bytes 16793600 | tf_op jit(solution)/shard_map/dot_general | solution.py:82
  39.8 15.0 %copy.22 = f32[160,320,40]{0,2,1:T(8,128)} copy(f32[160,320,40]{1,0,2:T(8,128)} %convolution_bitcast_fusion.1) | data formatting | bytes 16384000 | tf_op jit(solution)/shard_map/transpose | solution.py:83
  54.8 11.4 copy.23
  66.2 0.0 copy-start.4
  66.2 7.0 all-to-all-start
  73.2 0.0 copy-done.4
  73.2 95.1 %all_gather.10 = f32[320,320]{1,0:T(8,128)S(1)} all-gather(f32[160,320]{1,0:T(8,128)S(1)} %copy-done.4), channel_id=1, replica_groups=mesh['wide'=16,'narrow'=2] {'narrow'}, dimensions={0}, use_global_device_ids=true | all-gather | bytes 614400 | tf_op jit(solution)/shard_map/all_gather | solution.py:71
  168.3 0.0 all-to-all-done
  168.3 18.0 %convolution_bitcast_fusion = f32[320,6400]{1,0:T(8,128)} fusion(f32[320,6400]{1,0:T(8,128)} %bitcast.4, f32[320,320]{1,0:T(8,128)S(1)} %all_gather.10), kind=kOutput, calls=%fused_computation.23 | convolution fusion | flops 7864320000 | bytes 16793600 | tf_op jit(solution)/shard_map/dot_general | solution.py:50
  186.3 9.2 all_to_all.56
  195.5 0.0 copy-start.5
  195.5 5.9 all-to-all-start.1
  201.4 0.3 all-gather.2.cloned.1.call-start
  201.7 0.5 all-gather.2.cloned.1.call-update
  202.2 0.8 dynamic_slice.6
  202.9 0.0 copy-done.5
  202.9 0.1 dynamic_slice.7
  203.0 0.1 broadcast_add_fusion
  203.1 0.1 add.189
  203.2 184.0 %all-to-all-done.1 = f32[16,20,6400]{2,1,0:T(8,128)} async-done(((f32[16,20,6400]{2,1,0:T(8,128)}), f32[16,20,6400]{2,1,0:T(8,128)}, u32[]{:S(2)}, u32[]{:S(2)}) %all-to-all-start.1) | async-done | bytes 8192032 | tf_op jit(solution)/shard_map/all_to_all | solution.py:91
  387.1 9.8 copy.24
  396.9 23.7 %reshape.62 = f32[20,16,160,40]{3,2,1,0:T(8,128)} reshape(f32[20,16,6400]{2,1,0:T(8,128)} %copy.24) | data formatting | bytes 16384000 | tf_op jit(solution)/shard_map/reshape | solution.py:92
  420.5 23.8 %copy.25 = f32[20,160,16,40]{1,0,3,2:T(8,128)} copy(f32[20,160,16,40]{3,1,2,0:T(8,128)} %bitcast.47) | data formatting | bytes 16384000 | tf_op jit(solution)/shard_map/transpose | solution.py:92
  444.3 13.9 reshape.63
  458.2 0.0 copy-start.6
  458.2 26.3 %fusion.31 = f32[3200,640]{1,0:T(8,128)S(1)} fusion(f32[3200,640]{0,1:T(8,128)} %reshape.63, f32[640,640]{1,0:T(8,128)} %all-gather.2.cloned.1.call-done), kind=kOutput, calls=%fused_computation.71 | convolution fusion | flops 15728640000 | bytes 18022400 | tf_op jit(solution)/shard_map/dot_general | solution.py:94
  484.5 0.0 copy-done.6
  484.5 0.0 copy-done.3
  484.5 24.7 %fusion.22 = f32[3200,640]{0,1:T(8,128)} fusion(f32[640,640]{1,0:T(8,128)S(1)} %copy-done.3, f32[3200,640]{1,0:T(8,128)S(1)} %fusion.31, f32[3200]{0:T(1024)S(1)} %add.189, f32[640]{0:T(1024)S(1)} %copy-done.6), kind=kOutput, calls=%fused_computation.58 | convolution fusion | flops 15732736000 | bytes 18037760 | tf_op jit(solution)/shard_map/dot_general | solution.py:54
  509.2 14.0 %reshape.64 = f32[20,160,16,40]{1,0,3,2:T(8,128)} reshape(f32[3200,640]{0,1:T(8,128)} %fusion.22) | data formatting | bytes 16384000 | tf_op jit(solution)/shard_map/reshape | solution.py:100
  523.2 21.3 %copy.32 = f32[20,16,160,40]{3,2,0,1:T(8,128)} copy(f32[20,16,160,40]{2,0,3,1:T(8,128)} %bitcast.48) | data formatting | bytes 16384000 | tf_op jit(solution)/shard_map/all_to_all | solution.py:102
  544.5 23.8 %reshape.67 = f32[20,16,6400]{2,0,1:T(8,128)} reshape(f32[20,16,160,40]{3,2,0,1:T(8,128)} %copy.32) | data formatting | bytes 16384000 | tf_op jit(solution)/shard_map/all_to_all | solution.py:102
  568.3 255.9 %all_to_all.70 = f32[20,16,6400]{2,0,1:T(8,128)} all-to-all(f32[20,16,6400]{2,0,1:T(8,128)} %reshape.67), channel_id=1, replica_groups=mesh['wide'=16,'narrow'=2] {'wide'}, dimensions={1} | all-to-all | bytes 16384000 | tf_op jit(solution)/shard_map/all_to_all | solution.py:102
  824.2 9.3 all_to_all.62
  833.5 17.9 %fusion.32 = f32[6400,320]{0,1:T(8,128)} fusion(f32[320,6400]{1,0:T(8,128)} %all_to_all.62, f32[320,320]{1,0:T(8,128)S(1)} %all_gather.10), kind=kOutput, calls=%fused_computation.72 | convolution fusion | flops 7864320000 | bytes 16793600 | tf_op jit(solution)/shard_map/dot_general | solution.py:103
  851.5 6.9 all-to-all-start.3
  859.0 90.8 %all-to-all-done.3 = f32[2,160,6400]{2,1,0:T(8,128)} async-done(((f32[2,160,6400]{2,1,0:T(8,128)}), f32[2,160,6400]{2,1,0:T(8,128)}, u32[]{:S(2)}, u32[]{:S(2)}) %all-to-all-start.3) | async-done | bytes 8192032 | tf_op jit(solution)/shard_map/all_to_all | solution.py:104
  949.8 11.6 copy.29
  961.4 13.2 copy.30
  974.5 0.0 copy-done.2
  974.5 23.4 %multiply_reduce_fusion.1 = (f32[]{:T(128)}, f32[40,160,320]{2,1,0:T(8,128)}) fusion(f32[40,160,320]{2,1,0:T(8,128)} %param.11, f32[320,320]{1,0:T(8,128)S(1)} %copy-done.2, f32[160,320,40]{1,0,2:T(8,128)} %copy.30), kind=kOutput, calls=%fused_computation.57 | convolution fusion | flops 7868416000 | bytes 24985604 | tf_op jit(solution)/shard_map/dot_general | solution.py:54
  997.9 39.3 %psum.14 = f32[]{:T(128)} all-reduce(f32[]{:T(128)} %get-tuple-element.11), channel_id=1, replica_groups=mesh['wide'=16,'narrow'=2] {'wide','narrow'}, use_global_device_ids=true, to_apply=%region_1.0 | all-reduce | flops 1 | bytes 8 | tf_op jit(solution)/shard_map/psum | solution.py:108
  1038.0 12.1 multiply_add_fusion.4
  1050.0 1.6 fusion.30
  1051.6 1.6 collective-permute-start
  1053.3 1.3 collective-permute-start.1
  1054.6 0.5 collective-permute-done
  1055.0 4.8 collective-permute-done.1
  1059.8 1.3 pad_maximum_fusion.3
  1061.1 3.1 collective-permute-start.2
  1064.2 1.3 collective-permute-start.3
  1065.5 2.8 collective-permute-done.2
  1068.2 4.4 collective-permute-done.3
  1072.6 0.0 copy-done
  1072.6 5.8 pad_maximum_fusion
  1078.4 90.7 %multiply_add_fusion.1 = (f32[46,166,320]{2,1,0:T(8,128)}, f32[46,166,320]{2,1,0:T(8,128)}) fusion(f32[46,166,320]{2,1,0:T(8,128)} %pad_maximum_fusion), kind=kLoop, calls=%fused_computation.2 | loop fusion | flops 63531520 | bytes 29322240 | tf_op jit(solution)/shard_map/add | solution.py:35
  1169.1 33.1 %multiply_add_fusion.2 = f32[46,160,320]{2,1,0:T(8,128)} fusion(f32[46,166,320]{2,1,0:T(8,128)} %get-tuple-element.5), kind=kLoop, calls=%fused_computation.17 | loop fusion | flops 30617600 | bytes 75366400 | tf_op jit(solution)/shard_map/add | solution.py:35
  1202.2 58.7 %fusion.1 = f32[46,160,320]{2,1,0:T(8,128)} fusion(f32[46,166,320]{2,1,0:T(8,128)} %get-tuple-element.6, f32[46,166,320]{2,1,0:T(8,128)} %get-tuple-element.5), kind=kLoop, calls=%fused_computation.5 | loop fusion | flops 63590400 | bytes 141312000 | tf_op jit(solution)/shard_map/add | solution.py:45
  1261.0 53.2 %multiply_reduce_fusion = (f32[]{:T(128)}, f32[40,160,320]{2,1,0:T(8,128)}) fusion(f32[40,160,320]{2,1,0:T(8,128)} %multiply_add_fusion.4, f32[46,160,320]{2,1,0:T(8,128)} %fusion.1, f32[46,160,320]{2,1,0:T(8,128)} %multiply_add_fusion.2), kind=kLoop, calls=%fused_computation.55 | loop fusion | flops 59392000 | bytes 131072000 | tf_op jit(solution)/shard_map/reduce_sum | solution.py:112
  1314.2 52.5 %psum.15 = f32[]{:T(128)} all-reduce(f32[]{:T(128)} %get-tuple-element.3), channel_id=1, replica_groups=mesh['wide'=16,'narrow'=2] {'wide','narrow'}, use_global_device_ids=true, to_apply=%region_3.4 | all-reduce | flops 1 | bytes 8 | tf_op jit(solution)/shard_map/psum | solution.py:112
  1368.1 21.5 %multiply_subtract_fusion = (f32[40,160,320]{2,1,0:T(8,128)}, f32[40,160,320]{2,1,0:T(8,128)}) fusion(f32[40,160,320]{2,1,0:T(8,128)} %param.11, f32[40,160,320]{2,1,0:T(8,128)} %get-tuple-element.4, f32[]{:T(128)S(6)} %div.11, f32[40,160,320]{2,1,0:T(8,128)} %param.10, f32[40,160,320]{2,1,0:T(8,128)} %multiply_add_fusion.4), kind=kLoop, calls=%fused_computation.53 | loop fusion | flops 8192000 | bytes 49152004 | tf_op jit(solution)/shard_map/sub | solution.py:115
  (4 shorter events, 0.0 us)
Async XLA Ops:
  17.0 0.8 copy-start.1
  66.2 7.0 copy-start.4
  66.2 102.1 %all-to-all-start = ((f32[160,2,6400]{2,0,1:T(8,128)}), f32[160,2,6400]{2,0,1:T(8,128)}, u32[]{:S(2)}, u32[]{:S(2)}) async-start(f32[160,2,6400]{2,0,1:T(8,128)} %copy.23), calls=%async_computation | async-start | bytes 16384000 | tf_op jit(solution)/shard_map/all_to_all | solution.py:87
  195.5 7.5 copy-start.5
  195.5 191.6 %all-to-all-start.1 = ((f32[16,20,6400]{2,1,0:T(8,128)}), f32[16,20,6400]{2,1,0:T(8,128)}, u32[]{:S(2)}, u32[]{:S(2)}) async-start(f32[16,20,6400]{2,1,0:T(8,128)} %all_to_all.56), calls=%async_computation.1 | async-start | bytes 19660800 | tf_op jit(solution)/shard_map/all_to_all | solution.py:91
  201.4 256.8 %all-gather.2.cloned.1.call-start = ((), (), s32[]{:S(2)}) async-start(), calls=%async_computation.4 | async-start | bytes 1740800 | tf_op jit(solution)/shard_map/all_gather | solution.py:69
  458.2 26.3 %copy-start.6 = (f32[640]{0:T(1024)S(1)}, f32[640]{0:T(1024)}, u32[]{:S(2)}) copy-start(f32[640]{0:T(1024)} %param.17) | copy-start | bytes 7684
  458.2 26.3 %copy-start.3 = (f32[640,640]{1,0:T(8,128)S(1)}, f32[640,640]{1,0:T(8,128)}, u32[]{:S(2)}) copy-start(f32[640,640]{1,0:T(8,128)} %all-gather.2.cloned.1.call-done) | copy-start | bytes 4915204
  851.5 98.3 %all-to-all-start.3 = ((f32[2,160,6400]{2,1,0:T(8,128)}), f32[2,160,6400]{2,1,0:T(8,128)}, u32[]{:S(2)}, u32[]{:S(2)}) async-start(f32[2,160,6400]{2,1,0:T(8,128)} %bitcast.51), calls=%async_computation.3 | async-start | bytes 16384000 | tf_op jit(solution)/shard_map/all_to_all | solution.py:104
  961.4 13.2 copy-start.2
  1050.0 22.6 %copy-start = (f32[40,160,320]{2,1,0:T(8,128)S(1)}, f32[40,160,320]{2,1,0:T(8,128)}, u32[]{:S(2)}) copy-start(f32[40,160,320]{2,1,0:T(8,128)} %multiply_add_fusion.4) | copy-start | bytes 24576004
  1051.6 3.4 collective-permute-start
  1053.3 6.5 collective-permute-start.1
  1061.1 7.2 collective-permute-start.2
  1064.2 8.5 collective-permute-start.3
Sparse Core Ops, SparseCore 0:
  204.4 145.7 all-gather.1
where the time goes:
time: 1410 us; the launch traced here: 1400 us
  blocking collectives  453 us (32%)
  waiting for transfers between devices  288 us (20%)
  other arithmetic  276 us (20%)
  local copies, waits for them, and re-layouts  203 us (14%)
  matrix products  132 us (9%)
  starting transfers between devices  27.4 us (2%)
  between operations  17.1 us (1%)
    all_to_all x1, blocking collectives, per_device(): lax.all_to_all(unlined, 'wide', split_axis=1, concat_axis=0, tiled=True)  256 us
    all_to_all x1, waiting for transfers between devices, per_device(): lax.all_to_all(pencil, 'wide', split_axis=0, concat_axis=1, tiled=True)  184 us
    add x2, other arithmetic, banded(): total + coeffs[offset] * lax.slice_in_dim(field, offset, offset + length,...  124 us
    all_gather x1, blocking collectives, per_device(): lax.all_gather(basis_y, 'narrow', axis=0, tiled=True)  95.1 us
    all_to_all x1, waiting for transfers between devices, per_device(): lax.all_to_all(pencil, 'narrow', split_axis=0, concat_axis=1, tiled=True)  90.8 us
    add x1, other arithmetic, apply_padded(): banded(mass_z, stiff_band, 1, length_y)  58.7 us
    all_to_all x3, local copies, waits for them, and re-layouts, per_device(): lax.all_to_all(unlined, 'wide', split_axis=1, concat_axis=0, tiled=True)  54.4 us
    reduce_sum x1, other arithmetic, per_device(): curvature = lax.psum(jnp.sum(direction * image), ('wide', 'narrow'))  53.2 us
  transfers between devices with their start and end apart: 8, of which 6 were waited for; matrix products, arithmetic and copies ran while one was open for 5% of the time, Pallas kernels for 0%

commit v1 on v0

--- a/solution.py
+++ b/solution.py
@@ -1,6 +1,10 @@
+import functools
+
 import jax
 import jax.numpy as jnp
 from jax import lax
+from jax.experimental import pallas as pl
+from jax.experimental.pallas import tpu as pltpu
 from jax.sharding import PartitionSpec as P
 
 mass_band = (
@@ -14,6 +18,540 @@
 )
 stiff_band = (-1.0 / 120.0, -0.2, -0.125, 2.0 / 3.0, -0.125, -0.2, -1.0 / 120.0)
 highest = lax.Precision.HIGHEST
+LANES = 128
+HALO = 3
+EDGE = 8
+both = ("wide", "narrow")
+budget = 100 * 1024 * 1024 // 2
+
+
+def split(x):
+    high = x.astype(jnp.bfloat16)
+    low = (x - high.astype(jnp.float32)).astype(jnp.bfloat16)
+    return high, low
+
+
+def dot3(left, right, over):
+    dims = ((over[:1], over[1:]), ((), ()))
+    one = functools.partial(
+        lax.dot_general, dimension_numbers=dims, preferred_element_type=jnp.float32
+    )
+    return one(left[0], right[0]) + one(left[1], right[0]) + one(left[0], right[1])
+
+
+class Plan:
+    def __init__(self, cells_x, cells_y, cells_z, total_x, total_y, wide, narrow):
+        self.cells_x, self.cells_y, self.cells_z = cells_x, cells_y, cells_z
+        self.total_x, self.total_y = total_x, total_y
+        self.wide, self.narrow, self.count = wide, narrow, wide * narrow
+        self.rest = cells_y - LANES
+        self.fits = (
+            cells_z % self.count == 0
+            and cells_x % 8 == 0
+            and self.rest > 0
+            and LANES % self.rest == 0
+            and self.rest < LANES
+            and total_y % LANES == LANES // 2
+            and wide % 2 == 0
+            and (total_x // 2) % 16 == 0
+            and self.count % 8 == 0
+        )
+        if not self.fits:
+            return
+        self.share = cells_z // self.count
+        self.group = LANES // self.rest
+        self.tiles = cells_x // 8
+        self.chunks = [
+            (start, min(self.group, self.share - start))
+            for start in range(0, self.share, self.group)
+        ]
+        self.fits = (
+            self.group % 2 == 0
+            and self.share % 2 == 0
+            and len(self.chunks) > 1
+            and self.chunks[-1][1] < self.group
+        )
+
+    def rows(self, chunk):
+        start, size = self.chunks[chunk]
+        return start * self.count, size * self.count
+
+    def message(self, chunk):
+        return (self.count, self.tiles, self.chunks[chunk][1] + 1, 8, LANES)
+
+
+def forward_kernel(plan, field_ref, basis_ref, *refs):
+    outs = refs[: len(plan.chunks)]
+    high_ref, low_ref, stage_ref = refs[len(plan.chunks) :]
+
+    @pl.when(pl.program_id(0) == 0)
+    def _():
+        high_ref[...], low_ref[...] = split(basis_ref[...])
+
+    basis = (high_ref[...], low_ref[...])
+    for i in range(8):
+        stage_ref[i] = dot3(basis, split(field_ref[i]), (1, 1))
+    for chunk, (start, size) in enumerate(plan.chunks):
+        rests = []
+        for j in range(size):
+            at = (start + j) * plan.count
+            turned = jnp.swapaxes(stage_ref[:, at : at + plan.count, :], 0, 1)
+            outs[chunk][:, 0, j] = turned[:, :, :LANES]
+            rests.append(turned[:, :, LANES:])
+        while len(rests) < plan.group:
+            rests.append(jnp.zeros_like(rests[0]))
+        outs[chunk][:, 0, size] = jnp.concatenate(rests, axis=2)
+
+
+def forward_z(plan, field, basis):
+    shapes = [jax.ShapeDtypeStruct(plan.message(k), jnp.float32) for k in range(len(plan.chunks))]
+    return pl.pallas_call(
+        functools.partial(forward_kernel, plan),
+        grid=(plan.tiles,),
+        in_specs=[
+            pl.BlockSpec((8, plan.cells_y, plan.cells_z), lambda t: (t, 0, 0)),
+            pl.BlockSpec(basis.shape, lambda t: (0, 0)),
+        ],
+        out_specs=[
+            pl.BlockSpec((s.shape[0], 1) + s.shape[2:], lambda t: (0, t, 0, 0, 0)) for s in shapes
+        ],
+        out_shape=shapes,
+        scratch_shapes=[
+            pltpu.VMEM(basis.shape, jnp.bfloat16),
+            pltpu.VMEM(basis.shape, jnp.bfloat16),
+            pltpu.VMEM((8, plan.cells_z, plan.cells_y), jnp.float32),
+        ],
+        compiler_params=pltpu.CompilerParams(vmem_limit_bytes=budget),
+        cost_estimate=pl.CostEstimate(
+            flops=6 * field.size * plan.cells_z, bytes_accessed=8 * field.size, transcendentals=0
+        ),
+        name="forward_z",
+    )(field, basis)
+
+
+def inverse_kernel(plan, chunks, final, *refs):
+    refs = list(refs)
+    parts = [refs.pop(0) for _ in chunks]
+    basis_ref = refs.pop(0)
+    if final:
+        base_ref, old_ref, before_ref = refs.pop(0), refs.pop(0), refs.pop(0)
+        out_ref, now_ref = refs.pop(0), refs.pop(0)
+    else:
+        out_ref = refs.pop(0)
+    high_ref, low_ref, stage_ref = refs
+
+    @pl.when(pl.program_id(0) == 0)
+    def _():
+        high_ref[...], low_ref[...] = split(basis_ref[...])
+
+    at = 0
+    for part, chunk in zip(parts, chunks):
+        size = plan.chunks[chunk][1]
+        rests = part[:, 0, size]
+        for q in range(size):
+            stage_ref[:, at : at + plan.count, :LANES] = jnp.swapaxes(part[:, 0, q], 0, 1)
+            stage_ref[:, at : at + plan.count, LANES:] = jnp.swapaxes(
+                rests[:, :, q * plan.rest : (q + 1) * plan.rest], 0, 1
+            )
+            at += plan.count
+    if final:
+        sums = parts[-1][:, 0, plan.chunks[chunks[-1]][1], 0, LANES - 1 :]
+        now = jnp.sum(sums, axis=0, keepdims=True)
+        now_ref[...] = jnp.broadcast_to(now, now_ref.shape)
+        beta = now / before_ref[...]
+    basis = (high_ref[...], low_ref[...])
+    for i in range(8):
+        value = dot3(split(stage_ref[i].T), basis, (1, 0))
+        if final:
+            value = base_ref[i] + value + beta * old_ref[i]
+        out_ref[i] = value
+
+
+def inverse_z(plan, parts, chunks, basis, base=None, old=None, before=None):
+    final = base is not None
+    brick = pl.BlockSpec((8, plan.cells_y, plan.cells_z), lambda t: (t, 0, 0))
+    shape = jax.ShapeDtypeStruct((plan.cells_x, plan.cells_y, plan.cells_z), jnp.float32)
+    low = plan.rows(chunks[0])[0]
+    high = sum(plan.rows(chunks[-1]))
+    basis = basis[low:high]
+    one = pl.BlockSpec((1, 1), lambda t: (0, 0))
+    in_specs = [
+        pl.BlockSpec((p.shape[0], 1) + p.shape[2:], lambda t: (0, t, 0, 0, 0)) for p in parts
+    ] + [pl.BlockSpec(basis.shape, lambda t: (0, 0))]
+    operands = list(parts) + [basis]
+    out_specs, out_shape = brick, shape
+    if final:
+        in_specs += [brick, brick, one]
+        operands += [base, old, before.reshape(1, 1)]
+        out_specs = [brick, pl.BlockSpec((8, LANES), lambda t: (0, 0))]
+        out_shape = [shape, jax.ShapeDtypeStruct((8, LANES), jnp.float32)]
+    return pl.pallas_call(
+        functools.partial(inverse_kernel, plan, chunks, final),
+        grid=(plan.tiles,),
+        in_specs=in_specs,
+        out_specs=out_specs,
+        out_shape=out_shape,
+        scratch_shapes=[
+            pltpu.VMEM(basis.shape, jnp.bfloat16),
+            pltpu.VMEM(basis.shape, jnp.bfloat16),
+            pltpu.VMEM((8, high - low, plan.cells_y), jnp.float32),
+        ],
+        compiler_params=pltpu.CompilerParams(vmem_limit_bytes=budget),
+        cost_estimate=pl.CostEstimate(
+            flops=6 * shape.size * (high - low),
+            bytes_accessed=8 * shape.size,
+            transcendentals=0,
+        ),
+        name="inverse_z",
+    )(*operands)
+
+
+def middle_kernel(plan, chunk, *refs):
+    (
+        in_ref,
+        basis_x_ref,
+        turned_x_ref,
+        main_y_ref,
+        rest_y_ref,
+        eigen_x_ref,
+        shift_ref,
+        total_ref,
+        out_ref,
+        sum_ref,
+        bx_high,
+        bx_low,
+        tx_high,
+        tx_low,
+        my_high,
+        my_low,
+        ry_high,
+        ry_low,
+        u_high,
+        u_low,
+        q_high,
+        q_low,
+        rest_acc,
+    ) = refs
+    size = plan.chunks[chunk][1]
+    last = chunk == len(plan.chunks) - 1
+    wide, narrow, tiles = plan.wide, plan.narrow, plan.tiles
+    half = plan.total_x // 2
+    lump = wide // 2
+    span = plan.total_y + LANES // 2
+    width = 2 * plan.total_y
+    bx_high[...], bx_low[...] = split(basis_x_ref[...])
+    tx_high[...], tx_low[...] = split(turned_x_ref[...])
+    my_high[...], my_low[...] = split(main_y_ref[...])
+    ry_high[...], ry_low[...] = split(rest_y_ref[...])
+    rest_acc[...] = jnp.zeros_like(rest_acc)
+
+    def gathered(piece, h):
+        rows = pl.ds(h * lump, lump)
+        return jnp.concatenate(
+            [in_ref[rows, n, :, piece].reshape(half, LANES) for n in range(narrow)], axis=1
+        )
+
+    def pair(p, total):
+        for h in range(2):
+            rest = split(gathered(size, h))
+            parts = []
+            for s in range(2):
+                j = 2 * p + s
+                parts.append(
+                    dot3(split(gathered(j, h)), (my_high[s], my_low[s]), (1, 0))
+                    + dot3(rest, (ry_high[j], ry_low[j]), (1, 0))
+                )
+            cut = span - LANES
+            joined = jnp.concatenate(
+                [
+                    parts[0][:, :cut],
+                    parts[0][:, cut:] + parts[1][:, :LANES],
+                    parts[1][:, LANES:],
+                ],
+                axis=1,
+            )
+            rows = pl.ds(h * half, half)
+            u_high[rows, :], u_low[rows, :] = split(joined)
+        shift = shift_ref[p]
+        for h in range(2):
+            rows = pl.ds(h * half, half)
+            spectral = dot3(
+                (tx_high[rows, :], tx_low[rows, :]), (u_high[...], u_low[...]), (1, 0)
+            )
+            scaled = spectral / (eigen_x_ref[rows, :] + shift)
+            total = total + jnp.sum((spectral * scaled).reshape(half // 8, 8, width), axis=0)
+            q_high[rows, :], q_low[rows, :] = split(scaled)
+        for h in range(2):
+            rows = pl.ds(h * half, half)
+            value = dot3((bx_high[rows, :], bx_low[rows, :]), (q_high[...], q_low[...]), (1, 0))
+            for s in range(2):
+                j = 2 * p + s
+                mine = split(value[:, s * (width - span) : s * (width - span) + span])
+                main = dot3(mine, (my_high[s], my_low[s]), (1, 1))
+                rest_acc[rows, :] += dot3(mine, (ry_high[j], ry_low[j]), (1, 1))
+                for n in range(narrow):
+                    out_ref[pl.ds(h * lump, lump), n, :, j] = main[
+                        :, n * LANES : (n + 1) * LANES
+                    ].reshape(lump, tiles, 8, LANES)
+        return total
+
+    total = lax.fori_loop(0, size // 2, pair, jnp.zeros((8, width), jnp.float32))
+    value = total_ref[...] + jnp.sum(total)
+    sum_ref[...] = value
+    for n in range(narrow):
+        rest = rest_acc[:, n * LANES : (n + 1) * LANES]
+        if last:
+            lane = lax.broadcasted_iota(jnp.int32, rest.shape, 1)
+            rest = jnp.where(lane >= size * plan.rest, value[:1, :], rest)
+        out_ref[:, n, :, size] = rest.reshape(wide, tiles, 8, LANES)
+
+
+def middle(plan, chunk, message, basis_x, turned_x, main_y, rest_y, eigen_x, shift, total):
+    size = plan.chunks[chunk][1]
+    shape = (plan.wide, plan.narrow) + message.shape[1:]
+    square = (plan.total_x, plan.total_x)
+    pencil = (plan.total_x, 2 * plan.total_y)
+    half = jnp.bfloat16
+    out, total = pl.pallas_call(
+        functools.partial(middle_kernel, plan, chunk),
+        out_shape=[
+            jax.ShapeDtypeStruct(shape, jnp.float32),
+            jax.ShapeDtypeStruct((8, LANES), jnp.float32),
+        ],
+        in_specs=[pl.BlockSpec(memory_space=pltpu.VMEM)] * 8,
+        out_specs=[pl.BlockSpec(memory_space=pltpu.VMEM)] * 2,
+        scratch_shapes=[
+            pltpu.VMEM(square, half),
+            pltpu.VMEM(square, half),
+            pltpu.VMEM(square, half),
+            pltpu.VMEM(square, half),
+            pltpu.VMEM(main_y.shape, half),
+            pltpu.VMEM(main_y.shape, half),
+            pltpu.VMEM(rest_y.shape, half),
+            pltpu.VMEM(rest_y.shape, half),
+            pltpu.VMEM(pencil, half),
+            pltpu.VMEM(pencil, half),
+            pltpu.VMEM(pencil, half),
+            pltpu.VMEM(pencil, half),
+            pltpu.VMEM((plan.total_x, plan.narrow * LANES), jnp.float32),
+        ],
+        compiler_params=pltpu.CompilerParams(vmem_limit_bytes=budget),
+        cost_estimate=pl.CostEstimate(
+            flops=12 * size * plan.total_x * plan.total_y * (plan.total_x + plan.total_y),
+            bytes_accessed=8 * message.size,
+            transcendentals=0,
+        ),
+        name="middle",
+    )(message.reshape(shape), basis_x, turned_x, main_y, rest_y, eigen_x, shift, total)
+    return out.reshape(message.shape), total
+
+
+def shifted(x, step_wide, step_narrow):
+    wide, narrow = lax.axis_size("wide"), lax.axis_size("narrow")
+    pairs = []
+    for w in range(wide):
+        for n in range(narrow):
+            v, m = w + step_wide, n + step_narrow
+            if 0 <= v < wide and 0 <= m < narrow:
+                pairs.append((v * narrow + m, w * narrow + n))
+    return lax.ppermute(x, both, pairs)
+
+
+def stencil_kernel(plan, *refs):
+    pieces = refs[:9]
+    bands_ref, image_ref, sum_ref, field, high_a, low_a, h_a, h_b, total, sems = refs[9:]
+    cells_x, cells_y, cells_z = plan.cells_x, plan.cells_y, plan.cells_z
+    xs = (pl.ds(0, HALO), pl.ds(HALO, cells_x), pl.ds(HALO + cells_x, HALO))
+    ys = (pl.ds(0, EDGE), pl.ds(EDGE, cells_y), pl.ds(EDGE + cells_y, EDGE))
+    step = pl.program_id(0)
+
+    @pl.when(step == 0)
+    def _():
+        copies = [
+            pltpu.make_async_copy(
+                pieces[3 * a + b], field.at[xs[a], ys[b], :], sems.at[3 * a + b]
+            )
+            for a in range(3)
+            for b in range(3)
+        ]
+        for copy in copies:
+            copy.start()
+        total[...] = jnp.zeros_like(total)
+        high_a[...], low_a[...] = split(bands_ref[...])
+        for copy in copies:
+            copy.wait()
+
+    mass_z = (high_a[0], low_a[0])
+    stiff_z = (high_a[1], low_a[1])
+    padded_y = cells_y + 2 * EDGE
+    blocks = -(-cells_z // LANES)
+
+    def plane(i, carry):
+        x = step * 8 + i
+        middle_plane = field[x + HALO]
+        first = stiff_band[HALO] * middle_plane
+        second = mass_band[HALO] * middle_plane
+        for o in range(1, HALO + 1):
+            around = field[x + HALO - o] + field[x + HALO + o]
+            first = first + stiff_band[HALO + o] * around
+            second = second + mass_band[HALO + o] * around
+        first, second = split(first), split(second)
+        a = dot3(first, mass_z, (1, 0)) + dot3(second, stiff_z, (1, 0))
+        b = dot3(second, mass_z, (1, 0))
+        for k in range(blocks):
+            lanes = min(LANES, cells_z - k * LANES)
+            h_a[k, :, :lanes] = a[:, k * LANES : k * LANES + lanes]
+            h_b[k, :, :lanes] = b[:, k * LANES : k * LANES + lanes]
+        for k in range(blocks):
+            lanes = min(LANES, cells_z - k * LANES)
+            at = lambda ref, o: ref[k, pl.ds(EDGE + o, cells_y), :]
+            image = mass_band[HALO] * at(h_a, 0) + stiff_band[HALO] * at(h_b, 0)
+            for o in range(1, HALO + 1):
+                image = image + mass_band[HALO + o] * (at(h_a, -o) + at(h_a, o))
+                image = image + stiff_band[HALO + o] * (at(h_b, -o) + at(h_b, o))
+            here = pl.ds(k * LANES, lanes)
+            image_ref[i, :, here] = image[:, :lanes]
+            product = image[:, :lanes] * field[x + HALO, pl.ds(EDGE, cells_y), here]
+            total[:, here] += jnp.sum(product.reshape(cells_y // 8, 8, lanes), axis=0)
+        return carry
+
+    lax.fori_loop(0, 8, plane, 0)
+
+    @pl.when(step == pl.num_programs(0) - 1)
+    def _():
+        sum_ref[...] = jnp.full(sum_ref.shape, jnp.sum(total[...]), jnp.float32)
+
+
+def stencil(plan, direction):
+    cells_x, cells_y, cells_z = direction.shape
+    low_x, high_x = direction[:HALO], direction[cells_x - HALO :]
+    low_y, high_y = direction[:, :EDGE], direction[:, cells_y - EDGE :]
+    pieces = [
+        shifted(high_x[:, cells_y - EDGE :], -1, -1),
+        shifted(high_x, -1, 0),
+        shifted(high_x[:, :EDGE], -1, 1),
+        shifted(high_y, 0, -1),
+        direction,
+        shifted(low_y, 0, 1),
+        shifted(low_x[:, cells_y - EDGE :], 1, -1),
+        shifted(low_x, 1, 0),
+        shifted(low_x[:, :EDGE], 1, 1),
+    ]
+    rows = lax.broadcasted_iota(jnp.int32, (cells_z, cells_z), 0)
+    columns = lax.broadcasted_iota(jnp.int32, (cells_z, cells_z), 1)
+    bands = []
+    for band in (mass_band, stiff_band):
+        matrix = jnp.zeros((cells_z, cells_z), jnp.float32)
+        for o in range(-HALO, HALO + 1):
+            matrix = jnp.where(rows - columns == o, band[o + HALO], matrix)
+        bands.append(matrix)
+    bands = jnp.stack(bands)
+    padded_y = cells_y + 2 * EDGE
+    blocks = -(-cells_z // LANES)
+    return pl.pallas_call(
+        functools.partial(stencil_kernel, plan),
+        grid=(cells_x // 8,),
+        in_specs=[pl.BlockSpec(memory_space=pl.ANY)] * 9
+        + [pl.BlockSpec(bands.shape, lambda t: (0, 0, 0))],
+        out_specs=[
+            pl.BlockSpec((8, cells_y, cells_z), lambda t: (t, 0, 0)),
+            pl.BlockSpec((8, LANES), lambda t: (0, 0)),
+        ],
+        out_shape=[
+            jax.ShapeDtypeStruct(direction.shape, jnp.float32),
+            jax.ShapeDtypeStruct((8, LANES), jnp.float32),
+        ],
+        scratch_shapes=[
+            pltpu.VMEM((cells_x + 2 * HALO, padded_y, cells_z), jnp.float32),
+            pltpu.VMEM(bands.shape, jnp.bfloat16),
+            pltpu.VMEM(bands.shape, jnp.bfloat16),
+            pltpu.VMEM((blocks, padded_y, LANES), jnp.float32),
+            pltpu.VMEM((blocks, padded_y, LANES), jnp.float32),
+            pltpu.VMEM((8, cells_z), jnp.float32),
+            pltpu.SemaphoreType.DMA((9,)),
+        ],
+        compiler_params=pltpu.CompilerParams(vmem_limit_bytes=budget),
+        cost_estimate=pl.CostEstimate(
+            flops=18 * direction.size * cells_z, bytes_accessed=8 * direction.size, transcendentals=0
+        ),
+        name="stencil",
+    )(*pieces, bands)
+
+
+def scatter(x):
+    return lax.all_to_all(x, both, split_axis=0, concat_axis=0, tiled=True)
+
+
+def dealt(plan, whole_z):
+    columns = whole_z.T.reshape(plan.count, plan.share, plan.cells_z)
+    return jnp.swapaxes(columns, 0, 1).reshape(plan.cells_z, plan.cells_z)
+
+
+def basis_y_blocks(plan, whole_y):
+    by_owner = whole_y.reshape(plan.narrow, plan.cells_y, plan.total_y)
+    main = by_owner[:, :LANES].reshape(plan.narrow * LANES, plan.total_y)
+    rest = by_owner[:, LANES:]
+    half = LANES // 2
+    sides = [(0, half), (half, 0)]
+    mains = jnp.stack([jnp.pad(main, ((0, 0), s)) for s in sides])
+    rests = []
+    for q in range(plan.group):
+        after = LANES - (q + 1) * plan.rest
+        padded = jnp.pad(rest, ((0, 0), (q * plan.rest, after), sides[q % 2]))
+        rests.append(padded.reshape(plan.narrow * LANES, plan.total_y + half))
+    return mains, jnp.stack(rests)
+
+
+def by_pencils(
+    plan,
+    solution,
+    residual,
+    direction,
+    previous_product,
+    basis_x,
+    basis_y,
+    basis_z,
+    eigen_x,
+    eigen_y,
+    eigen_z,
+):
+    whole_z = lax.all_gather(basis_z, "narrow", axis=0, tiled=True)
+    whole_y = lax.all_gather(basis_y, "narrow", axis=0, tiled=True)
+    whole_x = lax.all_gather(basis_x, "wide", axis=0, tiled=True)
+    turned_z = dealt(plan, whole_z)
+    messages = forward_z(plan, residual, turned_z)
+    main_y, rest_y = basis_y_blocks(plan, whole_y)
+    turned_x = whole_x.T
+    index = lax.axis_index("wide") * plan.narrow + lax.axis_index("narrow")
+    mine_z = lax.dynamic_slice_in_dim(eigen_z, index * plan.share, plan.share)
+    shifts = (mine_z[:, None] + eigen_y[None, :]).reshape(plan.share // 2, 1, 2 * plan.total_y)
+    arrived = [scatter(m) for m in messages]
+    total = jnp.zeros((8, LANES), jnp.float32)
+    returned = []
+    for k, (start, size) in enumerate(plan.chunks):
+        shift = shifts[start // 2 : (start + size) // 2]
+        back, total = middle(
+            plan,
+            k,
+            arrived[k],
+            whole_x,
+            turned_x,
+            main_y,
+            rest_y,
+            eigen_x.reshape(-1, 1),
+            shift,
+            total,
+        )
+        returned.append(scatter(back))
+    last = len(plan.chunks) - 1
+    base = inverse_z(plan, returned[:last], tuple(range(last)), turned_z)
+    direction, now = inverse_z(
+        plan, returned[last:], (last,), turned_z, base, direction, previous_product
+    )
+    image, part = stencil(plan, direction)
+    parts = lax.all_gather(part, both, axis=0, tiled=False)
+    alpha = now[0, 0] / jnp.sum(parts[:, 0, 0])
+    return solution + alpha * direction, residual - alpha * image, direction
 
 
 def padded_2(x, sides, width):
@@ -54,7 +592,7 @@
     return lax.dot_general(left, right, (((1,), (1,)), ((), ())), precision=highest)
 
 
-def per_device(
+def general(
     solution,
     residual,
     direction,
@@ -116,6 +654,15 @@
     return (solution, residual, direction)
 
 
+def per_device(*arrays):
+    residual, basis_x, basis_y = arrays[1], arrays[4], arrays[5]
+    wide, narrow = lax.axis_size("wide"), lax.axis_size("narrow")
+    plan = Plan(*residual.shape, basis_x.shape[1], basis_y.shape[1], wide, narrow)
+    if plan.fits:
+        return by_pencils(plan, *arrays)
+    return general(*arrays)
+
+
 def solution(mesh):
     placed = (
         P("wide", "narrow", None),

time: 1410 us -> 668 us (0.47)
  other arithmetic: 276 us -> 25.2 us
  blocking collectives: 453 us -> 231 us
  local copies, waits for them, and re-layouts: 203 us -> 17.9 us
  Pallas kernels: 0 us -> 153 us
  matrix products: 132 us -> 0 us
  waiting for transfers between devices: 288 us -> 181 us
    add x5 -> x2, other arithmetic: 195 us -> 12.1 us  [the longest x1 12.1 us: by_pencils(): return (solution + alpha * direction, residual - alpha * image, direction)]
    pallas_call x0 -> x7, Pallas kernels: none -> 153 us  [the longest x3 58.1 us: middle(): pl.pallas_call(functools.partial(middle_kernel, plan, chunk), out_shape=[...]
    all_to_all x3 -> x4, waiting for transfers between devices: 275 us -> 140 us  [scatter(): return lax.all_to_all(x, both, split_axis=0, concat_axis=0, tiled=True)]
    dot_general x6 -> x0, matrix products: 132 us -> none  [the longest x2 48.1 us: contract_last(): lax.dot_general(left, right, (((1,), (1,)), ((), ())), precision=highest)]
    all_to_all x1 -> x2, blocking collectives: 256 us -> 130 us  [scatter(): return lax.all_to_all(x, both, split_axis=0, concat_axis=0, tiled=True)]
    all_to_all x7 -> x0, local copies, waits for them, and re-layouts: 96.4 us -> none  [the longest x3 54.4 us: per_device(): lax.all_to_all(unlined, 'wide', split_axis=1, concat_axis=0, tiled=True)]
    psum x2 -> x0, blocking collectives: 91.8 us -> none  [the longest x1 52.5 us: per_device(): curvature = lax.psum(jnp.sum(direction * image), ('wide', 'narrow'))]
    reshape x4 -> x2, local copies, waits for them, and re-layouts: 64.7 us -> 0.21 us  [the longest x1 0.14 us: by_pencils(): eigen_x.reshape(-1, 1)]
  transfers between devices with their start and end apart: 8 -> 13, of which waited for: 6 -> 7; matrix products, arithmetic and copies ran while one was open for 5% -> 1% of each run, Pallas kernels for 0% -> 10%
where the time goes in v1:
time: 668 us; the launch traced here: 663 us
  blocking collectives  231 us (35%)
  waiting for transfers between devices  181 us (27%)
  Pallas kernels  153 us (23%)
  starting transfers between devices  38.6 us (6%)
  other arithmetic  25.2 us (4%)
  local copies, waits for them, and re-layouts  17.9 us (3%)
  between operations  16.6 us (2%)
    all_to_all x4, waiting for transfers between devices, scatter(): return lax.all_to_all(x, both, split_axis=0, concat_axis=0, tiled=True)  140 us
    all_to_all x2, blocking collectives, scatter(): return lax.all_to_all(x, both, split_axis=0, concat_axis=0, tiled=True)  130 us
    all_gather x1, blocking collectives, by_pencils(): parts = lax.all_gather(part, both, axis=0, tiled=False)  66.8 us
    pallas_call x3, Pallas kernels, middle(): pl.pallas_call(functools.partial(middle_kernel, plan, chunk), out_shape=[...  58.1 us
    pallas_call x1, Pallas kernels, stencil(): pl.pallas_call(functools.partial(stencil_kernel, plan), grid=(cells_x //...  54.4 us
    all_gather x1, waiting for transfers between devices, by_pencils(): whole_x = lax.all_gather(basis_x, 'wide', axis=0, tiled=True)  31.2 us
    pallas_call x2, Pallas kernels, inverse_z(): pl.pallas_call(functools.partial(inverse_kernel, plan, chunks, final), gr...  24.4 us
    all_gather x1, blocking collectives, by_pencils(): whole_y = lax.all_gather(basis_y, 'narrow', axis=0, tiled=True)  23.6 us
  transfers between devices with their start and end apart: 13, of which 7 were waited for; matrix products, arithmetic and copies ran while one was open for 1% of the time, Pallas kernels for 10%

profile of v1, /device:TPU:0, one launch (start us, length us, event | category | flops | bytes accessed | tf_op | source)
XLA Modules:
  0.0 663.2 jit_solution(8403837595663288885)
XLA Ops:
  7.2 9.9 %all_gather.15 = f32[320,320]{1,0:T(8,128)S(1)} all-gather(f32[160,320]{1,0:T(8,128)} %param.16), channel_id=1, replica_groups=mesh['wide'=16,'narrow'=2] {'narrow'}, dimensions={0}, use_global_device_ids=true | all-gather | bytes 614400 | tf_op jit(solution)/shard_map/all_gather | solution.py:518
  17.0 0.2 copy.29
  17.2 0.1 reshape.128
  17.3 0.2 copy.30
  17.5 15.9 %forward_z.1 = (f32[32,5,5,8,128]{4,3,2,1,0:T(8,128)}, f32[32,5,5,8,128]{4,3,2,1,0:T(8,128)}, f32[32,5,3,8,128]{4,3,2,1,0:T(8,128)S(1)}) custom-call(f32[40,160,320]{2,1,0:T(8,128)} %field_ref.1, f32[320,320]{1,0:T(8,128)S(1)} %bitcast.27), custom_call_target="tpu_custom_call" | custom-call | flops 3932160000 | bytes 16384000 | tf_op jit(solution)/shard_map/forward_z/pallas_call | solution.py:108
  33.4 51.8 %all_to_all.30 = f32[32,5,3,8,128]{4,3,2,1,0:T(8,128)} all-to-all(f32[32,5,3,8,128]{4,3,2,1,0:T(8,128)S(1)} %get-tuple-element.15), channel_id=1, replica_groups=mesh['wide'=16,'narrow'=2] {'wide','narrow'}, dimensions={0} | all-to-all | bytes 3932160 | tf_op jit(solution)/shard_map/all_to_all | solution.py:482
  85.3 78.5 %all_to_all.31 = f32[32,5,5,8,128]{4,3,2,1,0:T(8,128)} all-to-all(f32[32,5,5,8,128]{4,3,2,1,0:T(8,128)S(1)} %copy-done.10), channel_id=1, replica_groups=mesh['wide'=16,'narrow'=2] {'wide','narrow'}, dimensions={0} | all-to-all | bytes 6553600 | tf_op jit(solution)/shard_map/all_to_all | solution.py:482
  163.8 3.7 all-to-all-start.1
  167.5 0.7 all-gather.3.cloned.1.call-update
  168.2 23.6 %all_gather.17 = f32[320,320]{1,0:T(8,128)S(1)} all-gather(f32[160,320]{1,0:T(8,128)S(1)} %copy-done.11), channel_id=1, replica_groups=mesh['wide'=16,'narrow'=2] {'narrow'}, dimensions={0}, use_global_device_ids=true | all-gather | bytes 614400 | tf_op jit(solution)/shard_map/all_gather | solution.py:519
  191.9 0.8 dynamic_slice.3
  192.7 0.1 broadcast_add_fusion
  192.7 0.1 slice.77.refs_6_
  192.8 0.1 reshape.141.refs_5_
  193.0 0.2 pad_bitcast_fusion.1
  193.2 0.1 pad_maximum_fusion.2.refs_3_
  193.2 0.1 fusion.10
  193.3 0.1 pad_maximum_fusion.refs_4_
  193.5 31.2 %all-gather.3.cloned.1.call-done.refs_1_ = f32[640,640]{1,0:T(8,128)} async-done(((f32[40,640]{1,0:T(8,128)}), f32[640,640]{1,0:T(8,128)}) %all-gather.3.cloned.1.call-update) | async-done | bytes 1638416 | tf_op jit(solution)/shard_map/all_gather | solution.py:520
  224.7 2.7 copy.31
  227.4 22.8 %middle.3 = (f32[16,2,5,5,8,128]{5,4,3,2,1,0:T(8,128)}, f32[8,128]{1,0:T(8,128)S(1)}) custom-call(f32[16,2,5,5,8,128]{5,4,3,2,1,0:T(8,128)} %bitcast.32, f32[640,640]{1,0:T(8,128)} %all-gather.3.cloned.1.call-done.refs_1_, f32[640,640]{1,0:T(8,128)} %bitcast.40, f32[2,256,384]{2,1,0:T(8,128)S(1)} %pad_maximum_fusion.2.refs_3_, ...), custom_call_target="tpu_custom_call" | custom-call | flops 9437184000 | bytes 6553600 | tf_op jit(solution)/shard_map/middle/pallas_call | solution.py:315
  250.2 1.2 all-to-all-done.1
  251.4 5.2 all-to-all-start.4
  256.6 0.1 slice.75.refs_6_
  256.7 1.4 copy-done.1
  258.1 1.1 copy-done.4
  259.2 1.0 copy-done.7
  260.2 22.8 %middle.4 = (f32[16,2,5,5,8,128]{5,4,3,2,1,0:T(8,128)}, f32[8,128]{1,0:T(8,128)S(1)}) custom-call(f32[16,2,5,5,8,128]{5,4,3,2,1,0:T(8,128)} %bitcast.13.refs_0_, f32[640,640]{1,0:T(8,128)} %all-gather.3.cloned.1.call-done.refs_1_, f32[640,640]{1,0:T(8,128)} %bitcast.41, f32[2,256,384]{2,1,0:T(8,128)S(1)} %copy-done.4, f32[4,256,384]{2,1,0:T(8,128)S(1)} %copy-done.1, ...), custom_call_target="tpu_custom_call" | custom-call | flops 9437184000 | bytes 6553600 | tf_op jit(solution)/shard_map/middle/pallas_call | solution.py:315
  283.0 47.7 %all-to-all-done.4.refs_0_ = f32[32,5,5,8,128]{4,3,2,1,0:T(8,128)S(1)} async-done(((f32[32,5,5,8,128]{4,3,2,1,0:T(8,128)}), f32[32,5,5,8,128]{4,3,2,1,0:T(8,128)S(1)}, u32[]{:S(2)}, u32[]{:S(2)}) %all-to-all-start.4) | async-done | bytes 3276832 | tf_op jit(solution)/shard_map/all_to_all | solution.py:482
  330.7 4.0 all-to-all-start.5
  334.7 0.1 slice.73.refs_6_
  334.7 1.4 copy-done.2
  336.2 1.1 copy-done.5
  337.3 1.0 copy-done.8
  338.3 12.6 %middle.5 = (f32[16,2,5,3,8,128]{5,4,3,2,1,0:T(8,128)}, f32[8,128]{1,0:T(8,128)}) custom-call(f32[16,2,5,3,8,128]{5,4,3,2,1,0:T(8,128)} %bitcast.37, f32[640,640]{1,0:T(8,128)} %all-gather.3.cloned.1.call-done.refs_1_, f32[640,640]{1,0:T(8,128)} %bitcast.42, f32[2,256,384]{2,1,0:T(8,128)S(1)} %copy-done.5, f32[4,256,384]{2,1,0:T(8,128)S(1)} %copy-done.2, ...), custom_call_target="tpu_custom_call" | custom-call | flops 4718592000 | bytes 3932160 | tf_op jit(solution)/shard_map/middle/pallas_call | solution.py:315
  350.9 57.8 %all-to-all-done.5.refs_1_ = f32[32,5,5,8,128]{4,3,2,1,0:T(8,128)} async-done(((f32[32,5,5,8,128]{4,3,2,1,0:T(8,128)}), f32[32,5,5,8,128]{4,3,2,1,0:T(8,128)}, u32[]{:S(2)}, u32[]{:S(2)}) %all-to-all-start.5) | async-done | bytes 3276832 | tf_op jit(solution)/shard_map/all_to_all | solution.py:482
  408.7 3.8 all-to-all-start.3
  412.5 1.0 slice.97
  413.5 1.0 slice.98
  415.2 0.1 copy.36
  415.3 9.8 %inverse_z.2.refs_2_ = f32[40,160,320]{2,1,0:T(8,128)} custom-call(f32[32,5,5,8,128]{4,3,2,1,0:T(8,128)S(1)} %all-to-all-done.4.refs_0_, f32[32,5,5,8,128]{4,3,2,1,0:T(8,128)} %all-to-all-done.5.refs_1_, f32[256,320]{1,0:T(8,128)S(1)} %bitcast.26), custom_call_target="tpu_custom_call" | custom-call | flops 3145728000 | bytes 16384000 | tf_op jit(solution)/shard_map/inverse_z/pallas_call | solution.py:188
  425.1 33.3 %all-to-all-done.3.refs_0_ = f32[32,5,3,8,128]{4,3,2,1,0:T(8,128)} async-done(((f32[32,5,3,8,128]{4,3,2,1,0:T(8,128)}), f32[32,5,3,8,128]{4,3,2,1,0:T(8,128)}, u32[]{:S(2)}, u32[]{:S(2)}) %all-to-all-start.3) | async-done | bytes 1966112 | tf_op jit(solution)/shard_map/all_to_all | solution.py:482
  458.4 14.6 %inverse_z.3 = (f32[40,160,320]{2,1,0:T(8,128)}, f32[8,128]{1,0:T(8,128)S(1)}) custom-call(f32[32,5,3,8,128]{4,3,2,1,0:T(8,128)} %all-to-all-done.3.refs_0_, f32[64,320]{1,0:T(8,128)S(1)} %bitcast.28, f32[40,160,320]{2,1,0:T(8,128)} %inverse_z.2.refs_2_, f32[40,160,320]{2,1,0:T(8,128)} %refs_3_.1, f32[1,1]{1,0:T(1,128)} %bitcast.25.refs_4_), custom_call_target="tpu_custom_call" | custom-call | flops 786432000 | bytes 16384000 | tf_op jit(solution)/shard_map/inverse_z/pallas_call | solution.py:188
  473.0 1.4 fusion.8
  474.4 1.3 collective-permute-start.6
  475.7 3.1 collective-permute-start.1
  478.8 1.2 fusion.9
  480.1 1.3 collective-permute-start.4
  481.4 4.6 collective-permute-start.3
  486.0 0.8 fusion.7
  486.8 1.3 collective-permute-start.7
  488.1 8.7 %collective-permute-done.7.refs_8_ = f32[3,8,320]{2,1,0:T(8,128)S(1)} collective-permute-done((f32[3,8,320]{2,1,0:T(8,128)S(1)}, f32[3,8,320]{2,1,0:T(8,128)S(1)}, u32[]{:S(2)}, u32[]{:S(2)}) %collective-permute-start.7) | collective-permute-done | bytes 30752 | tf_op jit(solution)/shard_map/ppermute | solution.py:357
  496.8 0.7 collective-permute-start.5
  497.5 0.7 collective-permute-start.2
  498.2 0.2 select_select_fusion
  498.4 9.1 %collective-permute-start = (f32[3,8,320]{2,1,0:T(8,128)S(1)}, f32[3,8,320]{2,1,0:T(8,128)S(1)}, u32[]{:S(2)}, u32[]{:S(2)}) collective-permute-start(f32[3,8,320]{2,1,0:T(8,128)S(1)} %get-tuple-element.30), channel_id=1, source_target_pairs={{0,3},{2,5},{4,7},{6,9},{8,11},{10,13},{12,15},{14,17},{16,19},{18... | collective-permute-start | bytes 92168 | tf_op jit(solution)/shard_map/ppermute | solution.py:357
  507.4 0.1 pad_maximum_fusion.1.refs_9_
  507.5 0.5 slice.82
  508.0 0.8 collective-permute-done.refs_0_
  508.8 54.4 %stencil.1 = (f32[40,160,320]{2,1,0:T(8,128)}, f32[8,128]{1,0:T(8,128)S(1)}) custom-call(f32[3,8,320]{2,1,0:T(8,128)S(1)} %collective-permute-done.refs_0_, f32[3,160,320]{2,1,0:T(8,128)S(1)} %collective-permute-done.1.refs_1_, f32[3,8,320]{2,1,0:T(8,128)S(1)} %collective-permute-done.2.refs_2_, f32[40,8,320]{2,1,0:T(8,128)S(1)} %collective-permute-done.3.refs_3_, ...), custom_call_target="tpu_custom_call" | custom-call | flops 11796480000 | bytes 16384000 | tf_op jit(solution)/shard_map/stencil/pallas_call | solution.py:451
  563.2 66.8 %all-gather = f32[256,128]{1,0:T(8,128)S(1)} all-gather(f32[8,128]{1,0:T(8,128)S(1)} %get-tuple-element.25), channel_id=2, replica_groups=mesh['wide'=16,'narrow'=2] {'wide','narrow'}, dimensions={0}, use_global_device_ids=true | all-gather | bytes 135168 | tf_op jit(solution)/shard_map/all_gather | solution.py:552
  630.0 0.7 slice_reduce_fusion
  632.0 12.1 %multiply_subtract_fusion = f32[40,160,320]{2,1,0:T(8,128)} fusion(f32[40,160,320]{2,1,0:T(8,128)} %field_ref.1, f32[40,160,320]{2,1,0:T(8,128)} %get-tuple-element.26, f32[]{:T(128)S(6)} %div.3), kind=kLoop, calls=%fused_computation | loop fusion | flops 4096000 | bytes 24576004 | tf_op jit(solution)/shard_map/sub | solution.py:554
  644.1 12.1 %multiply_add_fusion = f32[40,160,320]{2,1,0:T(8,128)} fusion(f32[40,160,320]{2,1,0:T(8,128)} %param.10, f32[40,160,320]{2,1,0:T(8,128)} %get-tuple-element.14.refs_4_, f32[]{:T(128)S(6)} %div.3), kind=kLoop, calls=%fused_computation.1 | loop fusion | flops 4096000 | bytes 24576004 | tf_op jit(solution)/shard_map/add | solution.py:554
  (35 shorter events, 0.2 us)
Async XLA Ops:
  17.3 16.1 %copy-start.9 = (f32[32,10,320]{2,1,0:T(8,128)}, f32[32,10,320]{2,1,0:T(8,128)S(1)}, u32[]{:S(2)}) copy-start(f32[32,10,320]{2,1,0:T(8,128)S(1)} %reshape.128) | copy-start | bytes 1228804
  33.4 51.8 %copy-start.10 = (f32[32,5,5,8,128]{4,3,2,1,0:T(8,128)S(1)}, f32[32,5,5,8,128]{4,3,2,1,0:T(8,128)}, u32[]{:S(2)}) copy-start(f32[32,5,5,8,128]{4,3,2,1,0:T(8,128)} %get-tuple-element.17) | copy-start | bytes 9830404
  163.8 4.4 copy-start.11
  163.8 28.8 %copy-start.13 = (f32[320]{0:T(512)S(1)}, f32[320]{0:T(512)}, u32[]{:S(2)}) copy-start(f32[320]{0:T(512)} %param.18) | copy-start | bytes 3844
  163.8 29.0 %copy-start.12 = (f32[640]{0:T(1024)S(1)}, f32[640]{0:T(1024)}, u32[]{:S(2)}) copy-start(f32[640]{0:T(1024)} %param.17) | copy-start | bytes 7684
  163.8 87.6 %all-to-all-start.1 = ((f32[32,5,5,8,128]{4,3,2,1,0:T(8,128)}), f32[32,5,5,8,128]{4,3,2,1,0:T(8,128)}, u32[]{:S(2)}, u32[]{:S(2)}) async-start(f32[32,5,5,8,128]{4,3,2,1,0:T(8,128)} %get-tuple-element.16), calls=%async_computation.1 | async-start | bytes 6553600 | tf_op jit(solution)/shard_map/all_to_all | solution.py:482
  167.5 57.2 %all-gather.3.cloned.1.call-start = ((), (), s32[]{:S(2)}) async-start(), calls=%async_computation.6 | async-start | bytes 1740800 | tf_op jit(solution)/shard_map/all_gather | solution.py:520
  193.0 34.5 %copy-start.6 = (f32[640,1]{1,0:T(8,128)}, f32[640,1]{1,0:T(8,128)S(1)}, u32[]{:S(2)}) copy-start(f32[640,1]{1,0:T(8,128)S(1)} %reshape.141.refs_5_) | copy-start | bytes 7684
  193.2 34.2 %copy-start.3 = (f32[2,256,384]{2,1,0:T(8,128)}, f32[2,256,384]{2,1,0:T(8,128)S(1)}, u32[]{:S(2)}) copy-start(f32[2,256,384]{2,1,0:T(8,128)S(1)} %pad_maximum_fusion.2.refs_3_) | copy-start | bytes 2359300
  193.5 56.8 %copy-start = (f32[4,256,384]{2,1,0:T(8,128)}, f32[4,256,384]{2,1,0:T(8,128)S(1)}, u32[]{:S(2)}) copy-start(f32[4,256,384]{2,1,0:T(8,128)S(1)} %pad_maximum_fusion.refs_4_) | copy-start | bytes 4718596
  251.4 79.3 %all-to-all-start.4 = ((f32[32,5,5,8,128]{4,3,2,1,0:T(8,128)}), f32[32,5,5,8,128]{4,3,2,1,0:T(8,128)S(1)}, u32[]{:S(2)}, u32[]{:S(2)}) async-start(f32[32,5,5,8,128]{4,3,2,1,0:T(8,128)} %bitcast.34), calls=%async_computation.4 | async-start | bytes 6553600 | tf_op jit(solution)/shard_map/all_to_all | solution.py:482
  256.7 1.4 copy-start.1
  258.1 1.1 copy-start.4
  259.2 1.0 copy-start.7
  330.7 78.0 %all-to-all-start.5 = ((f32[32,5,5,8,128]{4,3,2,1,0:T(8,128)}), f32[32,5,5,8,128]{4,3,2,1,0:T(8,128)}, u32[]{:S(2)}, u32[]{:S(2)}) async-start(f32[32,5,5,8,128]{4,3,2,1,0:T(8,128)} %bitcast.33), calls=%async_computation.5 | async-start | bytes 6553600 | tf_op jit(solution)/shard_map/all_to_all | solution.py:482
  334.7 1.4 copy-start.2
  336.1 1.1 copy-start.5
  337.3 1.0 copy-start.8
  408.7 49.7 %all-to-all-start.3 = ((f32[32,5,3,8,128]{4,3,2,1,0:T(8,128)}), f32[32,5,3,8,128]{4,3,2,1,0:T(8,128)}, u32[]{:S(2)}, u32[]{:S(2)}) async-start(f32[32,5,3,8,128]{4,3,2,1,0:T(8,128)} %bitcast.38), calls=%async_computation.3 | async-start | bytes 3932160 | tf_op jit(solution)/shard_map/all_to_all | solution.py:482
  474.4 34.4 %collective-permute-start.6 = (f32[3,160,320]{2,1,0:T(8,128)S(1)}, f32[3,160,320]{2,1,0:T(8,128)S(1)}, u32[]{:S(2)}, u32[]{:S(2)}) collective-permute-start(f32[3,160,320]{2,1,0:T(8,128)S(1)} %get-tuple-element.31), channel_id=1, source_target_pairs={{2,0},{3,1},{4,2},{5,3},{6,4},{7,5},{8,6},{9,7},{10,8},{11,9},{12,... | collective-permute-start | bytes 1843208 | tf_op jit(solution)/shard_map/ppermute | solution.py:357
  475.7 33.1 %collective-permute-start.1 = (f32[3,160,320]{2,1,0:T(8,128)S(1)}, f32[3,160,320]{2,1,0:T(8,128)S(1)}, u32[]{:S(2)}, u32[]{:S(2)}) collective-permute-start(f32[3,160,320]{2,1,0:T(8,128)S(1)} %get-tuple-element.32), channel_id=1, source_target_pairs={{0,2},{1,3},{2,4},{3,5},{4,6},{5,7},{6,8},{7,9},{8,10},{9,11},{10,... | collective-permute-start | bytes 1843208 | tf_op jit(solution)/shard_map/ppermute | solution.py:357
  480.1 28.8 %collective-permute-start.4 = (f32[40,8,320]{2,1,0:T(8,128)S(1)}, f32[40,8,320]{2,1,0:T(8,128)S(1)}, u32[]{:S(2)}, u32[]{:S(2)}) collective-permute-start(f32[40,8,320]{2,1,0:T(8,128)S(1)} %get-tuple-element.33), channel_id=1, source_target_pairs={{1,0},{3,2},{5,4},{7,6},{9,8},{11,10},{13,12},{15,14},{17,16},{19,... | collective-permute-start | bytes 1228808 | tf_op jit(solution)/shard_map/ppermute | solution.py:357
  481.4 27.5 %collective-permute-start.3 = (f32[40,8,320]{2,1,0:T(8,128)S(1)}, f32[40,8,320]{2,1,0:T(8,128)S(1)}, u32[]{:S(2)}, u32[]{:S(2)}) collective-permute-start(f32[40,8,320]{2,1,0:T(8,128)S(1)} %get-tuple-element.34), channel_id=1, source_target_pairs={{0,1},{2,3},{4,5},{6,7},{8,9},{10,11},{12,13},{14,15},{16,17},{18,... | collective-permute-start | bytes 1228808 | tf_op jit(solution)/shard_map/ppermute | solution.py:357
  486.8 10.0 %collective-permute-start.7 = (f32[3,8,320]{2,1,0:T(8,128)S(1)}, f32[3,8,320]{2,1,0:T(8,128)S(1)}, u32[]{:S(2)}, u32[]{:S(2)}) collective-permute-start(f32[3,8,320]{2,1,0:T(8,128)S(1)} %get-tuple-element.27), channel_id=1, source_target_pairs={{3,0},{5,2},{7,4},{9,6},{11,8},{13,10},{15,12},{17,14},{19,16},{21... | collective-permute-start | bytes 92168 | tf_op jit(solution)/shard_map/ppermute | solution.py:357
  496.8 0.7 collective-permute-start.5
  497.5 0.8 collective-permute-start.2
  498.4 10.5 %collective-permute-start = (f32[3,8,320]{2,1,0:T(8,128)S(1)}, f32[3,8,320]{2,1,0:T(8,128)S(1)}, u32[]{:S(2)}, u32[]{:S(2)}) collective-permute-start(f32[3,8,320]{2,1,0:T(8,128)S(1)} %get-tuple-element.30), channel_id=1, source_target_pairs={{0,3},{2,5},{4,7},{6,9},{8,11},{10,13},{12,15},{14,17},{16,19},{18... | collective-permute-start | bytes 92168 | tf_op jit(solution)/shard_map/ppermute | solution.py:357
Sparse Core Ops, SparseCore 0:
  170.5 54.1 all-gather.2

commit v2 on v1

--- a/solution.py
+++ b/solution.py
@@ -2,6 +2,8 @@
 
 import jax
 import jax.numpy as jnp
+import ml_dtypes
+import numpy as np
 from jax import lax
 from jax.experimental import pallas as pl
 from jax.experimental.pallas import tpu as pltpu
@@ -22,7 +24,7 @@
 HALO = 3
 EDGE = 8
 both = ("wide", "narrow")
-budget = 100 * 1024 * 1024 // 2
+MIB = 1024 * 1024
 
 
 def split(x):
@@ -61,15 +63,14 @@
         self.share = cells_z // self.count
         self.group = LANES // self.rest
         self.tiles = cells_x // 8
-        self.chunks = [
-            (start, min(self.group, self.share - start))
-            for start in range(0, self.share, self.group)
-        ]
+        self.chunks = [(0, self.group), (self.group, self.share - self.group)]
         self.fits = (
             self.group % 2 == 0
             and self.share % 2 == 0
-            and len(self.chunks) > 1
-            and self.chunks[-1][1] < self.group
+            and self.share > self.group
+            and self.share % self.group != 0
+            and self.tiles >= 3
+            and 2 * LANES < cells_z <= 3 * LANES
         )
 
     def rows(self, chunk):
@@ -77,12 +78,14 @@
         return start * self.count, size * self.count
 
     def message(self, chunk):
-        return (self.count, self.tiles, self.chunks[chunk][1] + 1, 8, LANES)
-
-
-def forward_kernel(plan, field_ref, basis_ref, *refs):
-    outs = refs[: len(plan.chunks)]
-    high_ref, low_ref, stage_ref = refs[len(plan.chunks) :]
+        return (self.count, self.tiles, self.pieces(chunk), 8, LANES)
+
+    def pieces(self, chunk):
+        size = self.chunks[chunk][1]
+        return size - (-size // self.group)
+
+
+def forward_kernel(plan, size, field_ref, basis_ref, out_ref, high_ref, low_ref, stage_ref):
 
     @pl.when(pl.program_id(0) == 0)
     def _():
@@ -91,118 +94,172 @@
     basis = (high_ref[...], low_ref[...])
     for i in range(8):
         stage_ref[i] = dot3(basis, split(field_ref[i]), (1, 1))
-    for chunk, (start, size) in enumerate(plan.chunks):
-        rests = []
-        for j in range(size):
-            at = (start + j) * plan.count
-            turned = jnp.swapaxes(stage_ref[:, at : at + plan.count, :], 0, 1)
-            outs[chunk][:, 0, j] = turned[:, :, :LANES]
-            rests.append(turned[:, :, LANES:])
-        while len(rests) < plan.group:
-            rests.append(jnp.zeros_like(rests[0]))
-        outs[chunk][:, 0, size] = jnp.concatenate(rests, axis=2)
-
-
-def forward_z(plan, field, basis):
-    shapes = [jax.ShapeDtypeStruct(plan.message(k), jnp.float32) for k in range(len(plan.chunks))]
+    rests = []
+    for j in range(size):
+        at = j * plan.count
+        turned = jnp.swapaxes(stage_ref[:, at : at + plan.count, :], 0, 1)
+        out_ref[:, 0, j] = turned[:, :, :LANES]
+        rests.append(turned[:, :, LANES:])
+    for piece, first in enumerate(range(0, size, plan.group)):
+        some = rests[first : first + plan.group]
+        some += [jnp.zeros_like(some[0])] * (plan.group - len(some))
+        out_ref[:, 0, size + piece] = jnp.concatenate(some, axis=2)
+
+
+def forward_z(plan, chunk, field, basis):
+    start, rows = plan.rows(chunk)
+    basis = basis[start : start + rows]
+    message = plan.message(chunk)
     return pl.pallas_call(
-        functools.partial(forward_kernel, plan),
+        functools.partial(forward_kernel, plan, plan.chunks[chunk][1]),
         grid=(plan.tiles,),
         in_specs=[
             pl.BlockSpec((8, plan.cells_y, plan.cells_z), lambda t: (t, 0, 0)),
             pl.BlockSpec(basis.shape, lambda t: (0, 0)),
         ],
-        out_specs=[
-            pl.BlockSpec((s.shape[0], 1) + s.shape[2:], lambda t: (0, t, 0, 0, 0)) for s in shapes
-        ],
-        out_shape=shapes,
+        out_specs=pl.BlockSpec((message[0], 1) + message[2:], lambda t: (0, t, 0, 0, 0)),
+        out_shape=jax.ShapeDtypeStruct(message, jnp.float32),
         scratch_shapes=[
             pltpu.VMEM(basis.shape, jnp.bfloat16),
             pltpu.VMEM(basis.shape, jnp.bfloat16),
-            pltpu.VMEM((8, plan.cells_z, plan.cells_y), jnp.float32),
+            pltpu.VMEM((8, rows, plan.cells_y), jnp.float32),
         ],
-        compiler_params=pltpu.CompilerParams(vmem_limit_bytes=budget),
+        compiler_params=pltpu.CompilerParams(vmem_limit_bytes=24 * MIB),
         cost_estimate=pl.CostEstimate(
-            flops=6 * field.size * plan.cells_z, bytes_accessed=8 * field.size, transcendentals=0
+            flops=6 * field.size * rows, bytes_accessed=8 * field.size, transcendentals=0
         ),
         name="forward_z",
     )(field, basis)
 
 
-def inverse_kernel(plan, chunks, final, *refs):
-    refs = list(refs)
-    parts = [refs.pop(0) for _ in chunks]
-    basis_ref = refs.pop(0)
-    if final:
-        base_ref, old_ref, before_ref = refs.pop(0), refs.pop(0), refs.pop(0)
-        out_ref, now_ref = refs.pop(0), refs.pop(0)
-    else:
-        out_ref = refs.pop(0)
-    high_ref, low_ref, stage_ref = refs
-
+def add_chunk(plan, size, part, stage_ref):
+    for j in range(size):
+        at, q = j * plan.count, j % plan.group
+        stage_ref[:, at : at + plan.count, :LANES] = jnp.swapaxes(part[:, 0, j], 0, 1)
+        stage_ref[:, at : at + plan.count, LANES:] = jnp.swapaxes(
+            part[:, 0, size + j // plan.group, :, q * plan.rest : (q + 1) * plan.rest], 0, 1
+        )
+
+
+def base_kernel(plan, size, part_ref, basis_ref, out_ref, high_ref, low_ref, stage_ref):
     @pl.when(pl.program_id(0) == 0)
     def _():
         high_ref[...], low_ref[...] = split(basis_ref[...])
 
-    at = 0
-    for part, chunk in zip(parts, chunks):
-        size = plan.chunks[chunk][1]
-        rests = part[:, 0, size]
-        for q in range(size):
-            stage_ref[:, at : at + plan.count, :LANES] = jnp.swapaxes(part[:, 0, q], 0, 1)
-            stage_ref[:, at : at + plan.count, LANES:] = jnp.swapaxes(
-                rests[:, :, q * plan.rest : (q + 1) * plan.rest], 0, 1
-            )
-            at += plan.count
-    if final:
-        sums = parts[-1][:, 0, plan.chunks[chunks[-1]][1], 0, LANES - 1 :]
-        now = jnp.sum(sums, axis=0, keepdims=True)
-        now_ref[...] = jnp.broadcast_to(now, now_ref.shape)
-        beta = now / before_ref[...]
+    add_chunk(plan, size, part_ref, stage_ref)
     basis = (high_ref[...], low_ref[...])
     for i in range(8):
-        value = dot3(split(stage_ref[i].T), basis, (1, 0))
-        if final:
-            value = base_ref[i] + value + beta * old_ref[i]
-        out_ref[i] = value
-
-
-def inverse_z(plan, parts, chunks, basis, base=None, old=None, before=None):
-    final = base is not None
-    brick = pl.BlockSpec((8, plan.cells_y, plan.cells_z), lambda t: (t, 0, 0))
-    shape = jax.ShapeDtypeStruct((plan.cells_x, plan.cells_y, plan.cells_z), jnp.float32)
-    low = plan.rows(chunks[0])[0]
-    high = sum(plan.rows(chunks[-1]))
-    basis = basis[low:high]
-    one = pl.BlockSpec((1, 1), lambda t: (0, 0))
+        out_ref[i] = dot3(split(stage_ref[i].T), basis, (1, 0))
+
+
+def final_kernel(plan, size, ends, part_ref, basis_ref, base_ref, old_ref, before_ref, *refs):
+    if ends:
+        out_ref, now_ref, high_ref, low_ref, stage_ref = refs
+    else:
+        done_ref, out_ref, high_ref, low_ref, stage_ref = refs
+    step = pl.program_id(0)
+
+    @pl.when(step == 0)
+    def _():
+        high_ref[...], low_ref[...] = split(basis_ref[...])
+
+    def work():
+        add_chunk(plan, size, part_ref, stage_ref)
+        sums = part_ref[:, 0, part_ref.shape[2] - 1, 0, LANES - 1 :]
+        now = jnp.sum(sums, axis=0, keepdims=True)
+        beta = now / before_ref[...]
+        basis = (high_ref[...], low_ref[...])
+        for i in range(8):
+            value = dot3(split(stage_ref[i].T), basis, (1, 0))
+            out_ref[i] = base_ref[i] + value + beta * old_ref[i]
+        if ends:
+            now_ref[...] = jnp.broadcast_to(now, now_ref.shape)
+
+    if ends:
+        work()
+    else:
+        inner = (step > 0) & (step < plan.tiles - 1)
+        pl.when(inner)(work)
+
+        @pl.when(jnp.logical_not(inner))
+        def _():
+            out_ref[...] = done_ref[...]
+
+
+def inverse_scratch(plan, basis):
+    return [
+        pltpu.VMEM(basis.shape, jnp.bfloat16),
+        pltpu.VMEM(basis.shape, jnp.bfloat16),
+        pltpu.VMEM((8, basis.shape[0], plan.cells_y), jnp.float32),
+    ]
+
+
+def inverse_cost(plan, basis, tiles):
+    size = tiles * 8 * plan.cells_y * plan.cells_z
+    return pl.CostEstimate(
+        flops=6 * size * basis.shape[0], bytes_accessed=12 * size, transcendentals=0
+    )
+
+
+def inverse_base(plan, chunk, part, basis):
+    start, rows = plan.rows(chunk)
+    basis = basis[start : start + rows]
+    return pl.pallas_call(
+        functools.partial(base_kernel, plan, plan.chunks[chunk][1]),
+        grid=(plan.tiles,),
+        in_specs=[
+            pl.BlockSpec((part.shape[0], 1) + part.shape[2:], lambda t: (0, t, 0, 0, 0)),
+            pl.BlockSpec(basis.shape, lambda t: (0, 0)),
+        ],
+        out_specs=pl.BlockSpec((8, plan.cells_y, plan.cells_z), lambda t: (t, 0, 0)),
+        out_shape=jax.ShapeDtypeStruct((plan.cells_x, plan.cells_y, plan.cells_z), jnp.float32),
+        scratch_shapes=inverse_scratch(plan, basis),
+        compiler_params=pltpu.CompilerParams(vmem_limit_bytes=24 * MIB),
+        cost_estimate=inverse_cost(plan, basis, plan.tiles),
+        name="inverse_base",
+    )(part, basis)
+
+
+def inverse_final(plan, chunk, part, basis, base, old, before, done=None):
+    ends = done is None
+    start, rows = plan.rows(chunk)
+    basis = basis[start : start + rows]
+    last = plan.tiles - 1
+    if ends:
+        pick = lambda t: t * last
+    else:
+        pick = lambda t: jnp.clip(t, 1, last - 1)
+    tile = (8, plan.cells_y, plan.cells_z)
+    brick = pl.BlockSpec(tile, lambda t: (pick(t), 0, 0))
     in_specs = [
-        pl.BlockSpec((p.shape[0], 1) + p.shape[2:], lambda t: (0, t, 0, 0, 0)) for p in parts
-    ] + [pl.BlockSpec(basis.shape, lambda t: (0, 0))]
-    operands = list(parts) + [basis]
-    out_specs, out_shape = brick, shape
-    if final:
-        in_specs += [brick, brick, one]
-        operands += [base, old, before.reshape(1, 1)]
-        out_specs = [brick, pl.BlockSpec((8, LANES), lambda t: (0, 0))]
-        out_shape = [shape, jax.ShapeDtypeStruct((8, LANES), jnp.float32)]
+        pl.BlockSpec((part.shape[0], 1) + part.shape[2:], lambda t: (0, pick(t), 0, 0, 0)),
+        pl.BlockSpec(basis.shape, lambda t: (0, 0)),
+        brick,
+        brick,
+        pl.BlockSpec((1, 1), lambda t: (0, 0)),
+    ]
+    operands = [part, basis, base, old, before.reshape(1, 1)]
+    out_specs = pl.BlockSpec(tile, lambda t: (t, 0, 0))
+    if ends:
+        out_specs = [out_specs, pl.BlockSpec((8, LANES), lambda t: (0, 0))]
+        out_shape = [
+            jax.ShapeDtypeStruct((16,) + base.shape[1:], jnp.float32),
+            jax.ShapeDtypeStruct((8, LANES), jnp.float32),
+        ]
+    else:
+        in_specs.append(pl.BlockSpec(tile, lambda t: (t // last, 0, 0)))
+        operands.append(done)
+        out_shape = jax.ShapeDtypeStruct(base.shape, jnp.float32)
     return pl.pallas_call(
-        functools.partial(inverse_kernel, plan, chunks, final),
-        grid=(plan.tiles,),
+        functools.partial(final_kernel, plan, plan.chunks[chunk][1], ends),
+        grid=(2 if ends else plan.tiles,),
         in_specs=in_specs,
         out_specs=out_specs,
         out_shape=out_shape,
-        scratch_shapes=[
-            pltpu.VMEM(basis.shape, jnp.bfloat16),
-            pltpu.VMEM(basis.shape, jnp.bfloat16),
-            pltpu.VMEM((8, high - low, plan.cells_y), jnp.float32),
-        ],
-        compiler_params=pltpu.CompilerParams(vmem_limit_bytes=budget),
-        cost_estimate=pl.CostEstimate(
-            flops=6 * shape.size * (high - low),
-            bytes_accessed=8 * shape.size,
-            transcendentals=0,
-        ),
-        name="inverse_z",
+        scratch_shapes=inverse_scratch(plan, basis),
+        compiler_params=pltpu.CompilerParams(vmem_limit_bytes=28 * MIB),
+        cost_estimate=inverse_cost(plan, basis, 2 if ends else plan.tiles - 2),
+        name="inverse_ends" if ends else "inverse_inner",
     )(*operands)
 
 
@@ -253,13 +310,14 @@
 
     def pair(p, total):
         for h in range(2):
-            rest = split(gathered(size, h))
+            rest = split(gathered(size + 2 * p // plan.group, h))
             parts = []
             for s in range(2):
                 j = 2 * p + s
+                q = lax.rem(j, plan.group)
                 parts.append(
                     dot3(split(gathered(j, h)), (my_high[s], my_low[s]), (1, 0))
-                    + dot3(rest, (ry_high[j], ry_low[j]), (1, 0))
+                    + dot3(rest, (ry_high[q], ry_low[q]), (1, 0))
                 )
             cut = span - LANES
             joined = jnp.concatenate(
@@ -288,7 +346,10 @@
                 j = 2 * p + s
                 mine = split(value[:, s * (width - span) : s * (width - span) + span])
                 main = dot3(mine, (my_high[s], my_low[s]), (1, 1))
-                rest_acc[rows, :] += dot3(mine, (ry_high[j], ry_low[j]), (1, 1))
+                q = lax.rem(j, plan.group)
+                rest_acc[2 * p // plan.group, rows, :] += dot3(
+                    mine, (ry_high[q], ry_low[q]), (1, 1)
+                )
                 for n in range(narrow):
                     out_ref[pl.ds(h * lump, lump), n, :, j] = main[
                         :, n * LANES : (n + 1) * LANES
@@ -298,12 +359,14 @@
     total = lax.fori_loop(0, size // 2, pair, jnp.zeros((8, width), jnp.float32))
     value = total_ref[...] + jnp.sum(total)
     sum_ref[...] = value
-    for n in range(narrow):
-        rest = rest_acc[:, n * LANES : (n + 1) * LANES]
-        if last:
-            lane = lax.broadcasted_iota(jnp.int32, rest.shape, 1)
-            rest = jnp.where(lane >= size * plan.rest, value[:1, :], rest)
-        out_ref[:, n, :, size] = rest.reshape(wide, tiles, 8, LANES)
+    pieces = in_ref.shape[3] - size
+    for piece in range(pieces):
+        for n in range(narrow):
+            rest = rest_acc[piece, :, n * LANES : (n + 1) * LANES]
+            if last and piece == pieces - 1:
+                lane = lax.broadcasted_iota(jnp.int32, rest.shape, 1)
+                rest = jnp.where(lane == LANES - 1, value[:1, :], rest)
+            out_ref[:, n, :, size + piece] = rest.reshape(wide, tiles, 8, LANES)
 
 
 def middle(plan, chunk, message, basis_x, turned_x, main_y, rest_y, eigen_x, shift, total):
@@ -333,9 +396,9 @@
             pltpu.VMEM(pencil, half),
             pltpu.VMEM(pencil, half),
             pltpu.VMEM(pencil, half),
-            pltpu.VMEM((plan.total_x, plan.narrow * LANES), jnp.float32),
+            pltpu.VMEM((plan.pieces(chunk) - size, plan.total_x, plan.narrow * LANES), jnp.float32),
         ],
-        compiler_params=pltpu.CompilerParams(vmem_limit_bytes=budget),
+        compiler_params=pltpu.CompilerParams(vmem_limit_bytes=44 * MIB),
         cost_estimate=pl.CostEstimate(
             flops=12 * size * plan.total_x * plan.total_y * (plan.total_x + plan.total_y),
             bytes_accessed=8 * message.size,
@@ -346,113 +409,144 @@
     return out.reshape(message.shape), total
 
 
-def shifted(x, step_wide, step_narrow):
-    wide, narrow = lax.axis_size("wide"), lax.axis_size("narrow")
-    pairs = []
-    for w in range(wide):
-        for n in range(narrow):
-            v, m = w + step_wide, n + step_narrow
-            if 0 <= v < wide and 0 <= m < narrow:
-                pairs.append((v * narrow + m, w * narrow + n))
-    return lax.ppermute(x, both, pairs)
+def shifted(x, step, axis):
+    count = lax.axis_size(axis)
+    pairs = [(i + step, i) for i in range(count) if 0 <= i + step < count]
+    return lax.ppermute(x, axis, pairs)
+
+
+def from_sides(low, high, axis):
+    if lax.axis_size(axis) != 2:
+        return shifted(high, -1, axis), shifted(low, 1, axis)
+    second = lax.axis_index(axis) == 1
+    got = lax.ppermute(jnp.where(second, low, high), axis, [(0, 1), (1, 0)])
+    return jnp.where(second, got, 0.0), jnp.where(second, 0.0, got)
+
+
+mass_scale, stiff_scale = 5040.0, 120.0
+CUT = LANES + LANES // 2
+GROUP = 4
+
+
+def band_matrices(cells_z):
+    offset = np.arange(cells_z)[:, None] - np.arange(cells_z)[None, :]
+    near = np.abs(offset) <= HALO
+    tables = []
+    for band, scale in ((mass_band, mass_scale), (stiff_band, stiff_scale)):
+        whole = np.rint(np.asarray(band) * scale)
+        full = np.where(near, whole[np.clip(offset + HALO, 0, 2 * HALO)], 0.0)
+        first = np.zeros((2 * LANES, 2 * LANES))
+        first[:, :CUT] = full[: 2 * LANES, :CUT]
+        second = np.zeros((2 * LANES, 2 * LANES))
+        second[: cells_z - LANES, CUT - LANES : cells_z - LANES] = full[LANES:, CUT:]
+        tables.append(np.stack([first, second]).astype(np.float32))
+    mass, stiff = tables
+    high = mass.astype(ml_dtypes.bfloat16)
+    low = (mass - high.astype(np.float32)).astype(ml_dtypes.bfloat16)
+    return np.stack([high, low, stiff.astype(ml_dtypes.bfloat16)])
 
 
 def stencil_kernel(plan, *refs):
-    pieces = refs[:9]
-    bands_ref, image_ref, sum_ref, field, high_a, low_a, h_a, h_b, total, sems = refs[9:]
+    pieces = refs[:5]
+    bands_ref, image_ref, sum_ref, field, f_high, f_low, s_high, s_low, h_a, h_b, total, sems = refs[5:]
     cells_x, cells_y, cells_z = plan.cells_x, plan.cells_y, plan.cells_z
-    xs = (pl.ds(0, HALO), pl.ds(HALO, cells_x), pl.ds(HALO + cells_x, HALO))
-    ys = (pl.ds(0, EDGE), pl.ds(EDGE, cells_y), pl.ds(EDGE + cells_y, EDGE))
+    padded_y = cells_y + 2 * EDGE
+    own_y = pl.ds(EDGE, cells_y)
+    places = (
+        (pl.ds(HALO, cells_x), own_y),
+        (pl.ds(0, HALO), own_y),
+        (pl.ds(HALO + cells_x, HALO), own_y),
+        (pl.ds(0, cells_x + 2 * HALO), pl.ds(0, EDGE)),
+        (pl.ds(0, cells_x + 2 * HALO), pl.ds(EDGE + cells_y, EDGE)),
+    )
     step = pl.program_id(0)
 
     @pl.when(step == 0)
     def _():
         copies = [
-            pltpu.make_async_copy(
-                pieces[3 * a + b], field.at[xs[a], ys[b], :], sems.at[3 * a + b]
-            )
-            for a in range(3)
-            for b in range(3)
+            pltpu.make_async_copy(piece, field.at[xs, ys, :], sems.at[i])
+            for i, (piece, (xs, ys)) in enumerate(zip(pieces, places))
         ]
         for copy in copies:
             copy.start()
         total[...] = jnp.zeros_like(total)
-        high_a[...], low_a[...] = split(bands_ref[...])
         for copy in copies:
             copy.wait()
 
-    mass_z = (high_a[0], low_a[0])
-    stiff_z = (high_a[1], low_a[1])
-    padded_y = cells_y + 2 * EDGE
-    blocks = -(-cells_z // LANES)
-
-    def plane(i, carry):
-        x = step * 8 + i
-        middle_plane = field[x + HALO]
-        first = stiff_band[HALO] * middle_plane
-        second = mass_band[HALO] * middle_plane
-        for o in range(1, HALO + 1):
-            around = field[x + HALO - o] + field[x + HALO + o]
-            first = first + stiff_band[HALO + o] * around
-            second = second + mass_band[HALO + o] * around
-        first, second = split(first), split(second)
-        a = dot3(first, mass_z, (1, 0)) + dot3(second, stiff_z, (1, 0))
-        b = dot3(second, mass_z, (1, 0))
-        for k in range(blocks):
-            lanes = min(LANES, cells_z - k * LANES)
-            h_a[k, :, :lanes] = a[:, k * LANES : k * LANES + lanes]
-            h_b[k, :, :lanes] = b[:, k * LANES : k * LANES + lanes]
-        for k in range(blocks):
-            lanes = min(LANES, cells_z - k * LANES)
-            at = lambda ref, o: ref[k, pl.ds(EDGE + o, cells_y), :]
-            image = mass_band[HALO] * at(h_a, 0) + stiff_band[HALO] * at(h_b, 0)
+    blocks = h_a.shape[0]
+    ratio = stiff_scale / mass_scale
+
+    def one(left, right):
+        return lax.dot_general(
+            left, right, (((1,), (0,)), ((), ())), preferred_element_type=jnp.float32
+        )
+
+    def planes(g, carry):
+        for i in range(GROUP):
+            x = step * 8 + g * GROUP + i
+            middle_plane = field[x + HALO]
+            first = ratio * stiff_band[HALO] * middle_plane
+            second = mass_band[HALO] * middle_plane
             for o in range(1, HALO + 1):
-                image = image + mass_band[HALO + o] * (at(h_a, -o) + at(h_a, o))
-                image = image + stiff_band[HALO + o] * (at(h_b, -o) + at(h_b, o))
-            here = pl.ds(k * LANES, lanes)
-            image_ref[i, :, here] = image[:, :lanes]
-            product = image[:, :lanes] * field[x + HALO, pl.ds(EDGE, cells_y), here]
-            total[:, here] += jnp.sum(product.reshape(cells_y // 8, 8, lanes), axis=0)
+                around = field[x + HALO - o] + field[x + HALO + o]
+                first = first + ratio * stiff_band[HALO + o] * around
+                second = second + mass_band[HALO + o] * around
+            rows = pl.ds(i * padded_y, padded_y)
+            f_high[rows, :], f_low[rows, :] = split(first)
+            s_high[rows, :], s_low[rows, :] = split(second)
+        window_a, window_b = [], []
+        for w, lanes in enumerate((pl.ds(0, 2 * LANES), pl.ds(LANES, cells_z - LANES))):
+            high, low, stiff = (bands_ref[k, w, : lanes.size, :] for k in range(3))
+            fh, fl, sh, sl = (ref[:, lanes] for ref in (f_high, f_low, s_high, s_low))
+            window_a.append(
+                one(fh, high) + one(fl, high) + one(fh, low) + one(sh, stiff) + one(sl, stiff)
+            )
+            window_b.append(one(sh, high) + one(sl, high) + one(sh, low))
+        for ref, (left, right) in ((h_a, window_a), (h_b, window_b)):
+            ref[0] = left[:, :LANES]
+            ref[1] = left[:, LANES:] + right[:, :LANES]
+            ref[2] = right[:, LANES:]
+        for i in range(GROUP):
+            plane = g * GROUP + i
+            for k in range(blocks):
+                lanes = min(LANES, cells_z - k * LANES)
+                at = lambda ref, o: ref[k, pl.ds(i * padded_y + EDGE + o, cells_y), :]
+                image = (mass_band[HALO] / stiff_scale) * at(h_a, 0)
+                image = image + (stiff_band[HALO] / mass_scale) * at(h_b, 0)
+                for o in range(1, HALO + 1):
+                    image = image + (mass_band[HALO + o] / stiff_scale) * (at(h_a, -o) + at(h_a, o))
+                    image = image + (stiff_band[HALO + o] / mass_scale) * (at(h_b, -o) + at(h_b, o))
+                here = pl.ds(k * LANES, lanes)
+                image_ref[plane, :, here] = image[:, :lanes]
+                product = image[:, :lanes] * field[step * 8 + plane + HALO, own_y, here]
+                total[:, here] += jnp.sum(product.reshape(cells_y // 8, 8, lanes), axis=0)
         return carry
 
-    lax.fori_loop(0, 8, plane, 0)
+    lax.fori_loop(0, 8 // GROUP, planes, 0)
 
     @pl.when(step == pl.num_programs(0) - 1)
     def _():
         sum_ref[...] = jnp.full(sum_ref.shape, jnp.sum(total[...]), jnp.float32)
 
 
-def stencil(plan, direction):
+def stencil(plan, direction, before_x, after_x):
     cells_x, cells_y, cells_z = direction.shape
-    low_x, high_x = direction[:HALO], direction[cells_x - HALO :]
-    low_y, high_y = direction[:, :EDGE], direction[:, cells_y - EDGE :]
-    pieces = [
-        shifted(high_x[:, cells_y - EDGE :], -1, -1),
-        shifted(high_x, -1, 0),
-        shifted(high_x[:, :EDGE], -1, 1),
-        shifted(high_y, 0, -1),
-        direction,
-        shifted(low_y, 0, 1),
-        shifted(low_x[:, cells_y - EDGE :], 1, -1),
-        shifted(low_x, 1, 0),
-        shifted(low_x[:, :EDGE], 1, 1),
-    ]
-    rows = lax.broadcasted_iota(jnp.int32, (cells_z, cells_z), 0)
-    columns = lax.broadcasted_iota(jnp.int32, (cells_z, cells_z), 1)
-    bands = []
-    for band in (mass_band, stiff_band):
-        matrix = jnp.zeros((cells_z, cells_z), jnp.float32)
-        for o in range(-HALO, HALO + 1):
-            matrix = jnp.where(rows - columns == o, band[o + HALO], matrix)
-        bands.append(matrix)
-    bands = jnp.stack(bands)
+
+    def strip(rows):
+        return jnp.concatenate([before_x[:, rows], direction[:, rows], after_x[:, rows]], axis=0)
+
+    before_y, after_y = from_sides(
+        strip(slice(0, EDGE)), strip(slice(cells_y - EDGE, cells_y)), "narrow"
+    )
+    bands = band_matrices(cells_z)
     padded_y = cells_y + 2 * EDGE
     blocks = -(-cells_z // LANES)
+    lump = (GROUP * padded_y, cells_z)
     return pl.pallas_call(
         functools.partial(stencil_kernel, plan),
         grid=(cells_x // 8,),
-        in_specs=[pl.BlockSpec(memory_space=pl.ANY)] * 9
-        + [pl.BlockSpec(bands.shape, lambda t: (0, 0, 0))],
+        in_specs=[pl.BlockSpec(memory_space=pl.ANY)] * 5
+        + [pl.BlockSpec(bands.shape, lambda t: (0, 0, 0, 0))],
         out_specs=[
             pl.BlockSpec((8, cells_y, cells_z), lambda t: (t, 0, 0)),
             pl.BlockSpec((8, LANES), lambda t: (0, 0)),
@@ -463,19 +557,21 @@
         ],
         scratch_shapes=[
             pltpu.VMEM((cells_x + 2 * HALO, padded_y, cells_z), jnp.float32),
-            pltpu.VMEM(bands.shape, jnp.bfloat16),
-            pltpu.VMEM(bands.shape, jnp.bfloat16),
-            pltpu.VMEM((blocks, padded_y, LANES), jnp.float32),
-            pltpu.VMEM((blocks, padded_y, LANES), jnp.float32),
+            pltpu.VMEM(lump, jnp.bfloat16),
+            pltpu.VMEM(lump, jnp.bfloat16),
+            pltpu.VMEM(lump, jnp.bfloat16),
+            pltpu.VMEM(lump, jnp.bfloat16),
+            pltpu.VMEM((blocks, GROUP * padded_y, LANES), jnp.float32),
+            pltpu.VMEM((blocks, GROUP * padded_y, LANES), jnp.float32),
             pltpu.VMEM((8, cells_z), jnp.float32),
-            pltpu.SemaphoreType.DMA((9,)),
+            pltpu.SemaphoreType.DMA((5,)),
         ],
-        compiler_params=pltpu.CompilerParams(vmem_limit_bytes=budget),
+        compiler_params=pltpu.CompilerParams(vmem_limit_bytes=36 * MIB),
         cost_estimate=pl.CostEstimate(
-            flops=18 * direction.size * cells_z, bytes_accessed=8 * direction.size, transcendentals=0
+            flops=8 * direction.size * cells_z, bytes_accessed=8 * direction.size, transcendentals=0
         ),
         name="stencil",
-    )(*pieces, bands)
+    )(direction, before_x, after_x, before_y, after_y, bands)
 
 
 def scatter(x):
@@ -516,16 +612,18 @@
     eigen_z,
 ):
     whole_z = lax.all_gather(basis_z, "narrow", axis=0, tiled=True)
+    turned_z = dealt(plan, whole_z)
     whole_y = lax.all_gather(basis_y, "narrow", axis=0, tiled=True)
     whole_x = lax.all_gather(basis_x, "wide", axis=0, tiled=True)
-    turned_z = dealt(plan, whole_z)
-    messages = forward_z(plan, residual, turned_z)
+    sent = [forward_z(plan, k, residual, turned_z) for k in range(2)]
+    arrived = [scatter(sent[0])]
+    later, whole_x, whole_y = lax.optimization_barrier((sent[1], whole_x, whole_y))
+    arrived.append(scatter(later))
     main_y, rest_y = basis_y_blocks(plan, whole_y)
     turned_x = whole_x.T
     index = lax.axis_index("wide") * plan.narrow + lax.axis_index("narrow")
     mine_z = lax.dynamic_slice_in_dim(eigen_z, index * plan.share, plan.share)
     shifts = (mine_z[:, None] + eigen_y[None, :]).reshape(plan.share // 2, 1, 2 * plan.total_y)
-    arrived = [scatter(m) for m in messages]
     total = jnp.zeros((8, LANES), jnp.float32)
     returned = []
     for k, (start, size) in enumerate(plan.chunks):
@@ -543,13 +641,16 @@
             total,
         )
         returned.append(scatter(back))
-    last = len(plan.chunks) - 1
-    base = inverse_z(plan, returned[:last], tuple(range(last)), turned_z)
-    direction, now = inverse_z(
-        plan, returned[last:], (last,), turned_z, base, direction, previous_product
-    )
-    image, part = stencil(plan, direction)
-    parts = lax.all_gather(part, both, axis=0, tiled=False)
+    base = inverse_base(plan, 0, returned[0], turned_z)
+    inverse = functools.partial(
+        inverse_final, plan, 1, returned[1], turned_z, base, direction, previous_product
+    )
+    ends, now = inverse()
+    before_x = shifted(ends[16 - HALO :], -1, "wide")
+    after_x = shifted(ends[:HALO], 1, "wide")
+    direction = inverse(ends)
+    image, part = stencil(plan, direction, before_x, after_x)
+    parts = scatter(jnp.broadcast_to(part[None], (plan.count,) + part.shape))
     alpha = now[0, 0] / jnp.sum(parts[:, 0, 0])
     return solution + alpha * direction, residual - alpha * image, direction
 

time: 668 us -> 570 us (0.85)
  blocking collectives: 231 us -> 33.4 us
  waiting for transfers between devices: 181 us -> 298 us
  local copies, waits for them, and re-layouts: 17.9 us -> 50.3 us
  Pallas kernels: 153 us -> 124 us
  starting transfers between devices: 38.6 us -> 24.7 us
    all_to_all x2 -> x0, blocking collectives: 130 us -> none  [scatter(): return lax.all_to_all(x, both, split_axis=0, concat_axis=0, tiled=True)]
    all_to_all x4 -> x5, waiting for transfers between devices: 140 us -> 264 us  [scatter(): return lax.all_to_all(x, both, split_axis=0, concat_axis=0, tiled=True)]
    all_gather x1 -> x0, blocking collectives: 66.8 us -> none  [by_pencils(): parts = lax.all_gather(part, both, axis=0, tiled=False)]
    unnamed x28 -> x54, local copies, waits for them, and re-layouts: 7.06 us -> 39.5 us
    pallas_call x1, Pallas kernels: 54.4 us -> 33.4 us  [stencil(): pl.pallas_call(functools.partial(stencil_kernel, plan), grid=(cells_x //...]
    ppermute x8 -> x3, starting transfers between devices: 22 us -> 4.74 us  [the longest x2 4.62 us: shifted(): return lax.ppermute(x, axis, pairs)]
    all_gather x1, waiting for transfers between devices: 31.2 us -> 17.8 us  [by_pencils(): whole_x = lax.all_gather(basis_x, 'wide', axis=0, tiled=True)]
    add x1 -> x0, other arithmetic: 12.1 us -> none  [by_pencils(): return (solution + alpha * direction, residual - alpha * image, direction)]
  transfers between devices with their start and end apart: 13 -> 9, of which waited for: 7 -> 7; matrix products, arithmetic and copies ran while one was open for 1% -> 2% of each run, Pallas kernels for 10% -> 13%
where the time goes in v2:
time: 570 us; the launch traced here: 569 us
  waiting for transfers between devices  298 us (52%)
  Pallas kernels  124 us (22%)
  local copies, waits for them, and re-layouts  50.3 us (9%)
  blocking collectives  33.4 us (6%)
  starting transfers between devices  24.7 us (4%)
  other arithmetic  22.5 us (4%)
  between operations  16.4 us (3%)
    all_to_all x5, waiting for transfers between devices, scatter(): return lax.all_to_all(x, both, split_axis=0, concat_axis=0, tiled=True)  264 us
    pallas_call x2, Pallas kernels, middle(): pl.pallas_call(functools.partial(middle_kernel, plan, chunk), out_shape=[...  52 us
    unnamed x54, local copies, waits for them, and re-layouts  39.5 us
    pallas_call x1, Pallas kernels, stencil(): pl.pallas_call(functools.partial(stencil_kernel, plan), grid=(cells_x //...  33.4 us
    all_gather x1, blocking collectives, by_pencils(): whole_y = lax.all_gather(basis_y, 'narrow', axis=0, tiled=True)  23.6 us
    sub x1, other arithmetic, by_pencils(): return (solution + alpha * direction, residual - alpha * image, direction)  21.5 us
    all_to_all x5, starting transfers between devices, scatter(): return lax.all_to_all(x, both, split_axis=0, concat_axis=0, tiled=True)  19.9 us
    all_gather x1, waiting for transfers between devices, by_pencils(): whole_x = lax.all_gather(basis_x, 'wide', axis=0, tiled=True)  17.8 us
  transfers between devices with their start and end apart: 9, of which 7 were waited for; matrix products, arithmetic and copies ran while one was open for 2% of the time, Pallas kernels for 13%

profile of v2, /device:TPU:0, one launch (start us, length us, event | category | flops | bytes accessed | tf_op | source)
XLA Modules:
  0.0 569.2 jit_solution(13347906064521233795)
XLA Ops:
  7.2 9.9 %all_gather.9 = f32[320,320]{1,0:T(8,128)S(1)} all-gather(f32[160,320]{1,0:T(8,128)} %param.17), channel_id=1, replica_groups=mesh['wide'=16,'narrow'=2] {'narrow'}, dimensions={0}, use_global_device_ids=true | all-gather | bytes 614400 | tf_op jit(solution)/shard_map/all_gather | solution.py:614
  17.0 0.2 copy.38
  17.2 0.1 reshape.44
  17.4 3.8 copy-done
  21.2 8.6 %forward_z.3 = f32[32,5,5,8,128]{4,3,2,1,0:T(8,128)} custom-call(f32[40,160,320]{2,1,0:T(8,128)S(1)} %copy-done, f32[128,320]{1,0:T(8,128)S(1)} %bitcast.27), custom_call_target="tpu_custom_call" | custom-call | flops 1572864000 | bytes 16384000 | tf_op jit(solution)/shard_map/forward_z/pallas_call | solution.py:113
  29.7 6.1 %all-to-all-start.1 = ((f32[32,5,5,8,128]{4,3,2,1,0:T(8,128)}), f32[32,5,5,8,128]{4,3,2,1,0:T(8,128)}, u32[]{:S(2)}, u32[]{:S(2)}) async-start(f32[32,5,5,8,128]{4,3,2,1,0:T(8,128)} %forward_z.3), calls=%async_computation.1 | async-start | bytes 6553600 | tf_op jit(solution)/shard_map/all_to_all | solution.py:578
  35.9 0.7 all-gather.2.cloned.1.call-update
  36.7 23.6 %all_gather.11 = f32[320,320]{1,0:T(8,128)S(1)} all-gather(f32[160,320]{1,0:T(8,128)S(1)} %copy-done.24), channel_id=1, replica_groups=mesh['wide'=16,'narrow'=2] {'narrow'}, dimensions={0}, use_global_device_ids=true | all-gather | bytes 614400 | tf_op jit(solution)/shard_map/all_gather | solution.py:616
  60.3 3.8 copy-done.1
  64.1 8.7 %forward_z.2 = f32[32,5,8,8,128]{4,3,2,1,0:T(8,128)S(1)} custom-call(f32[40,160,320]{2,1,0:T(8,128)S(1)} %copy-done.1, f32[192,320]{1,0:T(8,128)S(1)} %bitcast.23), custom_call_target="tpu_custom_call" | custom-call | flops 2359296000 | bytes 16384000 | tf_op jit(solution)/shard_map/forward_z/pallas_call | solution.py:113
  72.8 2.3 copy-done.5
  75.2 17.8 %all-gather.2.cloned.1.call-done.refs_1_ = f32[640,640]{1,0:T(8,128)} async-done(((f32[40,640]{1,0:T(8,128)}), f32[640,640]{1,0:T(8,128)}) %all-gather.2.cloned.1.call-update) | async-done | bytes 1638416 | tf_op jit(solution)/shard_map/all_gather | solution.py:617
  93.0 26.8 %all-to-all-done.1 = f32[32,5,5,8,128]{4,3,2,1,0:T(8,128)} async-done(((f32[32,5,5,8,128]{4,3,2,1,0:T(8,128)}), f32[32,5,5,8,128]{4,3,2,1,0:T(8,128)}, u32[]{:S(2)}, u32[]{:S(2)}) %all-to-all-start.1) | async-done | bytes 3276832 | tf_op jit(solution)/shard_map/all_to_all | solution.py:578
  119.8 4.1 all-to-all-start
  123.9 0.8 dynamic_slice.3
  124.6 0.1 broadcast_add_fusion
  124.7 0.1 slice.72.refs_6_
  124.8 0.9 reshape.53.refs_5_
  125.7 0.7 slice.85
  126.3 0.8 slice.84
  127.1 1.0 copy.40
  128.2 1.9 pad_bitcast_fusion.1
  130.1 1.5 fusion.4
  131.6 0.1 pad_maximum_fusion.refs_4_
  131.8 20.1 %middle.2 = (f32[16,2,5,5,8,128]{5,4,3,2,1,0:T(8,128)S(1)}, f32[8,128]{1,0:T(8,128)S(1)}) custom-call(f32[16,2,5,5,8,128]{5,4,3,2,1,0:T(8,128)} %bitcast.14.refs_0_, f32[640,640]{1,0:T(8,128)S(1)} %copy-done.13, f32[640,640]{1,0:T(8,128)S(1)} %bitcast.29, f32[2,256,384]{2,1,0:T(8,128)S(1)} %pad_maximum_fusion.1.refs_3_, ...), custom_call_target="tpu_custom_call" | custom-call | flops 9437184000 | bytes 6553600 | tf_op jit(solution)/shard_map/middle/pallas_call | solution.py:378
  151.9 1.7 copy-done.12
  153.6 1.2 copy-done.17
  154.8 86.5 %all-to-all-done = f32[32,5,8,8,128]{4,3,2,1,0:T(8,128)} async-done(((f32[32,5,8,8,128]{4,3,2,1,0:T(8,128)}), f32[32,5,8,8,128]{4,3,2,1,0:T(8,128)}, u32[]{:S(2)}, u32[]{:S(2)}) %all-to-all-start) | async-done | bytes 5242912 | tf_op jit(solution)/shard_map/all_to_all | solution.py:578
  241.3 3.4 all-to-all-start.3
  244.7 0.1 slice.68.refs_6_
  244.8 1.4 copy-done.14
  246.2 1.4 copy-done.16
  247.6 1.4 copy-done.18
  249.0 1.1 copy-done.20
  250.2 1.0 copy-done.22
  251.2 31.9 %middle.3 = (f32[16,2,5,8,8,128]{5,4,3,2,1,0:T(8,128)}, f32[8,128]{1,0:T(8,128)}) custom-call(f32[16,2,5,8,8,128]{5,4,3,2,1,0:T(8,128)} %bitcast.3.refs_0_, f32[640,640]{1,0:T(8,128)S(1)} %copy-done.14, f32[640,640]{1,0:T(8,128)S(1)} %bitcast.30, f32[2,256,384]{2,1,0:T(8,128)S(1)} %copy-done.20, f32[4,256,384]{2,1,0:T(8,128)S(1)} %copy-done.18, ...), custom_call_target="tpu_custom_call" | custom-call | flops 14155776000 | bytes 10485760 | tf_op jit(solution)/shard_map/middle/pallas_call | solution.py:378
  283.0 35.6 %all-to-all-done.3.part_ref = f32[32,5,5,8,128]{4,3,2,1,0:T(8,128)S(1)} async-done(((f32[32,5,5,8,128]{4,3,2,1,0:T(8,128)}), f32[32,5,5,8,128]{4,3,2,1,0:T(8,128)S(1)}, u32[]{:S(2)}, u32[]{:S(2)}) %all-to-all-start.3) | async-done | bytes 3276832 | tf_op jit(solution)/shard_map/all_to_all | solution.py:578
  318.6 3.7 all-to-all-start.2
  322.9 5.6 inverse_base.1.base_ref
  328.6 3.9 copy-done.2
  332.5 107.3 %all-to-all-done.2.part_ref = f32[32,5,8,8,128]{4,3,2,1,0:T(8,128)} async-done(((f32[32,5,8,8,128]{4,3,2,1,0:T(8,128)}), f32[32,5,8,8,128]{4,3,2,1,0:T(8,128)}, u32[]{:S(2)}, u32[]{:S(2)}) %all-to-all-start.2) | async-done | bytes 5242912 | tf_op jit(solution)/shard_map/all_to_all | solution.py:578
  439.8 3.8 copy-done.3
  443.6 1.0 copy-done.10
  444.6 5.4 inverse_ends.1
  450.0 0.1 fusion.1
  450.1 1.9 copy-done.7
  452.0 1.3 collective-permute-start.1
  453.3 3.3 collective-permute-start
  456.6 3.8 copy-done.4
  460.4 2.1 copy-done.8
  462.5 10.2 %inverse_inner.1.refs_0_ = f32[40,160,320]{2,1,0:T(8,128)} custom-call(f32[32,5,8,8,128]{4,3,2,1,0:T(8,128)} %all-to-all-done.2.part_ref, f32[192,320]{1,0:T(8,128)S(1)} %bitcast.25, f32[40,160,320]{2,1,0:T(8,128)S(1)} %copy-done.4, f32[40,160,320]{2,1,0:T(8,128)} %old_ref.3, f32[1,1]{1,0:T(1,128)} %bitcast.22.before_ref, f32[16,160,320]{2,1,0:T(8,128)S(1)} %copy-done.8), custom_call_target="tpu_custom_call" | custom-call | flops 1415577600 | bytes 14745600 | tf_op jit(solution)/shard_map/inverse_inner/pallas_call | solution.py:253
  472.7 1.3 fusion
  474.1 0.1 maximum_select_fusion
  474.1 0.1 collective-permute-start.2
  474.3 15.5 %collective-permute-done.2 = f32[46,8,320]{2,1,0:T(8,128)S(1)} collective-permute-done((f32[46,8,320]{2,1,0:T(8,128)S(1)}, f32[46,8,320]{2,1,0:T(8,128)S(1)}, u32[]{:S(2)}, u32[]{:S(2)}) %collective-permute-start.2) | collective-permute-done | bytes 471072 | tf_op jit(solution)/shard_map/ppermute | solution.py:422
  489.8 0.1 broadcast_select_fusion
  489.8 33.4 %stencil.1 = (f32[40,160,320]{2,1,0:T(8,128)S(1)}, f32[8,128]{1,0:T(8,128)S(1)}) custom-call(f32[40,160,320]{2,1,0:T(8,128)} %inverse_inner.1.refs_0_, f32[3,160,320]{2,1,0:T(8,128)S(1)} %collective-permute-done.refs_1_, f32[3,160,320]{2,1,0:T(8,128)S(1)} %collective-permute-done.1.refs_2_, f32[46,8,320]{2,1,0:T(8,128)S(1)} %get-tuple-element.32.refs_3_, ...), custom_call_target="tpu_custom_call" | custom-call | flops 5242880000 | bytes 16384000 | tf_op jit(solution)/shard_map/stencil/pallas_call | solution.py:545
  523.2 3.9 copy-done.6
  527.1 0.7 broadcast_in_dim.19
  527.8 2.6 all-to-all-start.4
  530.3 0.6 slice.73
  530.9 8.1 %all-to-all-done.4 = f32[32,8,128]{2,1,0:T(8,128)S(1)} async-done(((f32[32,8,128]{2,1,0:T(8,128)}), f32[32,8,128]{2,1,0:T(8,128)S(1)}, u32[]{:S(2)}, u32[]{:S(2)}) %all-to-all-start.4) | async-done | bytes 131104 | tf_op jit(solution)/shard_map/all_to_all | solution.py:578
  539.0 0.6 slice_reduce_fusion
  540.9 21.5 %multiply_subtract_fusion = (f32[40,160,320]{2,1,0:T(8,128)}, f32[40,160,320]{2,1,0:T(8,128)}) fusion(f32[40,160,320]{2,1,0:T(8,128)} %field_ref.3, f32[40,160,320]{2,1,0:T(8,128)} %copy-done.6, f32[]{:T(128)S(6)} %div.3, f32[40,160,320]{2,1,0:T(8,128)} %param.11, f32[40,160,320]{2,1,0:T(8,128)} %inverse_inner.1.refs_0_), kind=kLoop, calls=%fused_computation | loop fusion | flops 8192000 | bytes 49152004 | tf_op jit(solution)/shard_map/sub | solution.py:655
  (50 shorter events, 0.4 us)
Async XLA Ops:
  17.4 3.8 copy-start
  29.7 7.0 %copy-start.24 = (f32[160,320]{1,0:T(8,128)S(1)}, f32[160,320]{1,0:T(8,128)}, u32[]{:S(2)}) copy-start(f32[160,320]{1,0:T(8,128)} %param.16) | copy-start | bytes 614404
  29.7 90.0 %all-to-all-start.1 = ((f32[32,5,5,8,128]{4,3,2,1,0:T(8,128)}), f32[32,5,5,8,128]{4,3,2,1,0:T(8,128)}, u32[]{:S(2)}, u32[]{:S(2)}) async-start(f32[32,5,5,8,128]{4,3,2,1,0:T(8,128)} %forward_z.3), calls=%async_computation.1 | async-start | bytes 6553600 | tf_op jit(solution)/shard_map/all_to_all | solution.py:578
  35.9 57.1 %all-gather.2.cloned.1.call-start = ((), (), s32[]{:S(2)}) async-start(), calls=%async_computation.5 | async-start | bytes 1740800 | tf_op jit(solution)/shard_map/all_gather | solution.py:617
  36.7 23.6 %copy-start.9 = (f32[6,32,320]{2,1,0:T(8,128)}, f32[6,32,320]{2,1,0:T(8,128)S(1)}, u32[]{:S(2)}) copy-start(f32[6,32,320]{2,1,0:T(8,128)S(1)} %copy.39) | copy-start | bytes 737284
  60.3 3.8 copy-start.1
  72.8 2.4 copy-start.5
  75.2 49.4 %copy-start.26 = (f32[320]{0:T(512)S(1)}, f32[320]{0:T(512)}, u32[]{:S(2)}) copy-start(f32[320]{0:T(512)} %param.19) | copy-start | bytes 3844
  75.2 49.6 %copy-start.25 = (f32[640]{0:T(1024)S(1)}, f32[640]{0:T(1024)}, u32[]{:S(2)}) copy-start(f32[640]{0:T(1024)} %param.18) | copy-start | bytes 7684
  93.0 34.1 %copy-start.13 = (f32[640,640]{1,0:T(8,128)S(1)}, f32[640,640]{1,0:T(8,128)}, u32[]{:S(2)}) copy-start(f32[640,640]{1,0:T(8,128)} %all-gather.2.cloned.1.call-done.refs_1_) | copy-start | bytes 4915204
  119.8 121.5 %all-to-all-start = ((f32[32,5,8,8,128]{4,3,2,1,0:T(8,128)}), f32[32,5,8,8,128]{4,3,2,1,0:T(8,128)}, u32[]{:S(2)}, u32[]{:S(2)}) async-start(f32[32,5,8,8,128]{4,3,2,1,0:T(8,128)} %copy-done.5), calls=%async_computation | async-start | bytes 10485760 | tf_op jit(solution)/shard_map/all_to_all | solution.py:578
  128.1 23.8 %copy-start.15 = (f32[640,640]{0,1:T(8,128)}, f32[640,640]{0,1:T(8,128)S(1)}, u32[]{:S(2)}) copy-start(f32[640,640]{0,1:T(8,128)S(1)} %copy.40) | copy-start | bytes 4915204
  128.2 3.6 copy-start.21
  130.1 1.6 copy-start.19
  151.9 1.7 copy-start.12
  153.6 1.2 copy-start.17
  241.3 77.3 %all-to-all-start.3 = ((f32[32,5,5,8,128]{4,3,2,1,0:T(8,128)}), f32[32,5,5,8,128]{4,3,2,1,0:T(8,128)S(1)}, u32[]{:S(2)}, u32[]{:S(2)}) async-start(f32[32,5,5,8,128]{4,3,2,1,0:T(8,128)} %bitcast.26), calls=%async_computation.3 | async-start | bytes 6553600 | tf_op jit(solution)/shard_map/all_to_all | solution.py:578
  244.8 1.4 copy-start.14
  246.2 1.4 copy-start.16
  247.6 1.4 copy-start.18
  249.0 1.1 copy-start.20
  250.2 1.0 copy-start.22
  318.6 121.2 %all-to-all-start.2 = ((f32[32,5,8,8,128]{4,3,2,1,0:T(8,128)}), f32[32,5,8,8,128]{4,3,2,1,0:T(8,128)}, u32[]{:S(2)}, u32[]{:S(2)}) async-start(f32[32,5,8,8,128]{4,3,2,1,0:T(8,128)} %bitcast.31), calls=%async_computation.2 | async-start | bytes 10485760 | tf_op jit(solution)/shard_map/all_to_all | solution.py:578
  328.6 3.9 copy-start.2
  439.8 3.8 copy-start.3
  443.6 1.0 copy-start.10
  444.6 12.0 %copy-start.11 = (f32[6,32,320]{2,1,0:T(8,128)S(1)}, f32[6,32,320]{2,1,0:T(8,128)}, u32[]{:S(2)}) copy-start(f32[6,32,320]{2,1,0:T(8,128)} %copy-done.9) | copy-start | bytes 737284
  450.1 1.9 copy-start.7
  452.0 22.0 %collective-permute-start.1 = (f32[3,160,320]{2,1,0:T(8,128)S(1)}, f32[3,160,320]{2,1,0:T(8,128)S(1)}, u32[]{:S(2)}, u32[]{:S(2)}) collective-permute-start(f32[3,160,320]{2,1,0:T(8,128)S(1)} %get-tuple-element.25), channel_id=1, source_target_pairs={{2,0},{4,2},{6,4},{8,6},{10,8},{12,10},{14,12},{16,14},{18,16},{20... | collective-permute-start | bytes 1843208 | tf_op jit(solution)/shard_map/ppermute | solution.py:415
  453.3 20.8 %collective-permute-start = (f32[3,160,320]{2,1,0:T(8,128)S(1)}, f32[3,160,320]{2,1,0:T(8,128)S(1)}, u32[]{:S(2)}, u32[]{:S(2)}) collective-permute-start(f32[3,160,320]{2,1,0:T(8,128)S(1)} %get-tuple-element.26), channel_id=1, source_target_pairs={{0,2},{2,4},{4,6},{6,8},{8,10},{10,12},{12,14},{14,16},{16,18},{18... | collective-permute-start | bytes 1843208 | tf_op jit(solution)/shard_map/ppermute | solution.py:415
  456.6 3.8 copy-start.4
  460.4 2.1 copy-start.8
  472.7 17.1 %copy-start.23 = (bf16[3,2,256,256]{3,2,1,0:T(8,128)(2,1)S(1)}, bf16[3,2,256,256]{3,2,1,0:T(8,128)(2,1)}, u32[]{:S(2)}) copy-start(bf16[3,2,256,256]{3,2,1,0:T(8,128)(2,1)} %constant.24.clone.refs_5_) | copy-start | bytes 2359300
  474.1 15.6 %collective-permute-start.2 = (f32[46,8,320]{2,1,0:T(8,128)S(1)}, f32[46,8,320]{2,1,0:T(8,128)S(1)}, u32[]{:S(2)}, u32[]{:S(2)}) collective-permute-start(f32[46,8,320]{2,1,0:T(8,128)S(1)} %maximum_select_fusion), channel_id=1, source_target_pairs={{0,1},{1,0},{2,3},{3,2},{4,5},{5,4},{6,7},{7,6},{8,9},{9,8},{10,11... | collective-permute-start | bytes 1413128 | tf_op jit(solution)/shard_map/ppermute | solution.py:422
  523.2 3.9 copy-start.6
  527.8 11.2 %all-to-all-start.4 = ((f32[32,8,128]{2,1,0:T(8,128)}), f32[32,8,128]{2,1,0:T(8,128)S(1)}, u32[]{:S(2)}, u32[]{:S(2)}) async-start(f32[32,8,128]{2,1,0:T(8,128)} %broadcast_in_dim.19), calls=%async_computation.4 | async-start | bytes 262144 | tf_op jit(solution)/shard_map/all_to_all | solution.py:578
Sparse Core Ops, SparseCore 0:
  38.9 54.0 all-gather.1

commit v3 on v2

--- a/solution.py
+++ b/solution.py
@@ -72,59 +72,84 @@
             and self.tiles >= 3
             and 2 * LANES < cells_z <= 3 * LANES
         )
+        if self.fits:
+            _, _, _, _, fit, width = self.shape_of(1)
+            self.fits = self.tiles % fit != 0 or fit * width < LANES
 
     def rows(self, chunk):
         start, size = self.chunks[chunk]
         return start * self.count, size * self.count
 
+    def shape_of(self, chunk):
+        size = self.chunks[chunk][1]
+        part = size % self.group
+        width = part * self.rest
+        fit = LANES // width if part else 1
+        tails = -(-self.tiles // fit) if part else 0
+        return size, size + size // self.group, part, tails, fit, width
+
     def message(self, chunk):
-        return (self.count, self.tiles, self.pieces(chunk), 8, LANES)
-
-    def pieces(self, chunk):
-        size = self.chunks[chunk][1]
-        return size - (-size // self.group)
-
-
-def forward_kernel(plan, size, field_ref, basis_ref, out_ref, high_ref, low_ref, stage_ref):
-
-    @pl.when(pl.program_id(0) == 0)
+        _, per, _, tails, _, _ = self.shape_of(chunk)
+        return (self.count, self.tiles * per + tails, 8, LANES)
+
+
+def forward_kernel(plan, chunk, field_ref, basis_ref, out_ref, high_ref, low_ref, stage_ref):
+    size, per, part, tails, fit, width = plan.shape_of(chunk)
+    step = pl.program_id(0)
+
+    @pl.when(step == 0)
     def _():
         high_ref[...], low_ref[...] = split(basis_ref[...])
+        if tails:
+            out_ref[:, plan.tiles * per :] = jnp.zeros((plan.count, tails, 8, LANES), jnp.float32)
 
     basis = (high_ref[...], low_ref[...])
     for i in range(8):
         stage_ref[i] = dot3(basis, split(field_ref[i]), (1, 1))
+    base = step * per if tails else 0
     rests = []
     for j in range(size):
         at = j * plan.count
         turned = jnp.swapaxes(stage_ref[:, at : at + plan.count, :], 0, 1)
-        out_ref[:, 0, j] = turned[:, :, :LANES]
+        out_ref[:, base + j] = turned[:, :, :LANES]
         rests.append(turned[:, :, LANES:])
-    for piece, first in enumerate(range(0, size, plan.group)):
-        some = rests[first : first + plan.group]
-        some += [jnp.zeros_like(some[0])] * (plan.group - len(some))
-        out_ref[:, 0, size + piece] = jnp.concatenate(some, axis=2)
+    for piece in range(size // plan.group):
+        some = rests[piece * plan.group : (piece + 1) * plan.group]
+        out_ref[:, base + size + piece] = jnp.concatenate(some, axis=2)
+    if tails:
+        some = jnp.concatenate(rests[size - part :], axis=2)
+        for place in range(fit):
+
+            @pl.when(step % fit == place)
+            def _():
+                lanes = slice(place * width, (place + 1) * width)
+                out_ref[:, plan.tiles * per + step // fit, :, lanes] = some
 
 
 def forward_z(plan, chunk, field, basis):
     start, rows = plan.rows(chunk)
     basis = basis[start : start + rows]
     message = plan.message(chunk)
+    _, per, _, tails, _, _ = plan.shape_of(chunk)
+    if tails:
+        out_spec = pl.BlockSpec(message, lambda t: (0, 0, 0, 0))
+    else:
+        out_spec = pl.BlockSpec((message[0], per) + message[2:], lambda t: (0, t, 0, 0))
     return pl.pallas_call(
-        functools.partial(forward_kernel, plan, plan.chunks[chunk][1]),
+        functools.partial(forward_kernel, plan, chunk),
         grid=(plan.tiles,),
         in_specs=[
             pl.BlockSpec((8, plan.cells_y, plan.cells_z), lambda t: (t, 0, 0)),
             pl.BlockSpec(basis.shape, lambda t: (0, 0)),
         ],
-        out_specs=pl.BlockSpec((message[0], 1) + message[2:], lambda t: (0, t, 0, 0, 0)),
+        out_specs=out_spec,
         out_shape=jax.ShapeDtypeStruct(message, jnp.float32),
         scratch_shapes=[
             pltpu.VMEM(basis.shape, jnp.bfloat16),
             pltpu.VMEM(basis.shape, jnp.bfloat16),
             pltpu.VMEM((8, rows, plan.cells_y), jnp.float32),
         ],
-        compiler_params=pltpu.CompilerParams(vmem_limit_bytes=24 * MIB),
+        compiler_params=pltpu.CompilerParams(vmem_limit_bytes=50 * MIB),
         cost_estimate=pl.CostEstimate(
             flops=6 * field.size * rows, bytes_accessed=8 * field.size, transcendentals=0
         ),
@@ -132,31 +157,43 @@
     )(field, basis)
 
 
-def add_chunk(plan, size, part, stage_ref):
+def add_chunk(plan, chunk, tile, part_ref, tail_ref, stage_ref):
+    size, _, part, tails, fit, width = plan.shape_of(chunk)
+    if tails:
+        tail = tail_ref[:, 0]
+        for place in range(1, fit):
+            turned = pltpu.roll(tail_ref[:, 0], LANES - place * width, 2)
+            tail = jnp.where(tile % fit == place, turned, tail)
     for j in range(size):
         at, q = j * plan.count, j % plan.group
-        stage_ref[:, at : at + plan.count, :LANES] = jnp.swapaxes(part[:, 0, j], 0, 1)
-        stage_ref[:, at : at + plan.count, LANES:] = jnp.swapaxes(
-            part[:, 0, size + j // plan.group, :, q * plan.rest : (q + 1) * plan.rest], 0, 1
-        )
-
-
-def base_kernel(plan, size, part_ref, basis_ref, out_ref, high_ref, low_ref, stage_ref):
-    @pl.when(pl.program_id(0) == 0)
+        lanes = slice(q * plan.rest, (q + 1) * plan.rest)
+        stage_ref[:, at : at + plan.count, :LANES] = jnp.swapaxes(part_ref[:, j], 0, 1)
+        if j < size - part:
+            rest = part_ref[:, size + j // plan.group, :, lanes]
+        else:
+            rest = tail[:, :, lanes]
+        stage_ref[:, at : at + plan.count, LANES:] = jnp.swapaxes(rest, 0, 1)
+
+
+def base_kernel(plan, chunk, part_ref, basis_ref, out_ref, high_ref, low_ref, stage_ref):
+    step = pl.program_id(0)
+
+    @pl.when(step == 0)
     def _():
         high_ref[...], low_ref[...] = split(basis_ref[...])
 
-    add_chunk(plan, size, part_ref, stage_ref)
+    add_chunk(plan, chunk, step, part_ref, None, stage_ref)
     basis = (high_ref[...], low_ref[...])
     for i in range(8):
         out_ref[i] = dot3(split(stage_ref[i].T), basis, (1, 0))
 
 
-def final_kernel(plan, size, ends, part_ref, basis_ref, base_ref, old_ref, before_ref, *refs):
+def final_kernel(plan, chunk, ends, pick, *refs):
+    part_ref, tail_ref, last_ref, basis_ref, base_ref, old_ref, before_ref = refs[:7]
     if ends:
-        out_ref, now_ref, high_ref, low_ref, stage_ref = refs
+        out_ref, now_ref, high_ref, low_ref, stage_ref = refs[7:]
     else:
-        done_ref, out_ref, high_ref, low_ref, stage_ref = refs
+        done_ref, out_ref, high_ref, low_ref, stage_ref = refs[7:]
     step = pl.program_id(0)
 
     @pl.when(step == 0)
@@ -164,9 +201,8 @@
         high_ref[...], low_ref[...] = split(basis_ref[...])
 
     def work():
-        add_chunk(plan, size, part_ref, stage_ref)
-        sums = part_ref[:, 0, part_ref.shape[2] - 1, 0, LANES - 1 :]
-        now = jnp.sum(sums, axis=0, keepdims=True)
+        add_chunk(plan, chunk, pick(step), part_ref, tail_ref, stage_ref)
+        now = jnp.sum(last_ref[:, 0, 0, LANES - 1 :], axis=0, keepdims=True)
         beta = now / before_ref[...]
         basis = (high_ref[...], low_ref[...])
         for i in range(8):
@@ -203,18 +239,19 @@
 
 def inverse_base(plan, chunk, part, basis):
     start, rows = plan.rows(chunk)
+    per = plan.shape_of(chunk)[1]
     basis = basis[start : start + rows]
     return pl.pallas_call(
-        functools.partial(base_kernel, plan, plan.chunks[chunk][1]),
+        functools.partial(base_kernel, plan, chunk),
         grid=(plan.tiles,),
         in_specs=[
-            pl.BlockSpec((part.shape[0], 1) + part.shape[2:], lambda t: (0, t, 0, 0, 0)),
+            pl.BlockSpec((plan.count, per, 8, LANES), lambda t: (0, t, 0, 0)),
             pl.BlockSpec(basis.shape, lambda t: (0, 0)),
         ],
         out_specs=pl.BlockSpec((8, plan.cells_y, plan.cells_z), lambda t: (t, 0, 0)),
         out_shape=jax.ShapeDtypeStruct((plan.cells_x, plan.cells_y, plan.cells_z), jnp.float32),
         scratch_shapes=inverse_scratch(plan, basis),
-        compiler_params=pltpu.CompilerParams(vmem_limit_bytes=24 * MIB),
+        compiler_params=pltpu.CompilerParams(vmem_limit_bytes=50 * MIB),
         cost_estimate=inverse_cost(plan, basis, plan.tiles),
         name="inverse_base",
     )(part, basis)
@@ -231,14 +268,19 @@
         pick = lambda t: jnp.clip(t, 1, last - 1)
     tile = (8, plan.cells_y, plan.cells_z)
     brick = pl.BlockSpec(tile, lambda t: (pick(t), 0, 0))
+    _, per, _, _, fit, _ = plan.shape_of(chunk)
     in_specs = [
-        pl.BlockSpec((part.shape[0], 1) + part.shape[2:], lambda t: (0, pick(t), 0, 0, 0)),
+        pl.BlockSpec((plan.count, per, 8, LANES), lambda t: (0, pick(t), 0, 0)),
+        pl.BlockSpec(
+            (plan.count, 1, 8, LANES), lambda t: (0, plan.tiles * per + pick(t) // fit, 0, 0)
+        ),
+        pl.BlockSpec((plan.count, 1, 8, LANES), lambda t: (0, part.shape[1] - 1, 0, 0)),
         pl.BlockSpec(basis.shape, lambda t: (0, 0)),
         brick,
         brick,
         pl.BlockSpec((1, 1), lambda t: (0, 0)),
     ]
-    operands = [part, basis, base, old, before.reshape(1, 1)]
+    operands = [part, part, part, basis, base, old, before.reshape(1, 1)]
     out_specs = pl.BlockSpec(tile, lambda t: (t, 0, 0))
     if ends:
         out_specs = [out_specs, pl.BlockSpec((8, LANES), lambda t: (0, 0))]
@@ -251,13 +293,13 @@
         operands.append(done)
         out_shape = jax.ShapeDtypeStruct(base.shape, jnp.float32)
     return pl.pallas_call(
-        functools.partial(final_kernel, plan, plan.chunks[chunk][1], ends),
+        functools.partial(final_kernel, plan, chunk, ends, pick),
         grid=(2 if ends else plan.tiles,),
         in_specs=in_specs,
         out_specs=out_specs,
         out_shape=out_shape,
         scratch_shapes=inverse_scratch(plan, basis),
-        compiler_params=pltpu.CompilerParams(vmem_limit_bytes=28 * MIB),
+        compiler_params=pltpu.CompilerParams(vmem_limit_bytes=50 * MIB),
         cost_estimate=inverse_cost(plan, basis, 2 if ends else plan.tiles - 2),
         name="inverse_ends" if ends else "inverse_inner",
     )(*operands)
@@ -289,7 +331,8 @@
         q_low,
         rest_acc,
     ) = refs
-    size = plan.chunks[chunk][1]
+    size, per, part, tails, fit, lanes = plan.shape_of(chunk)
+    full = size // plan.group
     last = chunk == len(plan.chunks) - 1
     wide, narrow, tiles = plan.wide, plan.narrow, plan.tiles
     half = plan.total_x // 2
@@ -302,21 +345,31 @@
     ry_high[...], ry_low[...] = split(rest_y_ref[...])
     rest_acc[...] = jnp.zeros_like(rest_acc)
 
-    def gathered(piece, h):
+    def gathered(h, places):
         rows = pl.ds(h * lump, lump)
-        return jnp.concatenate(
-            [in_ref[rows, n, :, piece].reshape(half, LANES) for n in range(narrow)], axis=1
-        )
-
-    def pair(p, total):
+        sides = []
+        for n in range(narrow):
+            some = []
+            for t in range(tiles):
+                piece, turn = places(t)
+                value = in_ref[rows, n, piece]
+                some.append(pltpu.roll(value, LANES - turn, 2) if turn else value)
+            sides.append(jnp.stack(some, axis=1).reshape(half, LANES))
+        return jnp.concatenate(sides, axis=1)
+
+    def pair(in_tail, p, total):
         for h in range(2):
-            rest = split(gathered(size + 2 * p // plan.group, h))
+            if in_tail:
+                rest = gathered(h, lambda t: (tiles * per + t // fit, t % fit * lanes))
+            else:
+                rest = gathered(h, lambda t: (t * per + size + 2 * p // plan.group, 0))
+            rest = split(rest)
             parts = []
             for s in range(2):
                 j = 2 * p + s
                 q = lax.rem(j, plan.group)
                 parts.append(
-                    dot3(split(gathered(j, h)), (my_high[s], my_low[s]), (1, 0))
+                    dot3(split(gathered(h, lambda t: (t * per + j, 0))), (my_high[s], my_low[s]), (1, 0))
                     + dot3(rest, (ry_high[q], ry_low[q]), (1, 0))
                 )
             cut = span - LANES
@@ -351,26 +404,37 @@
                     mine, (ry_high[q], ry_low[q]), (1, 1)
                 )
                 for n in range(narrow):
-                    out_ref[pl.ds(h * lump, lump), n, :, j] = main[
-                        :, n * LANES : (n + 1) * LANES
-                    ].reshape(lump, tiles, 8, LANES)
+                    side = main[:, n * LANES : (n + 1) * LANES].reshape(lump, tiles, 8, LANES)
+                    for t in range(tiles):
+                        out_ref[pl.ds(h * lump, lump), n, t * per + j] = side[:, t]
         return total
 
-    total = lax.fori_loop(0, size // 2, pair, jnp.zeros((8, width), jnp.float32))
+    total = jnp.zeros((8, width), jnp.float32)
+    total = lax.fori_loop(0, (size - part) // 2, functools.partial(pair, False), total)
+    if tails:
+        total = lax.fori_loop((size - part) // 2, size // 2, functools.partial(pair, True), total)
     value = total_ref[...] + jnp.sum(total)
     sum_ref[...] = value
-    pieces = in_ref.shape[3] - size
-    for piece in range(pieces):
-        for n in range(narrow):
-            rest = rest_acc[piece, :, n * LANES : (n + 1) * LANES]
-            if last and piece == pieces - 1:
-                lane = lax.broadcasted_iota(jnp.int32, rest.shape, 1)
-                rest = jnp.where(lane == LANES - 1, value[:1, :], rest)
-            out_ref[:, n, :, size + piece] = rest.reshape(wide, tiles, 8, LANES)
+    for n in range(narrow):
+        side = slice(n * LANES, (n + 1) * LANES)
+        for piece in range(full):
+            rest = rest_acc[piece, :, side].reshape(wide, tiles, 8, LANES)
+            for t in range(tiles):
+                out_ref[:, n, t * per + size + piece] = rest[:, t]
+        for tail in range(tails):
+            rest = rest_acc[full, :, side].reshape(wide, tiles, 8, LANES)
+            joined = rest[:, tail * fit]
+            for t in range(tail * fit + 1, min(tail * fit + fit, tiles)):
+                joined = joined + pltpu.roll(rest[:, t], t % fit * lanes, 2)
+            if last and tail == tails - 1:
+                lane = lax.broadcasted_iota(jnp.int32, joined.shape, 2)
+                joined = jnp.where(lane == LANES - 1, value[:1, :][None], joined)
+            out_ref[:, n, tiles * per + tail] = joined
 
 
 def middle(plan, chunk, message, basis_x, turned_x, main_y, rest_y, eigen_x, shift, total):
     size = plan.chunks[chunk][1]
+    pieces = -(-size // plan.group)
     shape = (plan.wide, plan.narrow) + message.shape[1:]
     square = (plan.total_x, plan.total_x)
     pencil = (plan.total_x, 2 * plan.total_y)
@@ -396,7 +460,7 @@
             pltpu.VMEM(pencil, half),
             pltpu.VMEM(pencil, half),
             pltpu.VMEM(pencil, half),
-            pltpu.VMEM((plan.pieces(chunk) - size, plan.total_x, plan.narrow * LANES), jnp.float32),
+            pltpu.VMEM((pieces, plan.total_x, plan.narrow * LANES), jnp.float32),
         ],
         compiler_params=pltpu.CompilerParams(vmem_limit_bytes=44 * MIB),
         cost_estimate=pl.CostEstimate(
@@ -447,31 +511,45 @@
 
 
 def stencil_kernel(plan, *refs):
-    pieces = refs[:5]
-    bands_ref, image_ref, sum_ref, field, f_high, f_low, s_high, s_low, h_a, h_b, total, sems = refs[5:]
+    own, before_x, after_x, before_y, after_y, bands_ref, image_ref, sum_ref = refs[:8]
+    field, f_high, f_low, s_high, s_low, h_a, h_b, total, sems = refs[8:]
     cells_x, cells_y, cells_z = plan.cells_x, plan.cells_y, plan.cells_z
+    tiles = plan.tiles
     padded_y = cells_y + 2 * EDGE
     own_y = pl.ds(EDGE, cells_y)
-    places = (
-        (pl.ds(HALO, cells_x), own_y),
-        (pl.ds(0, HALO), own_y),
-        (pl.ds(HALO + cells_x, HALO), own_y),
-        (pl.ds(0, cells_x + 2 * HALO), pl.ds(0, EDGE)),
-        (pl.ds(0, cells_x + 2 * HALO), pl.ds(EDGE + cells_y, EDGE)),
-    )
     step = pl.program_id(0)
+
+    def tile_copy(t):
+        return pltpu.make_async_copy(
+            own.at[pl.ds(8 * t, 8)], field.at[pl.ds(HALO + 8 * t, 8), own_y, :], sems.at[t]
+        )
+
+    first_copy = pltpu.make_async_copy(
+        before_x, field.at[pl.ds(0, HALO), own_y, :], sems.at[tiles]
+    )
+    last_copy = pltpu.make_async_copy(
+        after_x, field.at[pl.ds(HALO + cells_x, HALO), own_y, :], sems.at[tiles + 1]
+    )
 
     @pl.when(step == 0)
     def _():
-        copies = [
-            pltpu.make_async_copy(piece, field.at[xs, ys, :], sems.at[i])
-            for i, (piece, (xs, ys)) in enumerate(zip(pieces, places))
-        ]
-        for copy in copies:
-            copy.start()
+        first_copy.start()
+        for t in range(tiles):
+            tile_copy(t).start()
+        last_copy.start()
         total[...] = jnp.zeros_like(total)
-        for copy in copies:
-            copy.wait()
+        field[:, EDGE - HALO : EDGE, :] = jnp.swapaxes(before_y[...], 0, 1)
+        field[:, EDGE + cells_y : EDGE + cells_y + HALO, :] = jnp.swapaxes(after_y[...], 0, 1)
+        first_copy.wait()
+        tile_copy(0).wait()
+
+    @pl.when(step < tiles - 1)
+    def _():
+        tile_copy(step + 1).wait()
+
+    @pl.when(step == tiles - 1)
+    def _():
+        last_copy.wait()
 
     blocks = h_a.shape[0]
     ratio = stiff_scale / mass_scale
@@ -533,10 +611,11 @@
     cells_x, cells_y, cells_z = direction.shape
 
     def strip(rows):
-        return jnp.concatenate([before_x[:, rows], direction[:, rows], after_x[:, rows]], axis=0)
+        parts = [jnp.swapaxes(v[:, rows], 0, 1) for v in (before_x, direction, after_x)]
+        return jnp.concatenate(parts, axis=1)
 
     before_y, after_y = from_sides(
-        strip(slice(0, EDGE)), strip(slice(cells_y - EDGE, cells_y)), "narrow"
+        strip(slice(0, HALO)), strip(slice(cells_y - HALO, cells_y)), "narrow"
     )
     bands = band_matrices(cells_z)
     padded_y = cells_y + 2 * EDGE
@@ -545,15 +624,16 @@
     return pl.pallas_call(
         functools.partial(stencil_kernel, plan),
         grid=(cells_x // 8,),
-        in_specs=[pl.BlockSpec(memory_space=pl.ANY)] * 5
+        in_specs=[pl.BlockSpec(memory_space=pl.ANY)] * 3
+        + [pl.BlockSpec(before_y.shape, lambda t: (0, 0, 0))] * 2
         + [pl.BlockSpec(bands.shape, lambda t: (0, 0, 0, 0))],
         out_specs=[
             pl.BlockSpec((8, cells_y, cells_z), lambda t: (t, 0, 0)),
-            pl.BlockSpec((8, LANES), lambda t: (0, 0)),
+            pl.BlockSpec((plan.count, 8, LANES), lambda t: (0, 0, 0)),
         ],
         out_shape=[
             jax.ShapeDtypeStruct(direction.shape, jnp.float32),
-            jax.ShapeDtypeStruct((8, LANES), jnp.float32),
+            jax.ShapeDtypeStruct((plan.count, 8, LANES), jnp.float32),
         ],
         scratch_shapes=[
             pltpu.VMEM((cells_x + 2 * HALO, padded_y, cells_z), jnp.float32),
@@ -564,14 +644,38 @@
             pltpu.VMEM((blocks, GROUP * padded_y, LANES), jnp.float32),
             pltpu.VMEM((blocks, GROUP * padded_y, LANES), jnp.float32),
             pltpu.VMEM((8, cells_z), jnp.float32),
-            pltpu.SemaphoreType.DMA((5,)),
+            pltpu.SemaphoreType.DMA((plan.tiles + 2,)),
         ],
-        compiler_params=pltpu.CompilerParams(vmem_limit_bytes=36 * MIB),
+        compiler_params=pltpu.CompilerParams(vmem_limit_bytes=50 * MIB),
         cost_estimate=pl.CostEstimate(
             flops=8 * direction.size * cells_z, bytes_accessed=8 * direction.size, transcendentals=0
         ),
         name="stencil",
     )(direction, before_x, after_x, before_y, after_y, bands)
+
+
+def update_kernel(now_ref, parts_ref, solution_ref, residual_ref, direction_ref, image_ref, *outs):
+    curvature = jnp.sum(parts_ref[:, 0, :1], axis=0, keepdims=True)
+    alpha = (now_ref[:1, :1] / curvature)[None]
+    outs[0][...] = solution_ref[...] + alpha * direction_ref[...]
+    outs[1][...] = residual_ref[...] - alpha * image_ref[...]
+
+
+def update(now, parts, solution, residual, direction, image):
+    brick = pl.BlockSpec((4,) + image.shape[1:], lambda t: (t, 0, 0))
+    return pl.pallas_call(
+        update_kernel,
+        grid=(image.shape[0] // 4,),
+        in_specs=[
+            pl.BlockSpec(now.shape, lambda t: (0, 0)),
+            pl.BlockSpec(parts.shape, lambda t: (0, 0, 0)),
+        ]
+        + [brick] * 4,
+        out_specs=[brick] * 2,
+        out_shape=[jax.ShapeDtypeStruct(image.shape, jnp.float32)] * 2,
+        compiler_params=pltpu.CompilerParams(vmem_limit_bytes=50 * MIB),
+        name="update",
+    )(now, parts, solution, residual, direction, image)
 
 
 def scatter(x):
@@ -650,9 +754,8 @@
     after_x = shifted(ends[:HALO], 1, "wide")
     direction = inverse(ends)
     image, part = stencil(plan, direction, before_x, after_x)
-    parts = scatter(jnp.broadcast_to(part[None], (plan.count,) + part.shape))
-    alpha = now[0, 0] / jnp.sum(parts[:, 0, 0])
-    return solution + alpha * direction, residual - alpha * image, direction
+    solution, residual = update(now, scatter(part), solution, residual, direction, image)
+    return solution, residual, direction
 
 
 def padded_2(x, sides, width):

time: 570 us -> 541 us (0.949)
  Pallas kernels: 124 us -> 156 us
  local copies, waits for them, and re-layouts: 50.3 us -> 21.1 us
  other arithmetic: 22.5 us -> 0.33 us
  waiting for transfers between devices: 298 us -> 276 us
  blocking collectives: 33.4 us -> 45.3 us
    pallas_call x5 -> x6, Pallas kernels: 38.4 us -> 70.7 us  [the longest x2 22.9 us: forward_z(): pl.pallas_call(functools.partial(forward_kernel, plan, chunk), grid=(plan...]
    unnamed x54 -> x34, local copies, waits for them, and re-layouts: 39.5 us -> 10.3 us
    sub x1 -> x0, other arithmetic: 21.5 us -> none  [by_pencils(): return (solution + alpha * direction, residual - alpha * image, direction)]
    all_to_all x5 -> x4, waiting for transfers between devices: 264 us -> 247 us  [scatter(): return lax.all_to_all(x, both, split_axis=0, concat_axis=0, tiled=True)]
    all_to_all x0 -> x1, blocking collectives: none -> 11.9 us  [scatter(): return lax.all_to_all(x, both, split_axis=0, concat_axis=0, tiled=True)]
    ppermute x1, waiting for transfers between devices: 15.5 us -> 7.83 us  [from_sides(): got = lax.ppermute(jnp.where(second, low, high), axis, [(0, 1), (1, 0)])]
    all_to_all x5 -> x4, starting transfers between devices: 19.9 us -> 17.8 us  [scatter(): return lax.all_to_all(x, both, split_axis=0, concat_axis=0, tiled=True)]
  transfers between devices with their start and end apart: 9 -> 8, of which waited for: 7 -> 6; matrix products, arithmetic and copies ran while one was open for 2% -> 2% of each run, Pallas kernels for 13% -> 16%
where the time goes in v3:
time: 541 us; the launch traced here: 537 us
  waiting for transfers between devices  276 us (51%)
  Pallas kernels  156 us (29%)
  blocking collectives  45.3 us (8%)
  starting transfers between devices  22.5 us (4%)
  local copies, waits for them, and re-layouts  21.1 us (4%)
  between operations  15.3 us (3%)
    all_to_all x4, waiting for transfers between devices, scatter(): return lax.all_to_all(x, both, split_axis=0, concat_axis=0, tiled=True)  247 us
    pallas_call x2, Pallas kernels, middle(): pl.pallas_call(functools.partial(middle_kernel, plan, chunk), out_shape=[...  51.9 us
    pallas_call x1, Pallas kernels, stencil(): pl.pallas_call(functools.partial(stencil_kernel, plan), grid=(cells_x //...  33.7 us
    all_gather x1, blocking collectives, by_pencils(): whole_y = lax.all_gather(basis_y, 'narrow', axis=0, tiled=True)  23.6 us
    pallas_call x2, Pallas kernels, forward_z(): pl.pallas_call(functools.partial(forward_kernel, plan, chunk), grid=(plan...  22.9 us
    pallas_call x1, Pallas kernels, update(): pl.pallas_call(update_kernel, grid=(image.shape[0] // 4,), in_specs=[pl.B...  20.5 us
    all_gather x1, waiting for transfers between devices, by_pencils(): whole_x = lax.all_gather(basis_x, 'wide', axis=0, tiled=True)  20.3 us
    pallas_call x2, Pallas kernels, inverse_final(): pl.pallas_call(functools.partial(final_kernel, plan, chunk, ends, pick),...  20 us
  transfers between devices with their start and end apart: 8, of which 6 were waited for; matrix products, arithmetic and copies ran while one was open for 2% of the time, Pallas kernels for 16%

profile of v3, /device:TPU:0, one launch (start us, length us, event | category | flops | bytes accessed | tf_op | source)
XLA Modules:
  0.0 537.0 jit_solution(126732343868351856)
XLA Ops:
  7.2 9.9 %all_gather.9 = f32[320,320]{1,0:T(8,128)S(1)} all-gather(f32[160,320]{1,0:T(8,128)} %param.17), channel_id=1, replica_groups=mesh['wide'=16,'narrow'=2] {'narrow'}, dimensions={0}, use_global_device_ids=true | all-gather | bytes 614400 | tf_op jit(solution)/shard_map/all_gather | solution.py:718
  17.0 0.2 copy.38
  17.2 0.1 reshape.43
  17.4 10.6 %forward_z.3 = f32[32,25,8,128]{3,2,1,0:T(8,128)} custom-call(f32[40,160,320]{2,1,0:T(8,128)} %residual_ref.1, f32[128,320]{1,0:T(8,128)S(1)} %bitcast.38), custom_call_target="tpu_custom_call" | custom-call | flops 1572864000 | bytes 16384000 | tf_op jit(solution)/shard_map/forward_z/pallas_call | solution.py:138
  28.0 6.1 %all-to-all-start.1 = ((f32[32,25,8,128]{3,2,1,0:T(8,128)}), f32[32,25,8,128]{3,2,1,0:T(8,128)}, u32[]{:S(2)}, u32[]{:S(2)}) async-start(f32[32,25,8,128]{3,2,1,0:T(8,128)} %forward_z.3), calls=%async_computation.1 | async-start | bytes 6553600 | tf_op jit(solution)/shard_map/all_to_all | solution.py:682
  34.1 0.0 all-gather.2.cloned.1.call-start
  34.2 0.7 all-gather.2.cloned.1.call-update
  34.9 0.1 copy.39
  35.0 0.0 copy-done.14
  35.0 0.0 copy-start
  35.0 23.6 %all_gather.11 = f32[320,320]{1,0:T(8,128)S(1)} all-gather(f32[160,320]{1,0:T(8,128)S(1)} %copy-done.14), channel_id=1, replica_groups=mesh['wide'=16,'narrow'=2] {'narrow'}, dimensions={0}, use_global_device_ids=true | all-gather | bytes 614400 | tf_op jit(solution)/shard_map/all_gather | solution.py:720
  58.6 0.0 copy-done
  58.6 12.3 %forward_z.2 = f32[32,38,8,128]{3,2,1,0:T(8,128)} custom-call(f32[40,160,320]{2,1,0:T(8,128)} %residual_ref.1, f32[192,320]{1,0:T(8,128)S(1)} %bitcast.34), custom_call_target="tpu_custom_call" | custom-call | flops 2359296000 | bytes 16384000 | tf_op jit(solution)/shard_map/forward_z/pallas_call | solution.py:138
  70.9 20.3 %all-gather.2.cloned.1.call-done.refs_1_ = f32[640,640]{1,0:T(8,128)} async-done(((f32[40,640]{1,0:T(8,128)}), f32[640,640]{1,0:T(8,128)}) %all-gather.2.cloned.1.call-update) | async-done | bytes 1638416 | tf_op jit(solution)/shard_map/all_gather | solution.py:721
  91.3 26.8 %all-to-all-done.1 = f32[32,25,8,128]{3,2,1,0:T(8,128)} async-done(((f32[32,25,8,128]{3,2,1,0:T(8,128)}), f32[32,25,8,128]{3,2,1,0:T(8,128)}, u32[]{:S(2)}, u32[]{:S(2)}) %all-to-all-start.1) | async-done | bytes 3276832 | tf_op jit(solution)/shard_map/all_to_all | solution.py:682
  118.0 4.4 all-to-all-start
  122.5 0.8 dynamic_slice.3
  123.2 0.0 copy-done.16
  123.2 0.1 broadcast_add_fusion
  123.3 0.1 slice.66.refs_6_
  123.4 0.9 reshape.52.refs_5_
  124.3 0.6 slice.77
  124.9 0.8 slice.76
  125.7 1.0 copy.40
  126.7 0.0 copy-start.5
  126.7 0.0 copy-start.11
  126.8 1.9 pad_bitcast_fusion.1
  128.6 0.1 pad_maximum_fusion.1.refs_3_
  128.7 0.0 copy-start.9
  128.7 1.5 fusion.4
  130.2 0.1 pad_maximum_fusion.refs_4_
  130.3 20.1 %middle.2 = (f32[16,2,25,8,128]{4,3,2,1,0:T(8,128)S(1)}, f32[8,128]{1,0:T(8,128)S(1)}) custom-call(f32[16,2,25,8,128]{4,3,2,1,0:T(8,128)} %bitcast.14.refs_0_, f32[640,640]{1,0:T(8,128)S(1)} %copy-done.3, f32[640,640]{1,0:T(8,128)S(1)} %bitcast.40, f32[2,256,384]{2,1,0:T(8,128)S(1)} %pad_maximum_fusion.1.refs_3_, ...), custom_call_target="tpu_custom_call" | custom-call | flops 9437184000 | bytes 6553600 | tf_op jit(solution)/shard_map/middle/pallas_call | solution.py:442
  150.5 0.0 copy-start.2
  150.5 1.7 copy-done.2
  152.2 1.2 copy-done.7
  153.4 80.9 %all-to-all-done = f32[32,38,8,128]{3,2,1,0:T(8,128)} async-done(((f32[32,38,8,128]{3,2,1,0:T(8,128)}), f32[32,38,8,128]{3,2,1,0:T(8,128)}, u32[]{:S(2)}, u32[]{:S(2)}) %all-to-all-start) | async-done | bytes 4980768 | tf_op jit(solution)/shard_map/all_to_all | solution.py:682
  234.2 3.5 all-to-all-start.3
  237.7 0.1 slice.62.refs_6_
  237.8 1.4 copy-done.4
  239.2 1.4 copy-done.6
  240.7 1.4 copy-done.8
  242.1 1.1 copy-done.10
  243.2 1.0 copy-done.12
  244.2 31.7 %middle.3 = (f32[16,2,38,8,128]{4,3,2,1,0:T(8,128)}, f32[8,128]{1,0:T(8,128)}) custom-call(f32[16,2,38,8,128]{4,3,2,1,0:T(8,128)} %bitcast.3.refs_0_, f32[640,640]{1,0:T(8,128)S(1)} %copy-done.4, f32[640,640]{1,0:T(8,128)S(1)} %bitcast.41, f32[2,256,384]{2,1,0:T(8,128)S(1)} %copy-done.10, f32[4,256,384]{2,1,0:T(8,128)S(1)} %copy-done.8, ...), custom_call_target="tpu_custom_call" | custom-call | flops 14155776000 | bytes 9961472 | tf_op jit(solution)/shard_map/middle/pallas_call | solution.py:442
  275.9 35.9 %all-to-all-done.3.part_ref = f32[32,25,8,128]{3,2,1,0:T(8,128)S(1)} async-done(((f32[32,25,8,128]{3,2,1,0:T(8,128)}), f32[32,25,8,128]{3,2,1,0:T(8,128)S(1)}, u32[]{:S(2)}, u32[]{:S(2)}) %all-to-all-start.3) | async-done | bytes 3276832 | tf_op jit(solution)/shard_map/all_to_all | solution.py:682
  311.8 3.8 all-to-all-start.2
  316.2 7.2 %inverse_base.1.refs_4_ = f32[40,160,320]{2,1,0:T(8,128)} custom-call(f32[32,25,8,128]{3,2,1,0:T(8,128)S(1)} %all-to-all-done.3.part_ref, f32[128,320]{1,0:T(8,128)S(1)} %bitcast.39), custom_call_target="tpu_custom_call" | custom-call | flops 1572864000 | bytes 24576000 | tf_op jit(solution)/shard_map/inverse_base/pallas_call | solution.py:244
  323.4 103.9 %all-to-all-done.2.refs_0_.refs_1_.refs_2_ = f32[32,38,8,128]{3,2,1,0:T(8,128)} async-done(((f32[32,38,8,128]{3,2,1,0:T(8,128)}), f32[32,38,8,128]{3,2,1,0:T(8,128)}, u32[]{:S(2)}, u32[]{:S(2)}) %all-to-all-start.2) | async-done | bytes 4980768 | tf_op jit(solution)/shard_map/all_to_all | solution.py:682
  427.3 1.0 copy-done.1
  428.3 7.2 %inverse_ends.1 = (f32[16,160,320]{2,1,0:T(8,128)}, f32[8,128]{1,0:T(8,128)S(1)}) custom-call(f32[32,38,8,128]{3,2,1,0:T(8,128)} %all-to-all-done.2.refs_0_.refs_1_.refs_2_, f32[32,38,8,128]{3,2,1,0:T(8,128)} %all-to-all-done.2.refs_0_.refs_1_.refs_2_, f32[32,38,8,128]{3,2,1,0:T(8,128)} %all-to-all-done.2.refs_0_.refs_1_.refs_2_, f32[192,320]{1,0:T(8,128)S(1)} %bitcast.35, ...), custom_call_target="tpu_custom_call" | custom-call | flops 943718400 | bytes 9830400 | tf_op jit(solution)/shard_map/inverse_ends/pallas_call | solution.py:295
  435.5 1.4 fusion.1
  437.0 1.3 collective-permute-start.1
  438.3 3.1 collective-permute-start
  441.4 0.0 copy-start.13
  441.4 12.8 %inverse_inner.1.refs_0_.direction_ref = f32[40,160,320]{2,1,0:T(8,128)} custom-call(f32[32,38,8,128]{3,2,1,0:T(8,128)} %all-to-all-done.2.refs_0_.refs_1_.refs_2_, f32[32,38,8,128]{3,2,1,0:T(8,128)} %all-to-all-done.2.refs_0_.refs_1_.refs_2_, f32[32,38,8,128]{3,2,1,0:T(8,128)} %all-to-all-done.2.refs_0_.refs_1_.refs_2_, f32[192,320]{1,0:T(8,128)S(1)} %bitcast.36, ...), custom_call_target="tpu_custom_call" | custom-call | flops 1415577600 | bytes 14745600 | tf_op jit(solution)/shard_map/inverse_inner/pallas_call | solution.py:295
  454.2 1.3 fusion
  455.5 0.0 collective-permute-done.1.refs_2_
  455.5 0.0 collective-permute-done.refs_1_
  455.6 0.1 maximum_select_fusion
  455.6 0.2 collective-permute-start.2
  455.9 7.8 %collective-permute-done.2 = f32[3,46,320]{2,1,0:T(8,128)S(1)} collective-permute-done((f32[3,46,320]{2,1,0:T(8,128)S(1)}, f32[3,46,320]{2,1,0:T(8,128)S(1)}, u32[]{:S(2)}, u32[]{:S(2)}) %collective-permute-start.2) | collective-permute-done | bytes 176672 | tf_op jit(solution)/shard_map/ppermute | solution.py:486
  463.8 33.7 %stencil.1 = (f32[40,160,320]{2,1,0:T(8,128)}, f32[32,8,128]{2,1,0:T(8,128)S(1)}) custom-call(f32[40,160,320]{2,1,0:T(8,128)} %inverse_inner.1.refs_0_.direction_ref, f32[3,160,320]{2,1,0:T(8,128)S(1)} %collective-permute-done.refs_1_, f32[3,160,320]{2,1,0:T(8,128)S(1)} %collective-permute-done.1.refs_2_, f32[3,46,320]{2,1,0:T(8,128)S(1)} %get-tuple-element.38.refs_3_, ...), custom_call_target="tpu_custom_call" | custom-call | flops 5242880000 | bytes 16384000 | tf_op jit(solution)/shard_map/stencil/pallas_call | solution.py:624
  497.5 11.9 %all_to_all.25.parts_ref = f32[32,8,128]{2,1,0:T(8,128)S(1)} all-to-all(f32[32,8,128]{2,1,0:T(8,128)S(1)} %get-tuple-element.23), channel_id=1, replica_groups=mesh['wide'=16,'narrow'=2] {'wide','narrow'}, dimensions={0} | all-to-all | bytes 262144 | tf_op jit(solution)/shard_map/all_to_all | solution.py:682
  509.3 20.5 %update.1 = (f32[40,160,320]{2,1,0:T(8,128)}, f32[40,160,320]{2,1,0:T(8,128)}) custom-call(f32[8,128]{1,0:T(8,128)S(1)} %get-tuple-element.21.now_ref, f32[32,8,128]{2,1,0:T(8,128)S(1)} %all_to_all.25.parts_ref, f32[40,160,320]{2,1,0:T(8,128)} %solution_ref.1, f32[40,160,320]{2,1,0:T(8,128)} %residual_ref.1, ...), custom_call_target="tpu_custom_call" | custom-call | tf_op jit(solution)/shard_map/update/pallas_call | solution.py:666
  (29 shorter events, 0.2 us)
Async XLA Ops:
  28.0 7.0 %copy-start.14 = (f32[160,320]{1,0:T(8,128)S(1)}, f32[160,320]{1,0:T(8,128)}, u32[]{:S(2)}) copy-start(f32[160,320]{1,0:T(8,128)} %param.16) | copy-start | bytes 614404
  28.0 90.1 %all-to-all-start.1 = ((f32[32,25,8,128]{3,2,1,0:T(8,128)}), f32[32,25,8,128]{3,2,1,0:T(8,128)}, u32[]{:S(2)}, u32[]{:S(2)}) async-start(f32[32,25,8,128]{3,2,1,0:T(8,128)} %forward_z.3), calls=%async_computation.1 | async-start | bytes 6553600 | tf_op jit(solution)/shard_map/all_to_all | solution.py:682
  34.1 57.1 %all-gather.2.cloned.1.call-start = ((), (), s32[]{:S(2)}) async-start(), calls=%async_computation.5 | async-start | bytes 1740800 | tf_op jit(solution)/shard_map/all_gather | solution.py:721
  35.0 23.6 %copy-start = (f32[6,32,320]{2,1,0:T(8,128)}, f32[6,32,320]{2,1,0:T(8,128)S(1)}, u32[]{:S(2)}) copy-start(f32[6,32,320]{2,1,0:T(8,128)S(1)} %copy.39) | copy-start | bytes 737284
  70.9 52.3 %copy-start.16 = (f32[320]{0:T(512)S(1)}, f32[320]{0:T(512)}, u32[]{:S(2)}) copy-start(f32[320]{0:T(512)} %param.19) | copy-start | bytes 3844
  70.9 52.5 %copy-start.15 = (f32[640]{0:T(1024)S(1)}, f32[640]{0:T(1024)}, u32[]{:S(2)}) copy-start(f32[640]{0:T(1024)} %param.18) | copy-start | bytes 7684
  91.2 34.4 %copy-start.3 = (f32[640,640]{1,0:T(8,128)S(1)}, f32[640,640]{1,0:T(8,128)}, u32[]{:S(2)}) copy-start(f32[640,640]{1,0:T(8,128)} %all-gather.2.cloned.1.call-done.refs_1_) | copy-start | bytes 4915204
  118.0 116.2 %all-to-all-start = ((f32[32,38,8,128]{3,2,1,0:T(8,128)}), f32[32,38,8,128]{3,2,1,0:T(8,128)}, u32[]{:S(2)}, u32[]{:S(2)}) async-start(f32[32,38,8,128]{3,2,1,0:T(8,128)} %forward_z.2), calls=%async_computation | async-start | bytes 9961472 | tf_op jit(solution)/shard_map/all_to_all | solution.py:682
  126.7 23.8 %copy-start.5 = (f32[640,640]{0,1:T(8,128)}, f32[640,640]{0,1:T(8,128)S(1)}, u32[]{:S(2)}) copy-start(f32[640,640]{0,1:T(8,128)S(1)} %copy.40) | copy-start | bytes 4915204
  126.7 3.6 copy-start.11
  128.7 1.6 copy-start.9
  150.5 1.7 copy-start.2
  152.2 1.2 copy-start.7
  234.2 77.5 %all-to-all-start.3 = ((f32[32,25,8,128]{3,2,1,0:T(8,128)}), f32[32,25,8,128]{3,2,1,0:T(8,128)S(1)}, u32[]{:S(2)}, u32[]{:S(2)}) async-start(f32[32,25,8,128]{3,2,1,0:T(8,128)} %bitcast.37), calls=%async_computation.3 | async-start | bytes 6553600 | tf_op jit(solution)/shard_map/all_to_all | solution.py:682
  237.8 1.4 copy-start.4
  239.2 1.4 copy-start.6
  240.7 1.4 copy-start.8
  242.1 1.1 copy-start.10
  243.2 1.0 copy-start.12
  311.8 115.6 %all-to-all-start.2 = ((f32[32,38,8,128]{3,2,1,0:T(8,128)}), f32[32,38,8,128]{3,2,1,0:T(8,128)}, u32[]{:S(2)}, u32[]{:S(2)}) async-start(f32[32,38,8,128]{3,2,1,0:T(8,128)} %bitcast.42), calls=%async_computation.2 | async-start | bytes 9961472 | tf_op jit(solution)/shard_map/all_to_all | solution.py:682
  427.3 1.0 copy-start.1
  437.0 18.5 %collective-permute-start.1 = (f32[3,160,320]{2,1,0:T(8,128)S(1)}, f32[3,160,320]{2,1,0:T(8,128)S(1)}, u32[]{:S(2)}, u32[]{:S(2)}) collective-permute-start(f32[3,160,320]{2,1,0:T(8,128)S(1)} %get-tuple-element.29), channel_id=1, source_target_pairs={{2,0},{4,2},{6,4},{8,6},{10,8},{12,10},{14,12},{16,14},{18,16},{20... | collective-permute-start | bytes 1843208 | tf_op jit(solution)/shard_map/ppermute | solution.py:479
  438.3 17.2 %collective-permute-start = (f32[3,160,320]{2,1,0:T(8,128)S(1)}, f32[3,160,320]{2,1,0:T(8,128)S(1)}, u32[]{:S(2)}, u32[]{:S(2)}) collective-permute-start(f32[3,160,320]{2,1,0:T(8,128)S(1)} %get-tuple-element.30), channel_id=1, source_target_pairs={{0,2},{2,4},{4,6},{6,8},{8,10},{10,12},{12,14},{14,16},{16,18},{18... | collective-permute-start | bytes 1843208 | tf_op jit(solution)/shard_map/ppermute | solution.py:479
  441.4 22.4 %copy-start.13 = (bf16[3,2,256,256]{3,2,1,0:T(8,128)(2,1)S(1)}, bf16[3,2,256,256]{3,2,1,0:T(8,128)(2,1)}, u32[]{:S(2)}) copy-start(bf16[3,2,256,256]{3,2,1,0:T(8,128)(2,1)} %constant.24.clone.refs_5_) | copy-start | bytes 2359300
  455.6 8.1 %collective-permute-start.2 = (f32[3,46,320]{2,1,0:T(8,128)S(1)}, f32[3,46,320]{2,1,0:T(8,128)S(1)}, u32[]{:S(2)}, u32[]{:S(2)}) collective-permute-start(f32[3,46,320]{2,1,0:T(8,128)S(1)} %maximum_select_fusion), channel_id=1, source_target_pairs={{0,1},{1,0},{2,3},{3,2},{4,5},{5,4},{6,7},{7,6},{8,9},{9,8},{10,11... | collective-permute-start | bytes 529928 | tf_op jit(solution)/shard_map/ppermute | solution.py:486
Sparse Core Ops, SparseCore 0:
  37.1 54.0 all-gather.1

commit v4 on v3

--- a/solution.py
+++ b/solution.py
@@ -193,7 +193,7 @@
     if ends:
         out_ref, now_ref, high_ref, low_ref, stage_ref = refs[7:]
     else:
-        done_ref, out_ref, high_ref, low_ref, stage_ref = refs[7:]
+        _, out_ref, high_ref, low_ref, stage_ref = refs[7:]
     step = pl.program_id(0)
 
     @pl.when(step == 0)
@@ -211,15 +211,7 @@
         if ends:
             now_ref[...] = jnp.broadcast_to(now, now_ref.shape)
 
-    if ends:
-        work()
-    else:
-        inner = (step > 0) & (step < plan.tiles - 1)
-        pl.when(inner)(work)
-
-        @pl.when(jnp.logical_not(inner))
-        def _():
-            out_ref[...] = done_ref[...]
+    work()
 
 
 def inverse_scratch(plan, basis):
@@ -265,7 +257,7 @@
     if ends:
         pick = lambda t: t * last
     else:
-        pick = lambda t: jnp.clip(t, 1, last - 1)
+        pick = lambda t: t + 1
     tile = (8, plan.cells_y, plan.cells_z)
     brick = pl.BlockSpec(tile, lambda t: (pick(t), 0, 0))
     _, per, _, _, fit, _ = plan.shape_of(chunk)
@@ -281,20 +273,21 @@
         pl.BlockSpec((1, 1), lambda t: (0, 0)),
     ]
     operands = [part, part, part, basis, base, old, before.reshape(1, 1)]
-    out_specs = pl.BlockSpec(tile, lambda t: (t, 0, 0))
+    out_specs = brick
     if ends:
         out_specs = [out_specs, pl.BlockSpec((8, LANES), lambda t: (0, 0))]
         out_shape = [
-            jax.ShapeDtypeStruct((16,) + base.shape[1:], jnp.float32),
+            jax.ShapeDtypeStruct(base.shape, jnp.float32),
             jax.ShapeDtypeStruct((8, LANES), jnp.float32),
         ]
     else:
-        in_specs.append(pl.BlockSpec(tile, lambda t: (t // last, 0, 0)))
+        in_specs.append(pl.BlockSpec(memory_space=pl.ANY))
         operands.append(done)
         out_shape = jax.ShapeDtypeStruct(base.shape, jnp.float32)
     return pl.pallas_call(
         functools.partial(final_kernel, plan, chunk, ends, pick),
-        grid=(2 if ends else plan.tiles,),
+        grid=(2 if ends else plan.tiles - 2,),
+        input_output_aliases={} if ends else {len(operands) - 1: 0},
         in_specs=in_specs,
         out_specs=out_specs,
         out_shape=out_shape,
@@ -511,13 +504,15 @@
 
 
 def stencil_kernel(plan, *refs):
-    own, before_x, after_x, before_y, after_y, bands_ref, image_ref, sum_ref = refs[:8]
-    field, f_high, f_low, s_high, s_low, h_a, h_b, total, sems = refs[8:]
+    own, before_x, after_x, before_y, after_y, bands_ref, out, sum_ref = refs[:8]
+    field, image_ref, f_high, f_low, s_high, s_low, h_a, h_b, total, sems, out_sems = refs[8:]
     cells_x, cells_y, cells_z = plan.cells_x, plan.cells_y, plan.cells_z
     tiles = plan.tiles
     padded_y = cells_y + 2 * EDGE
     own_y = pl.ds(EDGE, cells_y)
-    step = pl.program_id(0)
+    groups = cells_x // GROUP
+    blocks = h_a.shape[1]
+    ratio = stiff_scale / mass_scale
 
     def tile_copy(t):
         return pltpu.make_async_copy(
@@ -531,37 +526,18 @@
         after_x, field.at[pl.ds(HALO + cells_x, HALO), own_y, :], sems.at[tiles + 1]
     )
 
-    @pl.when(step == 0)
-    def _():
-        first_copy.start()
-        for t in range(tiles):
-            tile_copy(t).start()
-        last_copy.start()
-        total[...] = jnp.zeros_like(total)
-        field[:, EDGE - HALO : EDGE, :] = jnp.swapaxes(before_y[...], 0, 1)
-        field[:, EDGE + cells_y : EDGE + cells_y + HALO, :] = jnp.swapaxes(after_y[...], 0, 1)
-        first_copy.wait()
-        tile_copy(0).wait()
-
-    @pl.when(step < tiles - 1)
-    def _():
-        tile_copy(step + 1).wait()
-
-    @pl.when(step == tiles - 1)
-    def _():
-        last_copy.wait()
-
-    blocks = h_a.shape[0]
-    ratio = stiff_scale / mass_scale
+    def out_copy(t):
+        rows = pl.ds(8 * t, 8)
+        return pltpu.make_async_copy(image_ref.at[rows], out.at[rows], out_sems.at[t])
 
     def one(left, right):
         return lax.dot_general(
             left, right, (((1,), (0,)), ((), ())), preferred_element_type=jnp.float32
         )
 
-    def planes(g, carry):
+    def bands_x(g, slot):
         for i in range(GROUP):
-            x = step * 8 + g * GROUP + i
+            x = g * GROUP + i
             middle_plane = field[x + HALO]
             first = ratio * stiff_band[HALO] * middle_plane
             second = mass_band[HALO] * middle_plane
@@ -570,41 +546,81 @@
                 first = first + ratio * stiff_band[HALO + o] * around
                 second = second + mass_band[HALO + o] * around
             rows = pl.ds(i * padded_y, padded_y)
-            f_high[rows, :], f_low[rows, :] = split(first)
-            s_high[rows, :], s_low[rows, :] = split(second)
+            f_high[slot, rows, :], f_low[slot, rows, :] = split(first)
+            s_high[slot, rows, :], s_low[slot, rows, :] = split(second)
+
+    def bands_z(slot):
         window_a, window_b = [], []
         for w, lanes in enumerate((pl.ds(0, 2 * LANES), pl.ds(LANES, cells_z - LANES))):
             high, low, stiff = (bands_ref[k, w, : lanes.size, :] for k in range(3))
-            fh, fl, sh, sl = (ref[:, lanes] for ref in (f_high, f_low, s_high, s_low))
+            fh, fl, sh, sl = (ref[slot, :, lanes] for ref in (f_high, f_low, s_high, s_low))
             window_a.append(
                 one(fh, high) + one(fl, high) + one(fh, low) + one(sh, stiff) + one(sl, stiff)
             )
             window_b.append(one(sh, high) + one(sl, high) + one(sh, low))
         for ref, (left, right) in ((h_a, window_a), (h_b, window_b)):
-            ref[0] = left[:, :LANES]
-            ref[1] = left[:, LANES:] + right[:, :LANES]
-            ref[2] = right[:, LANES:]
+            ref[slot, 0] = left[:, :LANES]
+            ref[slot, 1] = left[:, LANES:] + right[:, :LANES]
+            ref[slot, 2] = right[:, LANES:]
+
+    def bands_y(g, slot, valid=None):
         for i in range(GROUP):
-            plane = g * GROUP + i
+            x = g * GROUP + i
             for k in range(blocks):
                 lanes = min(LANES, cells_z - k * LANES)
-                at = lambda ref, o: ref[k, pl.ds(i * padded_y + EDGE + o, cells_y), :]
+                at = lambda ref, o: ref[slot, k, pl.ds(i * padded_y + EDGE + o, cells_y), :]
                 image = (mass_band[HALO] / stiff_scale) * at(h_a, 0)
                 image = image + (stiff_band[HALO] / mass_scale) * at(h_b, 0)
                 for o in range(1, HALO + 1):
                     image = image + (mass_band[HALO + o] / stiff_scale) * (at(h_a, -o) + at(h_a, o))
                     image = image + (stiff_band[HALO + o] / mass_scale) * (at(h_b, -o) + at(h_b, o))
                 here = pl.ds(k * LANES, lanes)
-                image_ref[plane, :, here] = image[:, :lanes]
-                product = image[:, :lanes] * field[step * 8 + plane + HALO, own_y, here]
-                total[:, here] += jnp.sum(product.reshape(cells_y // 8, 8, lanes), axis=0)
+                image_ref[x, :, here] = image[:, :lanes]
+                product = image[:, :lanes] * field[x + HALO, own_y, here]
+                product = jnp.sum(product.reshape(cells_y // 8, 8, lanes), axis=0)
+                if valid is not None:
+                    product = jnp.where(valid, product, 0.0)
+                total[:, here] += product
+
+    first_copy.start()
+    for t in range(tiles):
+        tile_copy(t).start()
+    last_copy.start()
+    total[...] = jnp.zeros_like(total)
+    field[:, EDGE - HALO : EDGE, :] = jnp.swapaxes(before_y[...], 0, 1)
+    field[:, EDGE + cells_y : EDGE + cells_y + HALO, :] = jnp.swapaxes(after_y[...], 0, 1)
+    first_copy.wait()
+    tile_copy(0).wait()
+    bands_x(0, 0)
+
+    def step(k, carry):
+        @pl.when(k < tiles - 1)
+        def _():
+            tile_copy(k + 1).wait()
+
+        @pl.when(k == tiles - 1)
+        def _():
+            last_copy.wait()
+
+        bands_z(0)
+        bands_x(2 * k + 1, 1)
+        bands_y(jnp.maximum(2 * k - 1, 0), 1, k > 0)
+
+        @pl.when(k > 0)
+        def _():
+            out_copy(k - 1).start()
+
+        bands_z(1)
+        bands_x(jnp.minimum(2 * k + 2, groups - 1), 0)
+        bands_y(2 * k, 0)
         return carry
 
-    lax.fori_loop(0, 8 // GROUP, planes, 0)
-
-    @pl.when(step == pl.num_programs(0) - 1)
-    def _():
-        sum_ref[...] = jnp.full(sum_ref.shape, jnp.sum(total[...]), jnp.float32)
+    lax.fori_loop(0, tiles, step, 0)
+    bands_y(groups - 1, 1)
+    out_copy(tiles - 1).start()
+    sum_ref[...] = jnp.full(sum_ref.shape, jnp.sum(total[...]), jnp.float32)
+    for t in range(tiles):
+        out_copy(t).wait()
 
 
 def stencil(plan, direction, before_x, after_x):
@@ -620,31 +636,29 @@
     bands = band_matrices(cells_z)
     padded_y = cells_y + 2 * EDGE
     blocks = -(-cells_z // LANES)
-    lump = (GROUP * padded_y, cells_z)
+    lump = (2, GROUP * padded_y, cells_z)
+    rows = (2, blocks, GROUP * padded_y, LANES)
+    whole = pl.BlockSpec(memory_space=pltpu.VMEM)
     return pl.pallas_call(
         functools.partial(stencil_kernel, plan),
-        grid=(cells_x // 8,),
-        in_specs=[pl.BlockSpec(memory_space=pl.ANY)] * 3
-        + [pl.BlockSpec(before_y.shape, lambda t: (0, 0, 0))] * 2
-        + [pl.BlockSpec(bands.shape, lambda t: (0, 0, 0, 0))],
-        out_specs=[
-            pl.BlockSpec((8, cells_y, cells_z), lambda t: (t, 0, 0)),
-            pl.BlockSpec((plan.count, 8, LANES), lambda t: (0, 0, 0)),
-        ],
+        in_specs=[pl.BlockSpec(memory_space=pl.ANY)] * 3 + [whole] * 3,
+        out_specs=[pl.BlockSpec(memory_space=pl.ANY), whole],
         out_shape=[
             jax.ShapeDtypeStruct(direction.shape, jnp.float32),
             jax.ShapeDtypeStruct((plan.count, 8, LANES), jnp.float32),
         ],
         scratch_shapes=[
             pltpu.VMEM((cells_x + 2 * HALO, padded_y, cells_z), jnp.float32),
+            pltpu.VMEM(direction.shape, jnp.float32),
             pltpu.VMEM(lump, jnp.bfloat16),
             pltpu.VMEM(lump, jnp.bfloat16),
             pltpu.VMEM(lump, jnp.bfloat16),
             pltpu.VMEM(lump, jnp.bfloat16),
-            pltpu.VMEM((blocks, GROUP * padded_y, LANES), jnp.float32),
-            pltpu.VMEM((blocks, GROUP * padded_y, LANES), jnp.float32),
+            pltpu.VMEM(rows, jnp.float32),
+            pltpu.VMEM(rows, jnp.float32),
             pltpu.VMEM((8, cells_z), jnp.float32),
             pltpu.SemaphoreType.DMA((plan.tiles + 2,)),
+            pltpu.SemaphoreType.DMA((plan.tiles,)),
         ],
         compiler_params=pltpu.CompilerParams(vmem_limit_bytes=50 * MIB),
         cost_estimate=pl.CostEstimate(
@@ -750,7 +764,7 @@
         inverse_final, plan, 1, returned[1], turned_z, base, direction, previous_product
     )
     ends, now = inverse()
-    before_x = shifted(ends[16 - HALO :], -1, "wide")
+    before_x = shifted(ends[plan.cells_x - HALO :], -1, "wide")
     after_x = shifted(ends[:HALO], 1, "wide")
     direction = inverse(ends)
     image, part = stencil(plan, direction, before_x, after_x)

time: 541 us -> 544 us (level)
  transfers between devices with their start and end apart: 8 -> 8, of which waited for: 6 -> 6; matrix products, arithmetic and copies ran while one was open for 2% -> 2% of each run, Pallas kernels for 16% -> 15%
where the time goes in v4:
time: 544 us; the launch traced here: 540 us
  waiting for transfers between devices  275 us (51%)
  Pallas kernels  158 us (29%)
  blocking collectives  48.1 us (9%)
  starting transfers between devices  22.5 us (4%)
  local copies, waits for them, and re-layouts  21.1 us (4%)
  between operations  15.3 us (3%)
    all_to_all x4, waiting for transfers between devices, scatter(): return lax.all_to_all(x, both, split_axis=0, concat_axis=0, tiled=True)  247 us
    pallas_call x2, Pallas kernels, middle(): pl.pallas_call(functools.partial(middle_kernel, plan, chunk), out_shape=[...  51.9 us
    pallas_call x1, Pallas kernels, stencil(): pl.pallas_call(functools.partial(stencil_kernel, plan), in_specs=[pl.Bloc...  36.8 us
    all_gather x1, blocking collectives, by_pencils(): whole_y = lax.all_gather(basis_y, 'narrow', axis=0, tiled=True)  23.6 us
    pallas_call x2, Pallas kernels, forward_z(): pl.pallas_call(functools.partial(forward_kernel, plan, chunk), grid=(plan...  22.9 us
    pallas_call x1, Pallas kernels, update(): pl.pallas_call(update_kernel, grid=(image.shape[0] // 4,), in_specs=[pl.B...  20.5 us
    all_gather x1, waiting for transfers between devices, by_pencils(): whole_x = lax.all_gather(basis_x, 'wide', axis=0, tiled=True)  20.3 us
    pallas_call x2, Pallas kernels, inverse_final(): pl.pallas_call(functools.partial(final_kernel, plan, chunk, ends, pick),...  18.6 us
  transfers between devices with their start and end apart: 8, of which 6 were waited for; matrix products, arithmetic and copies ran while one was open for 2% of the time, Pallas kernels for 15%

profile of v4, /device:TPU:0, one launch (start us, length us, event | category | flops | bytes accessed | tf_op | source)
XLA Modules:
  0.0 539.8 jit_solution(17106427122100430156)
XLA Ops:
  7.2 9.9 %all_gather.9 = f32[320,320]{1,0:T(8,128)S(1)} all-gather(f32[160,320]{1,0:T(8,128)} %param.17), channel_id=1, replica_groups=mesh['wide'=16,'narrow'=2] {'narrow'}, dimensions={0}, use_global_device_ids=true | all-gather | bytes 614400 | tf_op jit(solution)/shard_map/all_gather | solution.py:732
  17.0 0.2 copy.39
  17.2 0.1 reshape.43
  17.4 10.6 %forward_z.3 = f32[32,25,8,128]{3,2,1,0:T(8,128)} custom-call(f32[40,160,320]{2,1,0:T(8,128)} %residual_ref.1, f32[128,320]{1,0:T(8,128)S(1)} %bitcast.38), custom_call_target="tpu_custom_call" | custom-call | flops 1572864000 | bytes 16384000 | tf_op jit(solution)/shard_map/forward_z/pallas_call | solution.py:138
  28.0 6.1 %all-to-all-start.1 = ((f32[32,25,8,128]{3,2,1,0:T(8,128)}), f32[32,25,8,128]{3,2,1,0:T(8,128)}, u32[]{:S(2)}, u32[]{:S(2)}) async-start(f32[32,25,8,128]{3,2,1,0:T(8,128)} %forward_z.3), calls=%async_computation.1 | async-start | bytes 6553600 | tf_op jit(solution)/shard_map/all_to_all | solution.py:696
  34.1 0.0 all-gather.2.cloned.1.call-start
  34.2 0.7 all-gather.2.cloned.1.call-update
  34.9 0.1 copy.40
  35.0 0.0 copy-done.14
  35.0 0.0 copy-start
  35.0 23.6 %all_gather.11 = f32[320,320]{1,0:T(8,128)S(1)} all-gather(f32[160,320]{1,0:T(8,128)S(1)} %copy-done.14), channel_id=1, replica_groups=mesh['wide'=16,'narrow'=2] {'narrow'}, dimensions={0}, use_global_device_ids=true | all-gather | bytes 614400 | tf_op jit(solution)/shard_map/all_gather | solution.py:734
  58.6 0.0 copy-done
  58.6 12.3 %forward_z.2 = f32[32,38,8,128]{3,2,1,0:T(8,128)} custom-call(f32[40,160,320]{2,1,0:T(8,128)} %residual_ref.1, f32[192,320]{1,0:T(8,128)S(1)} %bitcast.34), custom_call_target="tpu_custom_call" | custom-call | flops 2359296000 | bytes 16384000 | tf_op jit(solution)/shard_map/forward_z/pallas_call | solution.py:138
  70.9 20.3 %all-gather.2.cloned.1.call-done.refs_1_ = f32[640,640]{1,0:T(8,128)} async-done(((f32[40,640]{1,0:T(8,128)}), f32[640,640]{1,0:T(8,128)}) %all-gather.2.cloned.1.call-update) | async-done | bytes 1638416 | tf_op jit(solution)/shard_map/all_gather | solution.py:735
  91.3 26.8 %all-to-all-done.1 = f32[32,25,8,128]{3,2,1,0:T(8,128)} async-done(((f32[32,25,8,128]{3,2,1,0:T(8,128)}), f32[32,25,8,128]{3,2,1,0:T(8,128)}, u32[]{:S(2)}, u32[]{:S(2)}) %all-to-all-start.1) | async-done | bytes 3276832 | tf_op jit(solution)/shard_map/all_to_all | solution.py:696
  118.0 4.4 all-to-all-start
  122.5 0.8 dynamic_slice.3
  123.2 0.0 copy-done.16
  123.2 0.1 broadcast_add_fusion
  123.3 0.1 slice.66.refs_6_
  123.4 0.9 reshape.52.refs_5_
  124.3 0.6 slice.77
  124.9 0.8 slice.76
  125.7 1.0 copy.41
  126.7 0.0 copy-start.5
  126.7 0.0 copy-start.11
  126.8 1.9 pad_bitcast_fusion.1
  128.6 0.1 pad_maximum_fusion.1.refs_3_
  128.7 0.0 copy-start.9
  128.7 1.5 fusion.4
  130.2 0.1 pad_maximum_fusion.refs_4_
  130.3 20.1 %middle.2 = (f32[16,2,25,8,128]{4,3,2,1,0:T(8,128)S(1)}, f32[8,128]{1,0:T(8,128)S(1)}) custom-call(f32[16,2,25,8,128]{4,3,2,1,0:T(8,128)} %bitcast.14.refs_0_, f32[640,640]{1,0:T(8,128)S(1)} %copy-done.3, f32[640,640]{1,0:T(8,128)S(1)} %bitcast.40, f32[2,256,384]{2,1,0:T(8,128)S(1)} %pad_maximum_fusion.1.refs_3_, ...), custom_call_target="tpu_custom_call" | custom-call | flops 9437184000 | bytes 6553600 | tf_op jit(solution)/shard_map/middle/pallas_call | solution.py:435
  150.5 0.0 copy-start.2
  150.5 1.7 copy-done.2
  152.2 1.2 copy-done.7
  153.4 80.9 %all-to-all-done = f32[32,38,8,128]{3,2,1,0:T(8,128)} async-done(((f32[32,38,8,128]{3,2,1,0:T(8,128)}), f32[32,38,8,128]{3,2,1,0:T(8,128)}, u32[]{:S(2)}, u32[]{:S(2)}) %all-to-all-start) | async-done | bytes 4980768 | tf_op jit(solution)/shard_map/all_to_all | solution.py:696
  234.2 3.5 all-to-all-start.3
  237.7 0.1 slice.62.refs_6_
  237.8 1.4 copy-done.4
  239.2 1.4 copy-done.6
  240.7 1.4 copy-done.8
  242.1 1.1 copy-done.10
  243.2 1.0 copy-done.12
  244.2 31.7 %middle.3 = (f32[16,2,38,8,128]{4,3,2,1,0:T(8,128)}, f32[8,128]{1,0:T(8,128)}) custom-call(f32[16,2,38,8,128]{4,3,2,1,0:T(8,128)} %bitcast.3.refs_0_, f32[640,640]{1,0:T(8,128)S(1)} %copy-done.4, f32[640,640]{1,0:T(8,128)S(1)} %bitcast.41, f32[2,256,384]{2,1,0:T(8,128)S(1)} %copy-done.10, f32[4,256,384]{2,1,0:T(8,128)S(1)} %copy-done.8, ...), custom_call_target="tpu_custom_call" | custom-call | flops 14155776000 | bytes 9961472 | tf_op jit(solution)/shard_map/middle/pallas_call | solution.py:435
  275.9 35.9 %all-to-all-done.3.part_ref = f32[32,25,8,128]{3,2,1,0:T(8,128)S(1)} async-done(((f32[32,25,8,128]{3,2,1,0:T(8,128)}), f32[32,25,8,128]{3,2,1,0:T(8,128)S(1)}, u32[]{:S(2)}, u32[]{:S(2)}) %all-to-all-start.3) | async-done | bytes 3276832 | tf_op jit(solution)/shard_map/all_to_all | solution.py:696
  311.8 3.8 all-to-all-start.2
  316.2 7.2 %inverse_base.1.refs_4_ = f32[40,160,320]{2,1,0:T(8,128)} custom-call(f32[32,25,8,128]{3,2,1,0:T(8,128)S(1)} %all-to-all-done.3.part_ref, f32[128,320]{1,0:T(8,128)S(1)} %bitcast.39), custom_call_target="tpu_custom_call" | custom-call | flops 1572864000 | bytes 24576000 | tf_op jit(solution)/shard_map/inverse_base/pallas_call | solution.py:236
  323.4 103.9 %all-to-all-done.2.refs_0_.refs_1_.refs_2_ = f32[32,38,8,128]{3,2,1,0:T(8,128)} async-done(((f32[32,38,8,128]{3,2,1,0:T(8,128)}), f32[32,38,8,128]{3,2,1,0:T(8,128)}, u32[]{:S(2)}, u32[]{:S(2)}) %all-to-all-start.2) | async-done | bytes 4980768 | tf_op jit(solution)/shard_map/all_to_all | solution.py:696
  427.3 1.0 copy-done.1
  428.3 7.2 %inverse_ends.1 = (f32[40,160,320]{2,1,0:T(8,128)}, f32[8,128]{1,0:T(8,128)S(1)}) custom-call(f32[32,38,8,128]{3,2,1,0:T(8,128)} %all-to-all-done.2.refs_0_.refs_1_.refs_2_, f32[32,38,8,128]{3,2,1,0:T(8,128)} %all-to-all-done.2.refs_0_.refs_1_.refs_2_, f32[32,38,8,128]{3,2,1,0:T(8,128)} %all-to-all-done.2.refs_0_.refs_1_.refs_2_, f32[192,320]{1,0:T(8,128)S(1)} %bitcast.35, ...), custom_call_target="tpu_custom_call" | custom-call | flops 943718400 | bytes 9830400 | tf_op jit(solution)/shard_map/inverse_ends/pallas_call | solution.py:287
  435.5 1.4 fusion.1
  437.0 1.3 collective-permute-start.1
  438.3 3.1 collective-permute-start
  441.4 0.0 copy-start.13
  441.4 11.3 %inverse_inner.1.refs_0_.direction_ref = f32[40,160,320]{2,1,0:T(8,128)} custom-call(f32[32,38,8,128]{3,2,1,0:T(8,128)} %all-to-all-done.2.refs_0_.refs_1_.refs_2_, f32[32,38,8,128]{3,2,1,0:T(8,128)} %all-to-all-done.2.refs_0_.refs_1_.refs_2_, f32[32,38,8,128]{3,2,1,0:T(8,128)} %all-to-all-done.2.refs_0_.refs_1_.refs_2_, ...), custom_call_target="tpu_custom_call", output_to_operand_aliasing={{}: (7, {})} | custom-call | flops 1415577600 | bytes 14745600 | tf_op jit(solution)/shard_map/inverse_inner/pallas_call | solution.py:287
  452.7 1.3 fusion
  454.0 0.0 collective-permute-done.1.refs_2_
  454.1 0.0 collective-permute-done.refs_1_
  454.1 0.1 maximum_select_fusion
  454.2 0.2 collective-permute-start.2
  454.4 6.2 %collective-permute-done.2 = f32[3,46,320]{2,1,0:T(8,128)S(1)} collective-permute-done((f32[3,46,320]{2,1,0:T(8,128)S(1)}, f32[3,46,320]{2,1,0:T(8,128)S(1)}, u32[]{:S(2)}, u32[]{:S(2)}) %collective-permute-start.2) | collective-permute-done | bytes 176672 | tf_op jit(solution)/shard_map/ppermute | solution.py:479
  460.7 36.8 %stencil.1 = (f32[40,160,320]{2,1,0:T(8,128)}, f32[32,8,128]{2,1,0:T(8,128)S(1)}) custom-call(f32[40,160,320]{2,1,0:T(8,128)} %inverse_inner.1.refs_0_.direction_ref, f32[3,160,320]{2,1,0:T(8,128)S(1)} %collective-permute-done.refs_1_, f32[3,160,320]{2,1,0:T(8,128)S(1)} %collective-permute-done.1.refs_2_, f32[3,46,320]{2,1,0:T(8,128)S(1)} %get-tuple-element.38.refs_3_, ...), custom_call_target="tpu_custom_call" | custom-call | flops 5242880000 | bytes 16384000 | tf_op jit(solution)/shard_map/stencil/pallas_call | solution.py:642
  497.6 14.6 %all_to_all.25.parts_ref = f32[32,8,128]{2,1,0:T(8,128)S(1)} all-to-all(f32[32,8,128]{2,1,0:T(8,128)S(1)} %get-tuple-element.23), channel_id=1, replica_groups=mesh['wide'=16,'narrow'=2] {'wide','narrow'}, dimensions={0} | all-to-all | bytes 262144 | tf_op jit(solution)/shard_map/all_to_all | solution.py:696
  512.2 20.5 %update.1 = (f32[40,160,320]{2,1,0:T(8,128)}, f32[40,160,320]{2,1,0:T(8,128)}) custom-call(f32[8,128]{1,0:T(8,128)S(1)} %get-tuple-element.21.now_ref, f32[32,8,128]{2,1,0:T(8,128)S(1)} %all_to_all.25.parts_ref, f32[40,160,320]{2,1,0:T(8,128)} %solution_ref.1, f32[40,160,320]{2,1,0:T(8,128)} %residual_ref.1, ...), custom_call_target="tpu_custom_call" | custom-call | tf_op jit(solution)/shard_map/update/pallas_call | solution.py:680
  (29 shorter events, 0.2 us)
Async XLA Ops:
  28.0 7.0 %copy-start.14 = (f32[160,320]{1,0:T(8,128)S(1)}, f32[160,320]{1,0:T(8,128)}, u32[]{:S(2)}) copy-start(f32[160,320]{1,0:T(8,128)} %param.16) | copy-start | bytes 614404
  28.0 90.1 %all-to-all-start.1 = ((f32[32,25,8,128]{3,2,1,0:T(8,128)}), f32[32,25,8,128]{3,2,1,0:T(8,128)}, u32[]{:S(2)}, u32[]{:S(2)}) async-start(f32[32,25,8,128]{3,2,1,0:T(8,128)} %forward_z.3), calls=%async_computation.1 | async-start | bytes 6553600 | tf_op jit(solution)/shard_map/all_to_all | solution.py:696
  34.1 57.1 %all-gather.2.cloned.1.call-start = ((), (), s32[]{:S(2)}) async-start(), calls=%async_computation.5 | async-start | bytes 1740800 | tf_op jit(solution)/shard_map/all_gather | solution.py:735
  35.0 23.6 %copy-start = (f32[6,32,320]{2,1,0:T(8,128)}, f32[6,32,320]{2,1,0:T(8,128)S(1)}, u32[]{:S(2)}) copy-start(f32[6,32,320]{2,1,0:T(8,128)S(1)} %copy.40) | copy-start | bytes 737284
  70.9 52.3 %copy-start.16 = (f32[320]{0:T(512)S(1)}, f32[320]{0:T(512)}, u32[]{:S(2)}) copy-start(f32[320]{0:T(512)} %param.19) | copy-start | bytes 3844
  70.9 52.5 %copy-start.15 = (f32[640]{0:T(1024)S(1)}, f32[640]{0:T(1024)}, u32[]{:S(2)}) copy-start(f32[640]{0:T(1024)} %param.18) | copy-start | bytes 7684
  91.2 34.4 %copy-start.3 = (f32[640,640]{1,0:T(8,128)S(1)}, f32[640,640]{1,0:T(8,128)}, u32[]{:S(2)}) copy-start(f32[640,640]{1,0:T(8,128)} %all-gather.2.cloned.1.call-done.refs_1_) | copy-start | bytes 4915204
  118.0 116.2 %all-to-all-start = ((f32[32,38,8,128]{3,2,1,0:T(8,128)}), f32[32,38,8,128]{3,2,1,0:T(8,128)}, u32[]{:S(2)}, u32[]{:S(2)}) async-start(f32[32,38,8,128]{3,2,1,0:T(8,128)} %forward_z.2), calls=%async_computation | async-start | bytes 9961472 | tf_op jit(solution)/shard_map/all_to_all | solution.py:696
  126.7 23.8 %copy-start.5 = (f32[640,640]{0,1:T(8,128)}, f32[640,640]{0,1:T(8,128)S(1)}, u32[]{:S(2)}) copy-start(f32[640,640]{0,1:T(8,128)S(1)} %copy.41) | copy-start | bytes 4915204
  126.7 3.6 copy-start.11
  128.7 1.6 copy-start.9
  150.5 1.7 copy-start.2
  152.2 1.2 copy-start.7
  234.2 77.5 %all-to-all-start.3 = ((f32[32,25,8,128]{3,2,1,0:T(8,128)}), f32[32,25,8,128]{3,2,1,0:T(8,128)S(1)}, u32[]{:S(2)}, u32[]{:S(2)}) async-start(f32[32,25,8,128]{3,2,1,0:T(8,128)} %bitcast.37), calls=%async_computation.3 | async-start | bytes 6553600 | tf_op jit(solution)/shard_map/all_to_all | solution.py:696
  237.8 1.4 copy-start.4
  239.2 1.4 copy-start.6
  240.7 1.4 copy-start.8
  242.1 1.1 copy-start.10
  243.2 1.0 copy-start.12
  311.8 115.6 %all-to-all-start.2 = ((f32[32,38,8,128]{3,2,1,0:T(8,128)}), f32[32,38,8,128]{3,2,1,0:T(8,128)}, u32[]{:S(2)}, u32[]{:S(2)}) async-start(f32[32,38,8,128]{3,2,1,0:T(8,128)} %bitcast.42), calls=%async_computation.2 | async-start | bytes 9961472 | tf_op jit(solution)/shard_map/all_to_all | solution.py:696
  427.3 1.0 copy-start.1
  437.0 17.0 %collective-permute-start.1 = (f32[3,160,320]{2,1,0:T(8,128)S(1)}, f32[3,160,320]{2,1,0:T(8,128)S(1)}, u32[]{:S(2)}, u32[]{:S(2)}) collective-permute-start(f32[3,160,320]{2,1,0:T(8,128)S(1)} %get-tuple-element.29), channel_id=1, source_target_pairs={{2,0},{4,2},{6,4},{8,6},{10,8},{12,10},{14,12},{16,14},{18,16},{20... | collective-permute-start | bytes 1843208 | tf_op jit(solution)/shard_map/ppermute | solution.py:472
  438.3 15.8 %collective-permute-start = (f32[3,160,320]{2,1,0:T(8,128)S(1)}, f32[3,160,320]{2,1,0:T(8,128)S(1)}, u32[]{:S(2)}, u32[]{:S(2)}) collective-permute-start(f32[3,160,320]{2,1,0:T(8,128)S(1)} %get-tuple-element.30), channel_id=1, source_target_pairs={{0,2},{2,4},{4,6},{6,8},{8,10},{10,12},{12,14},{14,16},{16,18},{18... | collective-permute-start | bytes 1843208 | tf_op jit(solution)/shard_map/ppermute | solution.py:472
  441.4 19.4 %copy-start.13 = (bf16[3,2,256,256]{3,2,1,0:T(8,128)(2,1)S(1)}, bf16[3,2,256,256]{3,2,1,0:T(8,128)(2,1)}, u32[]{:S(2)}) copy-start(bf16[3,2,256,256]{3,2,1,0:T(8,128)(2,1)} %constant.24.clone.refs_5_) | copy-start | bytes 2359300
  454.2 6.5 %collective-permute-start.2 = (f32[3,46,320]{2,1,0:T(8,128)S(1)}, f32[3,46,320]{2,1,0:T(8,128)S(1)}, u32[]{:S(2)}, u32[]{:S(2)}) collective-permute-start(f32[3,46,320]{2,1,0:T(8,128)S(1)} %maximum_select_fusion), channel_id=1, source_target_pairs={{0,1},{1,0},{2,3},{3,2},{4,5},{5,4},{6,7},{7,6},{8,9},{9,8},{10,11... | collective-permute-start | bytes 529928 | tf_op jit(solution)/shard_map/ppermute | solution.py:479
Sparse Core Ops, SparseCore 0:
  37.1 54.0 all-gather.1

commit v5 on v3

--- a/solution.py
+++ b/solution.py
@@ -193,7 +193,7 @@
     if ends:
         out_ref, now_ref, high_ref, low_ref, stage_ref = refs[7:]
     else:
-        done_ref, out_ref, high_ref, low_ref, stage_ref = refs[7:]
+        _, out_ref, high_ref, low_ref, stage_ref = refs[7:]
     step = pl.program_id(0)
 
     @pl.when(step == 0)
@@ -211,15 +211,7 @@
         if ends:
             now_ref[...] = jnp.broadcast_to(now, now_ref.shape)
 
-    if ends:
-        work()
-    else:
-        inner = (step > 0) & (step < plan.tiles - 1)
-        pl.when(inner)(work)
-
-        @pl.when(jnp.logical_not(inner))
-        def _():
-            out_ref[...] = done_ref[...]
+    work()
 
 
 def inverse_scratch(plan, basis):
@@ -265,7 +257,7 @@
     if ends:
         pick = lambda t: t * last
     else:
-        pick = lambda t: jnp.clip(t, 1, last - 1)
+        pick = lambda t: t + 1
     tile = (8, plan.cells_y, plan.cells_z)
     brick = pl.BlockSpec(tile, lambda t: (pick(t), 0, 0))
     _, per, _, _, fit, _ = plan.shape_of(chunk)
@@ -281,20 +273,21 @@
         pl.BlockSpec((1, 1), lambda t: (0, 0)),
     ]
     operands = [part, part, part, basis, base, old, before.reshape(1, 1)]
-    out_specs = pl.BlockSpec(tile, lambda t: (t, 0, 0))
+    out_specs = brick
     if ends:
         out_specs = [out_specs, pl.BlockSpec((8, LANES), lambda t: (0, 0))]
         out_shape = [
-            jax.ShapeDtypeStruct((16,) + base.shape[1:], jnp.float32),
+            jax.ShapeDtypeStruct(base.shape, jnp.float32),
             jax.ShapeDtypeStruct((8, LANES), jnp.float32),
         ]
     else:
-        in_specs.append(pl.BlockSpec(tile, lambda t: (t // last, 0, 0)))
+        in_specs.append(pl.BlockSpec(memory_space=pl.ANY))
         operands.append(done)
         out_shape = jax.ShapeDtypeStruct(base.shape, jnp.float32)
     return pl.pallas_call(
         functools.partial(final_kernel, plan, chunk, ends, pick),
-        grid=(2 if ends else plan.tiles,),
+        grid=(2 if ends else plan.tiles - 2,),
+        input_output_aliases={} if ends else {len(operands) - 1: 0},
         in_specs=in_specs,
         out_specs=out_specs,
         out_shape=out_shape,
@@ -507,12 +500,14 @@
     mass, stiff = tables
     high = mass.astype(ml_dtypes.bfloat16)
     low = (mass - high.astype(np.float32)).astype(ml_dtypes.bfloat16)
-    return np.stack([high, low, stiff.astype(ml_dtypes.bfloat16)])
+    stiff = stiff.astype(ml_dtypes.bfloat16)
+    mixed = np.concatenate([high, high, low, stiff, stiff], axis=1)
+    return mixed, np.concatenate([high, high, low], axis=1)
 
 
 def stencil_kernel(plan, *refs):
-    own, before_x, after_x, before_y, after_y, bands_ref, image_ref, sum_ref = refs[:8]
-    field, f_high, f_low, s_high, s_low, h_a, h_b, total, sems = refs[8:]
+    own, before_x, after_x, before_y, after_y, mixed_ref, mass_ref, image_ref, sum_ref = refs[:9]
+    field, f_high, f_low, s_high, s_low, h_a, h_b, total, sems = refs[9:]
     cells_x, cells_y, cells_z = plan.cells_x, plan.cells_y, plan.cells_z
     tiles = plan.tiles
     padded_y = cells_y + 2 * EDGE
@@ -538,6 +533,8 @@
             tile_copy(t).start()
         last_copy.start()
         total[...] = jnp.zeros_like(total)
+        for ref in (f_high, f_low, s_high, s_low):
+            ref[:, cells_z:] = jnp.zeros((ref.shape[0], ref.shape[1] - cells_z), ref.dtype)
         field[:, EDGE - HALO : EDGE, :] = jnp.swapaxes(before_y[...], 0, 1)
         field[:, EDGE + cells_y : EDGE + cells_y + HALO, :] = jnp.swapaxes(after_y[...], 0, 1)
         first_copy.wait()
@@ -570,16 +567,14 @@
                 first = first + ratio * stiff_band[HALO + o] * around
                 second = second + mass_band[HALO + o] * around
             rows = pl.ds(i * padded_y, padded_y)
-            f_high[rows, :], f_low[rows, :] = split(first)
-            s_high[rows, :], s_low[rows, :] = split(second)
+            f_high[rows, :cells_z], f_low[rows, :cells_z] = split(first)
+            s_high[rows, :cells_z], s_low[rows, :cells_z] = split(second)
         window_a, window_b = [], []
-        for w, lanes in enumerate((pl.ds(0, 2 * LANES), pl.ds(LANES, cells_z - LANES))):
-            high, low, stiff = (bands_ref[k, w, : lanes.size, :] for k in range(3))
+        for w in range(2):
+            lanes = pl.ds(w * LANES, 2 * LANES)
             fh, fl, sh, sl = (ref[:, lanes] for ref in (f_high, f_low, s_high, s_low))
-            window_a.append(
-                one(fh, high) + one(fl, high) + one(fh, low) + one(sh, stiff) + one(sl, stiff)
-            )
-            window_b.append(one(sh, high) + one(sl, high) + one(sh, low))
+            window_a.append(one(jnp.concatenate([fh, fl, fh, sh, sl], axis=1), mixed_ref[w]))
+            window_b.append(one(jnp.concatenate([sh, sl, sh], axis=1), mass_ref[w]))
         for ref, (left, right) in ((h_a, window_a), (h_b, window_b)):
             ref[0] = left[:, :LANES]
             ref[1] = left[:, LANES:] + right[:, :LANES]
@@ -617,16 +612,16 @@
     before_y, after_y = from_sides(
         strip(slice(0, HALO)), strip(slice(cells_y - HALO, cells_y)), "narrow"
     )
-    bands = band_matrices(cells_z)
+    mixed, mass = band_matrices(cells_z)
     padded_y = cells_y + 2 * EDGE
     blocks = -(-cells_z // LANES)
-    lump = (GROUP * padded_y, cells_z)
+    lump = (GROUP * padded_y, blocks * LANES)
     return pl.pallas_call(
         functools.partial(stencil_kernel, plan),
         grid=(cells_x // 8,),
         in_specs=[pl.BlockSpec(memory_space=pl.ANY)] * 3
         + [pl.BlockSpec(before_y.shape, lambda t: (0, 0, 0))] * 2
-        + [pl.BlockSpec(bands.shape, lambda t: (0, 0, 0, 0))],
+        + [pl.BlockSpec(v.shape, lambda t: (0, 0, 0)) for v in (mixed, mass)],
         out_specs=[
             pl.BlockSpec((8, cells_y, cells_z), lambda t: (t, 0, 0)),
             pl.BlockSpec((plan.count, 8, LANES), lambda t: (0, 0, 0)),
@@ -651,7 +646,7 @@
             flops=8 * direction.size * cells_z, bytes_accessed=8 * direction.size, transcendentals=0
         ),
         name="stencil",
-    )(direction, before_x, after_x, before_y, after_y, bands)
+    )(direction, before_x, after_x, before_y, after_y, mixed, mass)
 
 
 def update_kernel(now_ref, parts_ref, solution_ref, residual_ref, direction_ref, image_ref, *outs):
@@ -750,7 +745,7 @@
         inverse_final, plan, 1, returned[1], turned_z, base, direction, previous_product
     )
     ends, now = inverse()
-    before_x = shifted(ends[16 - HALO :], -1, "wide")
+    before_x = shifted(ends[plan.cells_x - HALO :], -1, "wide")
     after_x = shifted(ends[:HALO], 1, "wide")
     direction = inverse(ends)
     image, part = stencil(plan, direction, before_x, after_x)

time: 541 us -> 541 us (level)
  transfers between devices with their start and end apart: 8 -> 8, of which waited for: 6 -> 6; matrix products, arithmetic and copies ran while one was open for 2% -> 2% of each run, Pallas kernels for 16% -> 15%
where the time goes in v5:
time: 541 us; the launch traced here: 536 us
  waiting for transfers between devices  275 us (51%)
  Pallas kernels  155 us (29%)
  blocking collectives  48.1 us (9%)
  starting transfers between devices  22.5 us (4%)
  local copies, waits for them, and re-layouts  21.1 us (4%)
  between operations  15.3 us (3%)
    all_to_all x4, waiting for transfers between devices, scatter(): return lax.all_to_all(x, both, split_axis=0, concat_axis=0, tiled=True)  247 us
    pallas_call x2, Pallas kernels, middle(): pl.pallas_call(functools.partial(middle_kernel, plan, chunk), out_shape=[...  51.9 us
    pallas_call x1, Pallas kernels, stencil(): pl.pallas_call(functools.partial(stencil_kernel, plan), grid=(cells_x //...  33.4 us
    all_gather x1, blocking collectives, by_pencils(): whole_y = lax.all_gather(basis_y, 'narrow', axis=0, tiled=True)  23.6 us
    pallas_call x2, Pallas kernels, forward_z(): pl.pallas_call(functools.partial(forward_kernel, plan, chunk), grid=(plan...  22.9 us
    pallas_call x1, Pallas kernels, update(): pl.pallas_call(update_kernel, grid=(image.shape[0] // 4,), in_specs=[pl.B...  20.5 us
    all_gather x1, waiting for transfers between devices, by_pencils(): whole_x = lax.all_gather(basis_x, 'wide', axis=0, tiled=True)  20.3 us
    pallas_call x2, Pallas kernels, inverse_final(): pl.pallas_call(functools.partial(final_kernel, plan, chunk, ends, pick),...  18.6 us
  transfers between devices with their start and end apart: 8, of which 6 were waited for; matrix products, arithmetic and copies ran while one was open for 2% of the time, Pallas kernels for 15%

profile of v5, /device:TPU:0, one launch (start us, length us, event | category | flops | bytes accessed | tf_op | source)
XLA Modules:
  0.0 536.4 jit_solution(15919133632418149860)
XLA Ops:
  7.2 9.9 %all_gather.9 = f32[320,320]{1,0:T(8,128)S(1)} all-gather(f32[160,320]{1,0:T(8,128)} %param.18), channel_id=1, replica_groups=mesh['wide'=16,'narrow'=2] {'narrow'}, dimensions={0}, use_global_device_ids=true | all-gather | bytes 614400 | tf_op jit(solution)/shard_map/all_gather | solution.py:713
  17.0 0.2 copy.40
  17.2 0.1 reshape.43
  17.4 10.6 %forward_z.3 = f32[32,25,8,128]{3,2,1,0:T(8,128)} custom-call(f32[40,160,320]{2,1,0:T(8,128)} %residual_ref.1, f32[128,320]{1,0:T(8,128)S(1)} %bitcast.38), custom_call_target="tpu_custom_call" | custom-call | flops 1572864000 | bytes 16384000 | tf_op jit(solution)/shard_map/forward_z/pallas_call | solution.py:138
  28.0 6.1 %all-to-all-start.1 = ((f32[32,25,8,128]{3,2,1,0:T(8,128)}), f32[32,25,8,128]{3,2,1,0:T(8,128)}, u32[]{:S(2)}, u32[]{:S(2)}) async-start(f32[32,25,8,128]{3,2,1,0:T(8,128)} %forward_z.3), calls=%async_computation.1 | async-start | bytes 6553600 | tf_op jit(solution)/shard_map/all_to_all | solution.py:677
  34.1 0.0 all-gather.2.cloned.1.call-start
  34.2 0.7 all-gather.2.cloned.1.call-update
  34.9 0.1 copy.41
  35.0 0.0 copy-done.14
  35.0 0.0 copy-start
  35.0 23.6 %all_gather.11 = f32[320,320]{1,0:T(8,128)S(1)} all-gather(f32[160,320]{1,0:T(8,128)S(1)} %copy-done.14), channel_id=1, replica_groups=mesh['wide'=16,'narrow'=2] {'narrow'}, dimensions={0}, use_global_device_ids=true | all-gather | bytes 614400 | tf_op jit(solution)/shard_map/all_gather | solution.py:715
  58.6 0.0 copy-done
  58.6 12.3 %forward_z.2 = f32[32,38,8,128]{3,2,1,0:T(8,128)} custom-call(f32[40,160,320]{2,1,0:T(8,128)} %residual_ref.1, f32[192,320]{1,0:T(8,128)S(1)} %bitcast.34), custom_call_target="tpu_custom_call" | custom-call | flops 2359296000 | bytes 16384000 | tf_op jit(solution)/shard_map/forward_z/pallas_call | solution.py:138
  70.9 20.3 %all-gather.2.cloned.1.call-done.refs_1_ = f32[640,640]{1,0:T(8,128)} async-done(((f32[40,640]{1,0:T(8,128)}), f32[640,640]{1,0:T(8,128)}) %all-gather.2.cloned.1.call-update) | async-done | bytes 1638416 | tf_op jit(solution)/shard_map/all_gather | solution.py:716
  91.3 26.8 %all-to-all-done.1 = f32[32,25,8,128]{3,2,1,0:T(8,128)} async-done(((f32[32,25,8,128]{3,2,1,0:T(8,128)}), f32[32,25,8,128]{3,2,1,0:T(8,128)}, u32[]{:S(2)}, u32[]{:S(2)}) %all-to-all-start.1) | async-done | bytes 3276832 | tf_op jit(solution)/shard_map/all_to_all | solution.py:677
  118.0 4.4 all-to-all-start
  122.5 0.8 dynamic_slice.3
  123.2 0.0 copy-done.16
  123.2 0.1 broadcast_add_fusion
  123.3 0.1 slice.66.refs_6_
  123.4 0.9 reshape.52.refs_5_
  124.3 0.6 slice.77
  124.9 0.8 slice.76
  125.7 1.0 copy.42
  126.7 0.0 copy-start.5
  126.7 0.0 copy-start.11
  126.8 1.9 pad_bitcast_fusion.1
  128.6 0.1 pad_maximum_fusion.1.refs_3_
  128.7 0.0 copy-start.9
  128.7 1.5 fusion.4
  130.2 0.1 pad_maximum_fusion.refs_4_
  130.3 20.1 %middle.2 = (f32[16,2,25,8,128]{4,3,2,1,0:T(8,128)S(1)}, f32[8,128]{1,0:T(8,128)S(1)}) custom-call(f32[16,2,25,8,128]{4,3,2,1,0:T(8,128)} %bitcast.14.refs_0_, f32[640,640]{1,0:T(8,128)S(1)} %copy-done.3, f32[640,640]{1,0:T(8,128)S(1)} %bitcast.40, f32[2,256,384]{2,1,0:T(8,128)S(1)} %pad_maximum_fusion.1.refs_3_, ...), custom_call_target="tpu_custom_call" | custom-call | flops 9437184000 | bytes 6553600 | tf_op jit(solution)/shard_map/middle/pallas_call | solution.py:435
  150.5 0.0 copy-start.2
  150.5 1.7 copy-done.2
  152.2 1.2 copy-done.7
  153.4 80.9 %all-to-all-done = f32[32,38,8,128]{3,2,1,0:T(8,128)} async-done(((f32[32,38,8,128]{3,2,1,0:T(8,128)}), f32[32,38,8,128]{3,2,1,0:T(8,128)}, u32[]{:S(2)}, u32[]{:S(2)}) %all-to-all-start) | async-done | bytes 4980768 | tf_op jit(solution)/shard_map/all_to_all | solution.py:677
  234.2 3.5 all-to-all-start.3
  237.7 0.1 slice.62.refs_6_
  237.8 1.4 copy-done.4
  239.2 1.4 copy-done.6
  240.7 1.4 copy-done.8
  242.1 1.1 copy-done.10
  243.2 1.0 copy-done.12
  244.2 31.7 %middle.3 = (f32[16,2,38,8,128]{4,3,2,1,0:T(8,128)}, f32[8,128]{1,0:T(8,128)}) custom-call(f32[16,2,38,8,128]{4,3,2,1,0:T(8,128)} %bitcast.3.refs_0_, f32[640,640]{1,0:T(8,128)S(1)} %copy-done.4, f32[640,640]{1,0:T(8,128)S(1)} %bitcast.41, f32[2,256,384]{2,1,0:T(8,128)S(1)} %copy-done.10, f32[4,256,384]{2,1,0:T(8,128)S(1)} %copy-done.8, ...), custom_call_target="tpu_custom_call" | custom-call | flops 14155776000 | bytes 9961472 | tf_op jit(solution)/shard_map/middle/pallas_call | solution.py:435
  275.9 35.9 %all-to-all-done.3.part_ref = f32[32,25,8,128]{3,2,1,0:T(8,128)S(1)} async-done(((f32[32,25,8,128]{3,2,1,0:T(8,128)}), f32[32,25,8,128]{3,2,1,0:T(8,128)S(1)}, u32[]{:S(2)}, u32[]{:S(2)}) %all-to-all-start.3) | async-done | bytes 3276832 | tf_op jit(solution)/shard_map/all_to_all | solution.py:677
  311.8 3.8 all-to-all-start.2
  316.2 7.2 %inverse_base.1.refs_4_ = f32[40,160,320]{2,1,0:T(8,128)} custom-call(f32[32,25,8,128]{3,2,1,0:T(8,128)S(1)} %all-to-all-done.3.part_ref, f32[128,320]{1,0:T(8,128)S(1)} %bitcast.39), custom_call_target="tpu_custom_call" | custom-call | flops 1572864000 | bytes 24576000 | tf_op jit(solution)/shard_map/inverse_base/pallas_call | solution.py:236
  323.4 103.9 %all-to-all-done.2.refs_0_.refs_1_.refs_2_ = f32[32,38,8,128]{3,2,1,0:T(8,128)} async-done(((f32[32,38,8,128]{3,2,1,0:T(8,128)}), f32[32,38,8,128]{3,2,1,0:T(8,128)}, u32[]{:S(2)}, u32[]{:S(2)}) %all-to-all-start.2) | async-done | bytes 4980768 | tf_op jit(solution)/shard_map/all_to_all | solution.py:677
  427.3 1.0 copy-done.1
  428.3 7.2 %inverse_ends.1 = (f32[40,160,320]{2,1,0:T(8,128)}, f32[8,128]{1,0:T(8,128)S(1)}) custom-call(f32[32,38,8,128]{3,2,1,0:T(8,128)} %all-to-all-done.2.refs_0_.refs_1_.refs_2_, f32[32,38,8,128]{3,2,1,0:T(8,128)} %all-to-all-done.2.refs_0_.refs_1_.refs_2_, f32[32,38,8,128]{3,2,1,0:T(8,128)} %all-to-all-done.2.refs_0_.refs_1_.refs_2_, f32[192,320]{1,0:T(8,128)S(1)} %bitcast.35, ...), custom_call_target="tpu_custom_call" | custom-call | flops 943718400 | bytes 9830400 | tf_op jit(solution)/shard_map/inverse_ends/pallas_call | solution.py:287
  435.5 1.4 fusion.1
  437.0 1.3 collective-permute-start.1
  438.3 3.1 collective-permute-start
  441.4 0.0 copy-start.13
  441.4 11.3 %inverse_inner.1.refs_0_.direction_ref = f32[40,160,320]{2,1,0:T(8,128)} custom-call(f32[32,38,8,128]{3,2,1,0:T(8,128)} %all-to-all-done.2.refs_0_.refs_1_.refs_2_, f32[32,38,8,128]{3,2,1,0:T(8,128)} %all-to-all-done.2.refs_0_.refs_1_.refs_2_, f32[32,38,8,128]{3,2,1,0:T(8,128)} %all-to-all-done.2.refs_0_.refs_1_.refs_2_, ...), custom_call_target="tpu_custom_call", output_to_operand_aliasing={{}: (7, {})} | custom-call | flops 1415577600 | bytes 14745600 | tf_op jit(solution)/shard_map/inverse_inner/pallas_call | solution.py:287
  452.7 1.3 fusion
  454.0 0.0 collective-permute-done.1.refs_2_
  454.1 0.0 collective-permute-done.refs_1_
  454.1 0.1 maximum_select_fusion
  454.2 0.2 collective-permute-start.2
  454.4 6.2 %collective-permute-done.2 = f32[3,46,320]{2,1,0:T(8,128)S(1)} collective-permute-done((f32[3,46,320]{2,1,0:T(8,128)S(1)}, f32[3,46,320]{2,1,0:T(8,128)S(1)}, u32[]{:S(2)}, u32[]{:S(2)}) %collective-permute-start.2) | collective-permute-done | bytes 176672 | tf_op jit(solution)/shard_map/ppermute | solution.py:479
  460.7 33.4 %stencil.1 = (f32[40,160,320]{2,1,0:T(8,128)}, f32[32,8,128]{2,1,0:T(8,128)S(1)}) custom-call(f32[40,160,320]{2,1,0:T(8,128)} %inverse_inner.1.refs_0_.direction_ref, f32[3,160,320]{2,1,0:T(8,128)S(1)} %collective-permute-done.refs_1_, f32[3,160,320]{2,1,0:T(8,128)S(1)} %collective-permute-done.1.refs_2_, f32[3,46,320]{2,1,0:T(8,128)S(1)} %get-tuple-element.38.refs_3_, ...), custom_call_target="tpu_custom_call" | custom-call | flops 5242880000 | bytes 16384000 | tf_op jit(solution)/shard_map/stencil/pallas_call | solution.py:619
  494.2 14.6 %all_to_all.25.parts_ref = f32[32,8,128]{2,1,0:T(8,128)S(1)} all-to-all(f32[32,8,128]{2,1,0:T(8,128)S(1)} %get-tuple-element.23), channel_id=1, replica_groups=mesh['wide'=16,'narrow'=2] {'wide','narrow'}, dimensions={0} | all-to-all | bytes 262144 | tf_op jit(solution)/shard_map/all_to_all | solution.py:677
  508.8 20.5 %update.1 = (f32[40,160,320]{2,1,0:T(8,128)}, f32[40,160,320]{2,1,0:T(8,128)}) custom-call(f32[8,128]{1,0:T(8,128)S(1)} %get-tuple-element.21.now_ref, f32[32,8,128]{2,1,0:T(8,128)S(1)} %all_to_all.25.parts_ref, f32[40,160,320]{2,1,0:T(8,128)} %solution_ref.1, f32[40,160,320]{2,1,0:T(8,128)} %residual_ref.1, ...), custom_call_target="tpu_custom_call" | custom-call | tf_op jit(solution)/shard_map/update/pallas_call | solution.py:661
  (29 shorter events, 0.2 us)
Async XLA Ops:
  28.0 7.0 %copy-start.14 = (f32[160,320]{1,0:T(8,128)S(1)}, f32[160,320]{1,0:T(8,128)}, u32[]{:S(2)}) copy-start(f32[160,320]{1,0:T(8,128)} %param.17) | copy-start | bytes 614404
  28.0 90.1 %all-to-all-start.1 = ((f32[32,25,8,128]{3,2,1,0:T(8,128)}), f32[32,25,8,128]{3,2,1,0:T(8,128)}, u32[]{:S(2)}, u32[]{:S(2)}) async-start(f32[32,25,8,128]{3,2,1,0:T(8,128)} %forward_z.3), calls=%async_computation.1 | async-start | bytes 6553600 | tf_op jit(solution)/shard_map/all_to_all | solution.py:677
  34.1 57.1 %all-gather.2.cloned.1.call-start = ((), (), s32[]{:S(2)}) async-start(), calls=%async_computation.5 | async-start | bytes 1740800 | tf_op jit(solution)/shard_map/all_gather | solution.py:716
  35.0 23.6 %copy-start = (f32[6,32,320]{2,1,0:T(8,128)}, f32[6,32,320]{2,1,0:T(8,128)S(1)}, u32[]{:S(2)}) copy-start(f32[6,32,320]{2,1,0:T(8,128)S(1)} %copy.41) | copy-start | bytes 737284
  70.9 52.3 %copy-start.16 = (f32[320]{0:T(512)S(1)}, f32[320]{0:T(512)}, u32[]{:S(2)}) copy-start(f32[320]{0:T(512)} %param.20) | copy-start | bytes 3844
  70.9 52.5 %copy-start.15 = (f32[640]{0:T(1024)S(1)}, f32[640]{0:T(1024)}, u32[]{:S(2)}) copy-start(f32[640]{0:T(1024)} %param.19) | copy-start | bytes 7684
  91.2 34.4 %copy-start.3 = (f32[640,640]{1,0:T(8,128)S(1)}, f32[640,640]{1,0:T(8,128)}, u32[]{:S(2)}) copy-start(f32[640,640]{1,0:T(8,128)} %all-gather.2.cloned.1.call-done.refs_1_) | copy-start | bytes 4915204
  118.0 116.2 %all-to-all-start = ((f32[32,38,8,128]{3,2,1,0:T(8,128)}), f32[32,38,8,128]{3,2,1,0:T(8,128)}, u32[]{:S(2)}, u32[]{:S(2)}) async-start(f32[32,38,8,128]{3,2,1,0:T(8,128)} %forward_z.2), calls=%async_computation | async-start | bytes 9961472 | tf_op jit(solution)/shard_map/all_to_all | solution.py:677
  126.7 23.8 %copy-start.5 = (f32[640,640]{0,1:T(8,128)}, f32[640,640]{0,1:T(8,128)S(1)}, u32[]{:S(2)}) copy-start(f32[640,640]{0,1:T(8,128)S(1)} %copy.42) | copy-start | bytes 4915204
  126.7 3.6 copy-start.11
  128.7 1.6 copy-start.9
  150.5 1.7 copy-start.2
  152.2 1.2 copy-start.7
  234.2 77.5 %all-to-all-start.3 = ((f32[32,25,8,128]{3,2,1,0:T(8,128)}), f32[32,25,8,128]{3,2,1,0:T(8,128)S(1)}, u32[]{:S(2)}, u32[]{:S(2)}) async-start(f32[32,25,8,128]{3,2,1,0:T(8,128)} %bitcast.37), calls=%async_computation.3 | async-start | bytes 6553600 | tf_op jit(solution)/shard_map/all_to_all | solution.py:677
  237.8 1.4 copy-start.4
  239.2 1.4 copy-start.6
  240.7 1.4 copy-start.8
  242.1 1.1 copy-start.10
  243.2 1.0 copy-start.12
  311.8 115.6 %all-to-all-start.2 = ((f32[32,38,8,128]{3,2,1,0:T(8,128)}), f32[32,38,8,128]{3,2,1,0:T(8,128)}, u32[]{:S(2)}, u32[]{:S(2)}) async-start(f32[32,38,8,128]{3,2,1,0:T(8,128)} %bitcast.42), calls=%async_computation.2 | async-start | bytes 9961472 | tf_op jit(solution)/shard_map/all_to_all | solution.py:677
  427.3 1.0 copy-start.1
  437.0 17.0 %collective-permute-start.1 = (f32[3,160,320]{2,1,0:T(8,128)S(1)}, f32[3,160,320]{2,1,0:T(8,128)S(1)}, u32[]{:S(2)}, u32[]{:S(2)}) collective-permute-start(f32[3,160,320]{2,1,0:T(8,128)S(1)} %get-tuple-element.29), channel_id=1, source_target_pairs={{2,0},{4,2},{6,4},{8,6},{10,8},{12,10},{14,12},{16,14},{18,16},{20... | collective-permute-start | bytes 1843208 | tf_op jit(solution)/shard_map/ppermute | solution.py:472
  438.3 15.8 %collective-permute-start = (f32[3,160,320]{2,1,0:T(8,128)S(1)}, f32[3,160,320]{2,1,0:T(8,128)S(1)}, u32[]{:S(2)}, u32[]{:S(2)}) collective-permute-start(f32[3,160,320]{2,1,0:T(8,128)S(1)} %get-tuple-element.30), channel_id=1, source_target_pairs={{0,2},{2,4},{4,6},{6,8},{8,10},{10,12},{12,14},{14,16},{16,18},{18... | collective-permute-start | bytes 1843208 | tf_op jit(solution)/shard_map/ppermute | solution.py:472
  441.4 19.4 %copy-start.13 = (bf16[2,768,256]{2,1,0:T(8,128)(2,1)S(1)}, bf16[2,768,256]{2,1,0:T(8,128)(2,1)}, u32[]{:S(2)}) copy-start(bf16[2,768,256]{2,1,0:T(8,128)(2,1)} %constant.27.clone.refs_6_) | copy-start | bytes 2359300
  454.2 6.5 %collective-permute-start.2 = (f32[3,46,320]{2,1,0:T(8,128)S(1)}, f32[3,46,320]{2,1,0:T(8,128)S(1)}, u32[]{:S(2)}, u32[]{:S(2)}) collective-permute-start(f32[3,46,320]{2,1,0:T(8,128)S(1)} %maximum_select_fusion), channel_id=1, source_target_pairs={{0,1},{1,0},{2,3},{3,2},{4,5},{5,4},{6,7},{7,6},{8,9},{9,8},{10,11... | collective-permute-start | bytes 529928 | tf_op jit(solution)/shard_map/ppermute | solution.py:479
Sparse Core Ops, SparseCore 0:
  37.1 54.0 all-gather.1

commit v6 on v5

--- a/solution.py
+++ b/solution.py
@@ -507,7 +507,7 @@
 
 def stencil_kernel(plan, *refs):
     own, before_x, after_x, before_y, after_y, mixed_ref, mass_ref, image_ref, sum_ref = refs[:9]
-    field, f_high, f_low, s_high, s_low, h_a, h_b, total, sems = refs[9:]
+    field, f_high, f_low, s_high, s_low, mixes, total, sems = refs[9:]
     cells_x, cells_y, cells_z = plan.cells_x, plan.cells_y, plan.cells_z
     tiles = plan.tiles
     padded_y = cells_y + 2 * EDGE
@@ -548,7 +548,7 @@
     def _():
         last_copy.wait()
 
-    blocks = h_a.shape[0]
+    blocks = mixes.shape[1]
     ratio = stiff_scale / mass_scale
 
     def one(left, right):
@@ -575,20 +575,21 @@
             fh, fl, sh, sl = (ref[:, lanes] for ref in (f_high, f_low, s_high, s_low))
             window_a.append(one(jnp.concatenate([fh, fl, fh, sh, sl], axis=1), mixed_ref[w]))
             window_b.append(one(jnp.concatenate([sh, sl, sh], axis=1), mass_ref[w]))
-        for ref, (left, right) in ((h_a, window_a), (h_b, window_b)):
-            ref[0] = left[:, :LANES]
-            ref[1] = left[:, LANES:] + right[:, :LANES]
-            ref[2] = right[:, LANES:]
+        (a_left, a_right), (b_left, b_right) = window_a, window_b
+        a = (a_left[:, :LANES], a_left[:, LANES:] + a_right[:, :LANES], a_right[:, LANES:])
+        b = (b_left[:, :LANES], b_left[:, LANES:] + b_right[:, :LANES], b_right[:, LANES:])
+        for k in range(blocks):
+            for o in range(HALO + 1):
+                mass = mass_band[HALO + o] / stiff_scale
+                mixes[o, k] = mass * a[k] + (stiff_band[HALO + o] / mass_scale) * b[k]
         for i in range(GROUP):
             plane = g * GROUP + i
             for k in range(blocks):
                 lanes = min(LANES, cells_z - k * LANES)
-                at = lambda ref, o: ref[k, pl.ds(i * padded_y + EDGE + o, cells_y), :]
-                image = (mass_band[HALO] / stiff_scale) * at(h_a, 0)
-                image = image + (stiff_band[HALO] / mass_scale) * at(h_b, 0)
+                at = lambda o, by: mixes[o, k, pl.ds(i * padded_y + EDGE + by, cells_y), :]
+                image = at(0, 0)
                 for o in range(1, HALO + 1):
-                    image = image + (mass_band[HALO + o] / stiff_scale) * (at(h_a, -o) + at(h_a, o))
-                    image = image + (stiff_band[HALO + o] / mass_scale) * (at(h_b, -o) + at(h_b, o))
+                    image = image + (at(o, -o) + at(o, o))
                 here = pl.ds(k * LANES, lanes)
                 image_ref[plane, :, here] = image[:, :lanes]
                 product = image[:, :lanes] * field[step * 8 + plane + HALO, own_y, here]
@@ -636,8 +637,7 @@
             pltpu.VMEM(lump, jnp.bfloat16),
             pltpu.VMEM(lump, jnp.bfloat16),
             pltpu.VMEM(lump, jnp.bfloat16),
-            pltpu.VMEM((blocks, GROUP * padded_y, LANES), jnp.float32),
-            pltpu.VMEM((blocks, GROUP * padded_y, LANES), jnp.float32),
+            pltpu.VMEM((HALO + 1, blocks, GROUP * padded_y, LANES), jnp.float32),
             pltpu.VMEM((8, cells_z), jnp.float32),
             pltpu.SemaphoreType.DMA((plan.tiles + 2,)),
         ],

time: 541 us -> 540 us (level)
  no operation moved by 1% of the time
where the time goes in v6:
time: 540 us; the launch traced here: 535 us
  waiting for transfers between devices  275 us (51%)
  Pallas kernels  154 us (29%)
  blocking collectives  48.1 us (9%)
  starting transfers between devices  22.5 us (4%)
  local copies, waits for them, and re-layouts  21.1 us (4%)
  between operations  15.3 us (3%)
    all_to_all x4, waiting for transfers between devices, scatter(): return lax.all_to_all(x, both, split_axis=0, concat_axis=0, tiled=True)  247 us
    pallas_call x2, Pallas kernels, middle(): pl.pallas_call(functools.partial(middle_kernel, plan, chunk), out_shape=[...  51.9 us
    pallas_call x1, Pallas kernels, stencil(): pl.pallas_call(functools.partial(stencil_kernel, plan), grid=(cells_x //...  32.5 us
    all_gather x1, blocking collectives, by_pencils(): whole_y = lax.all_gather(basis_y, 'narrow', axis=0, tiled=True)  23.6 us
    pallas_call x2, Pallas kernels, forward_z(): pl.pallas_call(functools.partial(forward_kernel, plan, chunk), grid=(plan...  22.9 us
    pallas_call x1, Pallas kernels, update(): pl.pallas_call(update_kernel, grid=(image.shape[0] // 4,), in_specs=[pl.B...  20.5 us
    all_gather x1, waiting for transfers between devices, by_pencils(): whole_x = lax.all_gather(basis_x, 'wide', axis=0, tiled=True)  20.3 us
    pallas_call x2, Pallas kernels, inverse_final(): pl.pallas_call(functools.partial(final_kernel, plan, chunk, ends, pick),...  18.6 us
  transfers between devices with their start and end apart: 8, of which 6 were waited for; matrix products, arithmetic and copies ran while one was open for 2% of the time, Pallas kernels for 15%

profile of v6, /device:TPU:0, one launch (start us, length us, event | category | flops | bytes accessed | tf_op | source)
XLA Modules:
  0.0 535.5 jit_solution(13044267001058071768)
XLA Ops:
  7.2 9.9 %all_gather.9 = f32[320,320]{1,0:T(8,128)S(1)} all-gather(f32[160,320]{1,0:T(8,128)} %param.18), channel_id=1, replica_groups=mesh['wide'=16,'narrow'=2] {'narrow'}, dimensions={0}, use_global_device_ids=true | all-gather | bytes 614400 | tf_op jit(solution)/shard_map/all_gather | solution.py:713
  17.0 0.2 copy.40
  17.2 0.1 reshape.43
  17.4 10.6 %forward_z.3 = f32[32,25,8,128]{3,2,1,0:T(8,128)} custom-call(f32[40,160,320]{2,1,0:T(8,128)} %residual_ref.1, f32[128,320]{1,0:T(8,128)S(1)} %bitcast.38), custom_call_target="tpu_custom_call" | custom-call | flops 1572864000 | bytes 16384000 | tf_op jit(solution)/shard_map/forward_z/pallas_call | solution.py:138
  28.0 6.1 %all-to-all-start.1 = ((f32[32,25,8,128]{3,2,1,0:T(8,128)}), f32[32,25,8,128]{3,2,1,0:T(8,128)}, u32[]{:S(2)}, u32[]{:S(2)}) async-start(f32[32,25,8,128]{3,2,1,0:T(8,128)} %forward_z.3), calls=%async_computation.1 | async-start | bytes 6553600 | tf_op jit(solution)/shard_map/all_to_all | solution.py:677
  34.1 0.0 all-gather.2.cloned.1.call-start
  34.2 0.7 all-gather.2.cloned.1.call-update
  34.9 0.1 copy.41
  35.0 0.0 copy-done.14
  35.0 0.0 copy-start
  35.0 23.6 %all_gather.11 = f32[320,320]{1,0:T(8,128)S(1)} all-gather(f32[160,320]{1,0:T(8,128)S(1)} %copy-done.14), channel_id=1, replica_groups=mesh['wide'=16,'narrow'=2] {'narrow'}, dimensions={0}, use_global_device_ids=true | all-gather | bytes 614400 | tf_op jit(solution)/shard_map/all_gather | solution.py:715
  58.6 0.0 copy-done
  58.6 12.3 %forward_z.2 = f32[32,38,8,128]{3,2,1,0:T(8,128)} custom-call(f32[40,160,320]{2,1,0:T(8,128)} %residual_ref.1, f32[192,320]{1,0:T(8,128)S(1)} %bitcast.34), custom_call_target="tpu_custom_call" | custom-call | flops 2359296000 | bytes 16384000 | tf_op jit(solution)/shard_map/forward_z/pallas_call | solution.py:138
  70.9 20.3 %all-gather.2.cloned.1.call-done.refs_1_ = f32[640,640]{1,0:T(8,128)} async-done(((f32[40,640]{1,0:T(8,128)}), f32[640,640]{1,0:T(8,128)}) %all-gather.2.cloned.1.call-update) | async-done | bytes 1638416 | tf_op jit(solution)/shard_map/all_gather | solution.py:716
  91.3 26.8 %all-to-all-done.1 = f32[32,25,8,128]{3,2,1,0:T(8,128)} async-done(((f32[32,25,8,128]{3,2,1,0:T(8,128)}), f32[32,25,8,128]{3,2,1,0:T(8,128)}, u32[]{:S(2)}, u32[]{:S(2)}) %all-to-all-start.1) | async-done | bytes 3276832 | tf_op jit(solution)/shard_map/all_to_all | solution.py:677
  118.0 4.4 all-to-all-start
  122.5 0.8 dynamic_slice.3
  123.2 0.0 copy-done.16
  123.2 0.1 broadcast_add_fusion
  123.3 0.1 slice.66.refs_6_
  123.4 0.9 reshape.52.refs_5_
  124.3 0.6 slice.77
  124.9 0.8 slice.76
  125.7 1.0 copy.42
  126.7 0.0 copy-start.5
  126.7 0.0 copy-start.11
  126.8 1.9 pad_bitcast_fusion.1
  128.6 0.1 pad_maximum_fusion.1.refs_3_
  128.7 0.0 copy-start.9
  128.7 1.5 fusion.4
  130.2 0.1 pad_maximum_fusion.refs_4_
  130.3 20.1 %middle.2 = (f32[16,2,25,8,128]{4,3,2,1,0:T(8,128)S(1)}, f32[8,128]{1,0:T(8,128)S(1)}) custom-call(f32[16,2,25,8,128]{4,3,2,1,0:T(8,128)} %bitcast.14.refs_0_, f32[640,640]{1,0:T(8,128)S(1)} %copy-done.3, f32[640,640]{1,0:T(8,128)S(1)} %bitcast.40, f32[2,256,384]{2,1,0:T(8,128)S(1)} %pad_maximum_fusion.1.refs_3_, ...), custom_call_target="tpu_custom_call" | custom-call | flops 9437184000 | bytes 6553600 | tf_op jit(solution)/shard_map/middle/pallas_call | solution.py:435
  150.5 0.0 copy-start.2
  150.5 1.7 copy-done.2
  152.2 1.2 copy-done.7
  153.4 80.9 %all-to-all-done = f32[32,38,8,128]{3,2,1,0:T(8,128)} async-done(((f32[32,38,8,128]{3,2,1,0:T(8,128)}), f32[32,38,8,128]{3,2,1,0:T(8,128)}, u32[]{:S(2)}, u32[]{:S(2)}) %all-to-all-start) | async-done | bytes 4980768 | tf_op jit(solution)/shard_map/all_to_all | solution.py:677
  234.2 3.5 all-to-all-start.3
  237.7 0.1 slice.62.refs_6_
  237.8 1.4 copy-done.4
  239.2 1.4 copy-done.6
  240.7 1.4 copy-done.8
  242.1 1.1 copy-done.10
  243.2 1.0 copy-done.12
  244.2 31.7 %middle.3 = (f32[16,2,38,8,128]{4,3,2,1,0:T(8,128)}, f32[8,128]{1,0:T(8,128)}) custom-call(f32[16,2,38,8,128]{4,3,2,1,0:T(8,128)} %bitcast.3.refs_0_, f32[640,640]{1,0:T(8,128)S(1)} %copy-done.4, f32[640,640]{1,0:T(8,128)S(1)} %bitcast.41, f32[2,256,384]{2,1,0:T(8,128)S(1)} %copy-done.10, f32[4,256,384]{2,1,0:T(8,128)S(1)} %copy-done.8, ...), custom_call_target="tpu_custom_call" | custom-call | flops 14155776000 | bytes 9961472 | tf_op jit(solution)/shard_map/middle/pallas_call | solution.py:435
  275.9 35.9 %all-to-all-done.3.part_ref = f32[32,25,8,128]{3,2,1,0:T(8,128)S(1)} async-done(((f32[32,25,8,128]{3,2,1,0:T(8,128)}), f32[32,25,8,128]{3,2,1,0:T(8,128)S(1)}, u32[]{:S(2)}, u32[]{:S(2)}) %all-to-all-start.3) | async-done | bytes 3276832 | tf_op jit(solution)/shard_map/all_to_all | solution.py:677
  311.8 3.8 all-to-all-start.2
  316.2 7.2 %inverse_base.1.refs_4_ = f32[40,160,320]{2,1,0:T(8,128)} custom-call(f32[32,25,8,128]{3,2,1,0:T(8,128)S(1)} %all-to-all-done.3.part_ref, f32[128,320]{1,0:T(8,128)S(1)} %bitcast.39), custom_call_target="tpu_custom_call" | custom-call | flops 1572864000 | bytes 24576000 | tf_op jit(solution)/shard_map/inverse_base/pallas_call | solution.py:236
  323.4 103.9 %all-to-all-done.2.refs_0_.refs_1_.refs_2_ = f32[32,38,8,128]{3,2,1,0:T(8,128)} async-done(((f32[32,38,8,128]{3,2,1,0:T(8,128)}), f32[32,38,8,128]{3,2,1,0:T(8,128)}, u32[]{:S(2)}, u32[]{:S(2)}) %all-to-all-start.2) | async-done | bytes 4980768 | tf_op jit(solution)/shard_map/all_to_all | solution.py:677
  427.3 1.0 copy-done.1
  428.3 7.2 %inverse_ends.1 = (f32[40,160,320]{2,1,0:T(8,128)}, f32[8,128]{1,0:T(8,128)S(1)}) custom-call(f32[32,38,8,128]{3,2,1,0:T(8,128)} %all-to-all-done.2.refs_0_.refs_1_.refs_2_, f32[32,38,8,128]{3,2,1,0:T(8,128)} %all-to-all-done.2.refs_0_.refs_1_.refs_2_, f32[32,38,8,128]{3,2,1,0:T(8,128)} %all-to-all-done.2.refs_0_.refs_1_.refs_2_, f32[192,320]{1,0:T(8,128)S(1)} %bitcast.35, ...), custom_call_target="tpu_custom_call" | custom-call | flops 943718400 | bytes 9830400 | tf_op jit(solution)/shard_map/inverse_ends/pallas_call | solution.py:287
  435.5 1.4 fusion.1
  437.0 1.3 collective-permute-start.1
  438.3 3.1 collective-permute-start
  441.4 0.0 copy-start.13
  441.4 11.3 %inverse_inner.1.refs_0_.direction_ref = f32[40,160,320]{2,1,0:T(8,128)} custom-call(f32[32,38,8,128]{3,2,1,0:T(8,128)} %all-to-all-done.2.refs_0_.refs_1_.refs_2_, f32[32,38,8,128]{3,2,1,0:T(8,128)} %all-to-all-done.2.refs_0_.refs_1_.refs_2_, f32[32,38,8,128]{3,2,1,0:T(8,128)} %all-to-all-done.2.refs_0_.refs_1_.refs_2_, ...), custom_call_target="tpu_custom_call", output_to_operand_aliasing={{}: (7, {})} | custom-call | flops 1415577600 | bytes 14745600 | tf_op jit(solution)/shard_map/inverse_inner/pallas_call | solution.py:287
  452.7 1.3 fusion
  454.0 0.0 collective-permute-done.1.refs_2_
  454.1 0.0 collective-permute-done.refs_1_
  454.1 0.1 maximum_select_fusion
  454.2 0.2 collective-permute-start.2
  454.4 6.2 %collective-permute-done.2 = f32[3,46,320]{2,1,0:T(8,128)S(1)} collective-permute-done((f32[3,46,320]{2,1,0:T(8,128)S(1)}, f32[3,46,320]{2,1,0:T(8,128)S(1)}, u32[]{:S(2)}, u32[]{:S(2)}) %collective-permute-start.2) | collective-permute-done | bytes 176672 | tf_op jit(solution)/shard_map/ppermute | solution.py:479
  460.7 32.5 %stencil.1 = (f32[40,160,320]{2,1,0:T(8,128)}, f32[32,8,128]{2,1,0:T(8,128)S(1)}) custom-call(f32[40,160,320]{2,1,0:T(8,128)} %inverse_inner.1.refs_0_.direction_ref, f32[3,160,320]{2,1,0:T(8,128)S(1)} %collective-permute-done.refs_1_, f32[3,160,320]{2,1,0:T(8,128)S(1)} %collective-permute-done.1.refs_2_, f32[3,46,320]{2,1,0:T(8,128)S(1)} %get-tuple-element.38.refs_3_, ...), custom_call_target="tpu_custom_call" | custom-call | flops 5242880000 | bytes 16384000 | tf_op jit(solution)/shard_map/stencil/pallas_call | solution.py:620
  493.2 14.6 %all_to_all.25.parts_ref = f32[32,8,128]{2,1,0:T(8,128)S(1)} all-to-all(f32[32,8,128]{2,1,0:T(8,128)S(1)} %get-tuple-element.23), channel_id=1, replica_groups=mesh['wide'=16,'narrow'=2] {'wide','narrow'}, dimensions={0} | all-to-all | bytes 262144 | tf_op jit(solution)/shard_map/all_to_all | solution.py:677
  507.8 20.5 %update.1 = (f32[40,160,320]{2,1,0:T(8,128)}, f32[40,160,320]{2,1,0:T(8,128)}) custom-call(f32[8,128]{1,0:T(8,128)S(1)} %get-tuple-element.21.now_ref, f32[32,8,128]{2,1,0:T(8,128)S(1)} %all_to_all.25.parts_ref, f32[40,160,320]{2,1,0:T(8,128)} %solution_ref.1, f32[40,160,320]{2,1,0:T(8,128)} %residual_ref.1, ...), custom_call_target="tpu_custom_call" | custom-call | tf_op jit(solution)/shard_map/update/pallas_call | solution.py:661
  (29 shorter events, 0.2 us)
Async XLA Ops:
  28.0 7.0 %copy-start.14 = (f32[160,320]{1,0:T(8,128)S(1)}, f32[160,320]{1,0:T(8,128)}, u32[]{:S(2)}) copy-start(f32[160,320]{1,0:T(8,128)} %param.17) | copy-start | bytes 614404
  28.0 90.1 %all-to-all-start.1 = ((f32[32,25,8,128]{3,2,1,0:T(8,128)}), f32[32,25,8,128]{3,2,1,0:T(8,128)}, u32[]{:S(2)}, u32[]{:S(2)}) async-start(f32[32,25,8,128]{3,2,1,0:T(8,128)} %forward_z.3), calls=%async_computation.1 | async-start | bytes 6553600 | tf_op jit(solution)/shard_map/all_to_all | solution.py:677
  34.1 57.1 %all-gather.2.cloned.1.call-start = ((), (), s32[]{:S(2)}) async-start(), calls=%async_computation.5 | async-start | bytes 1740800 | tf_op jit(solution)/shard_map/all_gather | solution.py:716
  35.0 23.6 %copy-start = (f32[6,32,320]{2,1,0:T(8,128)}, f32[6,32,320]{2,1,0:T(8,128)S(1)}, u32[]{:S(2)}) copy-start(f32[6,32,320]{2,1,0:T(8,128)S(1)} %copy.41) | copy-start | bytes 737284
  70.9 52.3 %copy-start.16 = (f32[320]{0:T(512)S(1)}, f32[320]{0:T(512)}, u32[]{:S(2)}) copy-start(f32[320]{0:T(512)} %param.20) | copy-start | bytes 3844
  70.9 52.5 %copy-start.15 = (f32[640]{0:T(1024)S(1)}, f32[640]{0:T(1024)}, u32[]{:S(2)}) copy-start(f32[640]{0:T(1024)} %param.19) | copy-start | bytes 7684
  91.2 34.4 %copy-start.3 = (f32[640,640]{1,0:T(8,128)S(1)}, f32[640,640]{1,0:T(8,128)}, u32[]{:S(2)}) copy-start(f32[640,640]{1,0:T(8,128)} %all-gather.2.cloned.1.call-done.refs_1_) | copy-start | bytes 4915204
  118.0 116.2 %all-to-all-start = ((f32[32,38,8,128]{3,2,1,0:T(8,128)}), f32[32,38,8,128]{3,2,1,0:T(8,128)}, u32[]{:S(2)}, u32[]{:S(2)}) async-start(f32[32,38,8,128]{3,2,1,0:T(8,128)} %forward_z.2), calls=%async_computation | async-start | bytes 9961472 | tf_op jit(solution)/shard_map/all_to_all | solution.py:677
  126.7 23.8 %copy-start.5 = (f32[640,640]{0,1:T(8,128)}, f32[640,640]{0,1:T(8,128)S(1)}, u32[]{:S(2)}) copy-start(f32[640,640]{0,1:T(8,128)S(1)} %copy.42) | copy-start | bytes 4915204
  126.7 3.6 copy-start.11
  128.7 1.6 copy-start.9
  150.5 1.7 copy-start.2
  152.2 1.2 copy-start.7
  234.2 77.5 %all-to-all-start.3 = ((f32[32,25,8,128]{3,2,1,0:T(8,128)}), f32[32,25,8,128]{3,2,1,0:T(8,128)S(1)}, u32[]{:S(2)}, u32[]{:S(2)}) async-start(f32[32,25,8,128]{3,2,1,0:T(8,128)} %bitcast.37), calls=%async_computation.3 | async-start | bytes 6553600 | tf_op jit(solution)/shard_map/all_to_all | solution.py:677
  237.8 1.4 copy-start.4
  239.2 1.4 copy-start.6
  240.7 1.4 copy-start.8
  242.1 1.1 copy-start.10
  243.2 1.0 copy-start.12
  311.8 115.6 %all-to-all-start.2 = ((f32[32,38,8,128]{3,2,1,0:T(8,128)}), f32[32,38,8,128]{3,2,1,0:T(8,128)}, u32[]{:S(2)}, u32[]{:S(2)}) async-start(f32[32,38,8,128]{3,2,1,0:T(8,128)} %bitcast.42), calls=%async_computation.2 | async-start | bytes 9961472 | tf_op jit(solution)/shard_map/all_to_all | solution.py:677
  427.3 1.0 copy-start.1
  437.0 17.0 %collective-permute-start.1 = (f32[3,160,320]{2,1,0:T(8,128)S(1)}, f32[3,160,320]{2,1,0:T(8,128)S(1)}, u32[]{:S(2)}, u32[]{:S(2)}) collective-permute-start(f32[3,160,320]{2,1,0:T(8,128)S(1)} %get-tuple-element.29), channel_id=1, source_target_pairs={{2,0},{4,2},{6,4},{8,6},{10,8},{12,10},{14,12},{16,14},{18,16},{20... | collective-permute-start | bytes 1843208 | tf_op jit(solution)/shard_map/ppermute | solution.py:472
  438.3 15.8 %collective-permute-start = (f32[3,160,320]{2,1,0:T(8,128)S(1)}, f32[3,160,320]{2,1,0:T(8,128)S(1)}, u32[]{:S(2)}, u32[]{:S(2)}) collective-permute-start(f32[3,160,320]{2,1,0:T(8,128)S(1)} %get-tuple-element.30), channel_id=1, source_target_pairs={{0,2},{2,4},{4,6},{6,8},{8,10},{10,12},{12,14},{14,16},{16,18},{18... | collective-permute-start | bytes 1843208 | tf_op jit(solution)/shard_map/ppermute | solution.py:472
  441.4 19.4 %copy-start.13 = (bf16[2,768,256]{2,1,0:T(8,128)(2,1)S(1)}, bf16[2,768,256]{2,1,0:T(8,128)(2,1)}, u32[]{:S(2)}) copy-start(bf16[2,768,256]{2,1,0:T(8,128)(2,1)} %constant.27.clone.refs_6_) | copy-start | bytes 2359300
  454.2 6.5 %collective-permute-start.2 = (f32[3,46,320]{2,1,0:T(8,128)S(1)}, f32[3,46,320]{2,1,0:T(8,128)S(1)}, u32[]{:S(2)}, u32[]{:S(2)}) collective-permute-start(f32[3,46,320]{2,1,0:T(8,128)S(1)} %maximum_select_fusion), channel_id=1, source_target_pairs={{0,1},{1,0},{2,3},{3,2},{4,5},{5,4},{6,7},{7,6},{8,9},{9,8},{10,11... | collective-permute-start | bytes 529928 | tf_op jit(solution)/shard_map/ppermute | solution.py:479
Sparse Core Ops, SparseCore 0:
  37.1 54.0 all-gather.1
